TPU v7x, 128 devices: a whole 4x4x4 slice. The times are simulated.
128 devices in a mesh: student: 16 (over x, z_hi, core), pool: 8 (over z_lo, y).
Axes of the slice: x: 4, y: 4, z: 4 (z_hi: 2, z_lo: 2; z = z_hi * 2 + z_lo), core: 2. Of those that a mesh axis runs over, the one named last changes fastest.
Arguments:
- pixels: bfloat16 [512, 128, 588], P(('student', 'pool')), may hold values from -6 to 6
- keyframes: int32 [128, 2], P(('student', 'pool')), may hold values from 0 to 3, as said below
- destination: int32 [128, 2], P(('student', 'pool')), may hold values from 0 to 7, as said below
- student_embed: float32 [588, 384], replicated, may hold values from -0.25 to 0.25
- student_gain: float32 [384], replicated, may hold values from 0.1 to 1.9
- student_up: float32 [384, 1536], replicated, may hold values from -0.3125 to 0.3125
- student_down: float32 [1536, 384], replicated, may hold values from -0.15625 to 0.15625
- student_head: float32 [384, 1536], replicated, may hold values from -0.3125 to 0.3125
- teacher_embed: bfloat16 [8, 588, 1536], P('pool', None, 'student'), may hold values from -0.25 to 0.25
- teacher_gain: float32 [8, 1536], P('pool'), may hold values from 0.1 to 1.9
- teacher_project: bfloat16 [8, 1536, 4608], P('pool', None, 'student'), may hold values from -1.8371173 to 1.8371173
- teacher_output: bfloat16 [8, 1536, 1536], P('pool', None, 'student'), may hold values from -0.15625 to 0.15625
Outputs:
- mean_distance: float32 [], replicated
- grad_embed: float32 [588, 384], replicated
- grad_gain: float32 [384], replicated
- grad_up: float32 [384, 1536], replicated
- grad_down: float32 [1536, 384], replicated
- grad_head: float32 [384, 1536], replicated
Inputs may be any that keep to these rules, and one draw needn't show every extreme that they name: `keyframes`: the 2 indices of one device are distinct. `destination`: the 2 teachers of one device are distinct. Among the 8 devices with one student index, some teacher is assigned a block by every one of them.
All inputs are finite; a program needn't handle non-finite values.
Results may differ from a plain program's by a relative error of at most 0.008.
Values may be sent and summed in bfloat16 or wider, within the bound.
No kernel may reach another device: no remote copies, remote signals or barrier semaphores. Data moves between devices by JAX's collectives and lax.ppermute only.
A program may use at most 192 MiB of HBM per device.

v0:
```python
import jax
import jax.numpy as jnp
from jax import lax
from jax.experimental import pallas as pl
from jax.experimental.pallas import tpu as pltpu
from jax.sharding import PartitionSpec as P

HEADS = 24
HDIM = 64
EPSILON = 1e-06
BOTH = ("student", "pool")
DEVICES = 128
PAIR = 2 * HDIM
LANES = 128
PIX = 588
PIX_PAD = 640
D_S = 384
D_T = 1536
S_HID = 1536
BLK = 128
RANKS = DEVICES // 2
CHUNK = 64
SUM_ROWS = 2 * RANKS * CHUNK
EMBED_ROWS = 592
UP_AT = S_HID
EMBED_AT = UP_AT + D_S * S_HID // LANES
GAIN_AT = EMBED_AT + (D_S // LANES) * EMBED_ROWS
NT = (((1,), (1,)), ((), ()))
TN = (((0,), (0,)), ((), ()))
NN = (((1,), (0,)), ((), ()))


def bf16_dot(left, right, dims):
    return lax.dot_general(left, right, dims, preferred_element_type=jnp.float32)


def rms_scale(values):
    return lax.rsqrt(jnp.mean(values * values, axis=-1, keepdims=True) + EPSILON)


def halved_dot(left, right):
    return (
        bf16_dot(left[0], right[0], NN)
        + bf16_dot(left[1], right[0], NN)
        + bf16_dot(left[0], right[1], NN)
    )


def attention_kernel(mixed_ref, out_ref):
    lane = lax.broadcasted_iota(jnp.int32, (BLK, PAIR), 1)
    first = lane < HDIM
    zero = jnp.zeros((BLK, PAIR), jnp.bfloat16)
    ones = jnp.concatenate(
        [jnp.where(first, 1.0, 0.0), jnp.where(first, 0.0, 1.0)], axis=0
    ).astype(jnp.bfloat16)
    for pair in range(HEADS // 2):
        at = pair * PAIR
        queries = mixed_ref[:, at : at + PAIR]
        keys = mixed_ref[:, D_T + at : D_T + at + PAIR]
        values = mixed_ref[:, 2 * D_T + at : 2 * D_T + at + PAIR]
        keys_two = jnp.concatenate(
            [jnp.where(first, keys, zero), jnp.where(first, zero, keys)], axis=0
        )
        values_two = jnp.concatenate(
            [jnp.where(first, values, zero), jnp.where(first, zero, values)], axis=0
        )
        scores = bf16_dot(queries, keys_two, NT)
        left, right = scores[:, :BLK], scores[:, BLK:]
        scale = HDIM ** (-0.5)
        left = jnp.exp((left - jnp.max(left, axis=1, keepdims=True)) * scale)
        right = jnp.exp((right - jnp.max(right, axis=1, keepdims=True)) * scale)
        weights = jnp.concatenate([left, right], axis=1).astype(jnp.bfloat16)
        summed = bf16_dot(weights, jnp.concatenate([values_two, ones], axis=1), NN)
        out_ref[:, at : at + PAIR] = (summed[:, :PAIR] / summed[:, PAIR:]).astype(jnp.bfloat16)


def attend(mixed):
    rows, total = mixed.shape
    return pl.pallas_call(
        attention_kernel,
        grid=(rows // BLK,),
        in_specs=[pl.BlockSpec((BLK, total), lambda b: (b, 0))],
        out_specs=pl.BlockSpec((BLK, D_T), lambda b: (b, 0)),
        out_shape=jax.ShapeDtypeStruct((rows, D_T), jnp.bfloat16),
        compiler_params=pltpu.CompilerParams(vmem_limit_bytes=32 * 1024 * 1024),
        cost_estimate=pl.CostEstimate(
            flops=rows * BLK * D_T * 8, bytes_accessed=rows * D_T * 8, transcendentals=rows * BLK * HEADS
        ),
        name="attention",
    )(mixed)


def core_groups():
    groups = [[], []]
    for device in range(DEVICES):
        groups[(device // 8) % 2].append(device)
    return groups


def core_swap(values):
    pairs = [(d, d ^ 8) for d in range(DEVICES)]
    return lax.ppermute(values, BOTH, pairs)


def halves_of(values):
    high = lax.reduce_precision(values, 8, 7)
    return high.astype(jnp.bfloat16), (values - high).astype(jnp.bfloat16)


def cut(values):
    high = values.astype(jnp.bfloat16)
    return high, (values - high.astype(jnp.float32)).astype(jnp.bfloat16)


def dot_three(left, right, dims):
    at_left, at_right = dims[0][0][0], dims[0][1][0]
    wide = jnp.concatenate([left[0], left[1], left[0]], axis=at_left)
    other = jnp.concatenate([right[0], right[0], right[1]], axis=at_right)
    return bf16_dot(wide, other, dims)


def scale_of(values):
    return lax.rsqrt(jnp.mean(values * values, axis=1, keepdims=True) + EPSILON)


def head_kernel(
    context, embedded, output, student_out, hidden_hi, hidden_lo, act_hi, act_lo, head_hi, head_lo,
    sums, down_rest, d_hidden_out, total,
):
    @pl.when(pl.program_id(0) == 0)
    def _():
        sums[...] = jnp.zeros_like(sums)
        down_rest[...] = jnp.zeros_like(down_rest)
        total[...] = jnp.zeros_like(total)

    finished = embedded[...] + bf16_dot(context[...], output[...], NT)
    features = (finished * scale_of(finished)).astype(jnp.bfloat16).astype(jnp.float32)
    out = student_out[...]
    dot_mean = jnp.mean(out * features, axis=1, keepdims=True)
    out_scale, feature_scale = scale_of(out), scale_of(features)
    both = out_scale * feature_scale
    total[...] += jnp.sum(dot_mean * both)
    along = both * (-1.0 / D_T)
    back = both * dot_mean * out_scale * out_scale * (1.0 / D_T)
    d_out = cut(along * features + back * out)
    grad_head = dot_three((hidden_hi[...], hidden_lo[...]), d_out, TN)
    for i in range(D_T // LANES):
        sums[i * D_S : (i + 1) * D_S, :] += grad_head[:, i * LANES : (i + 1) * LANES]
    d_hidden = dot_three(d_out, (head_hi[...], head_lo[...]), NT)
    d_hidden_out[...] = d_hidden
    grad_down = dot_three((act_hi[...], act_lo[...]), cut(d_hidden), TN)
    at = D_S * D_T // LANES
    for i in range(2):
        sums[at + i * S_HID : at + (i + 1) * S_HID, :] += grad_down[:, i * LANES : (i + 1) * LANES]
    down_rest[...] += grad_down[:, 2 * LANES :]


def head_backward(context, embedded, output, student_out, hidden, act, head):
    rows = context.shape[0]
    block = 256

    def by_row(columns):
        return pl.BlockSpec((block, columns), lambda r: (r, 0))

    def whole(shape):
        return pl.BlockSpec(shape, lambda r: (0, 0))

    return pl.pallas_call(
        head_kernel,
        grid=(rows // block,),
        in_specs=[
            by_row(D_T), by_row(D_T), whole((D_T, D_T)), by_row(D_T), by_row(D_S), by_row(D_S),
            by_row(S_HID), by_row(S_HID), whole((D_S, D_T)), whole((D_S, D_T)),
        ],
        out_specs=[whole((SUM_ROWS, LANES)), whole((S_HID, LANES)), by_row(D_S), whole((8, LANES))],
        out_shape=[
            jax.ShapeDtypeStruct((SUM_ROWS, LANES), jnp.float32),
            jax.ShapeDtypeStruct((S_HID, LANES), jnp.float32),
            jax.ShapeDtypeStruct((rows, D_S), jnp.float32),
            jax.ShapeDtypeStruct((8, LANES), jnp.float32),
        ],
        compiler_params=pltpu.CompilerParams(vmem_limit_bytes=56 * 1024 * 1024),
        cost_estimate=pl.CostEstimate(
            flops=2 * rows * D_T * (D_T + 9 * D_S), bytes_accessed=40 * 1024 * 1024, transcendentals=0
        ),
        name="head_backward",
    )(context, embedded, output, student_out, *hidden, *act, *head)


def trunk_kernel(
    d_hidden, slope, down_hi, down_lo, up_hi, up_lo, normed_hi, normed_lo, unit, scale, gain, rows,
    down_rest, total, sums, dh_hi, dh_lo, d_normed,
):
    step = pl.program_id(0)
    tile = slope.shape[1]

    @pl.when(step == 0)
    def _():
        dh_hi[...], dh_lo[...] = cut(d_hidden[...])
        d_normed[...] = jnp.zeros_like(d_normed)
        sums[:UP_AT, :] = down_rest[...]
        sums[GAIN_AT:, :] = jnp.zeros((SUM_ROWS - GAIN_AT, LANES), jnp.float32)

    d_act = dot_three((dh_hi[...], dh_lo[...]), (down_hi[...], down_lo[...]), NT)
    d_pre = cut(d_act * slope[...])
    grad_up = dot_three((normed_hi[...], normed_lo[...]), d_pre, TN)
    at = pl.multiple_of(UP_AT + step * (tile // LANES) * D_S, LANES)
    for i in range(tile // LANES):
        sums[pl.ds(at + i * D_S, D_S), :] = grad_up[:, i * LANES : (i + 1) * LANES]
    d_normed[...] += dot_three(d_pre, (up_hi[...], up_lo[...]), NT)

    @pl.when(step == pl.num_programs(0) - 1)
    def _():
        d_out = d_normed[...]
        across = unit[...]
        grad_gain = jnp.sum(d_out * across, axis=0, keepdims=True)
        d_unit = d_out * gain[...]
        inner = jnp.mean(d_unit * across, axis=1, keepdims=True)
        d_lifted = cut(d_hidden[...] + scale[...] * (d_unit - across * inner))
        grad_embed = bf16_dot(rows[...], d_lifted[0], TN) + bf16_dot(rows[...], d_lifted[1], TN)
        for i in range(D_S // LANES):
            columns = slice(i * LANES, (i + 1) * LANES)
            start = EMBED_AT + i * EMBED_ROWS
            sums[start : start + EMBED_ROWS, :] = grad_embed[:EMBED_ROWS, columns]
            sums[GAIN_AT + i : GAIN_AT + i + 1, :] = grad_gain[:, columns]
        first, rest = cut(total[0:1, :])
        first = first.astype(jnp.float32)
        second, third = cut(total[0:1, :] - first)
        lane = lax.broadcasted_iota(jnp.int32, (1, LANES), 1)
        row = jnp.where(
            lane == 0,
            first,
            jnp.where(lane == 1, second.astype(jnp.float32), third.astype(jnp.float32)),
        )
        sums[SUM_ROWS - 1 :, :] = jnp.where(lane < 3, row, 0.0)


def trunk_backward(d_hidden, slope, down, up, normed, unit, scale, gain, rows, down_rest, total):
    count = d_hidden.shape[0]
    tile = 256

    def whole(values):
        return pl.BlockSpec(values.shape, lambda j: (0, 0))

    down_spec = pl.BlockSpec((tile, D_S), lambda j: (j, 0))
    up_spec = pl.BlockSpec((D_S, tile), lambda j: (0, j))
    return pl.pallas_call(
        trunk_kernel,
        grid=(S_HID // tile,),
        in_specs=[
            whole(d_hidden), pl.BlockSpec((count, tile), lambda j: (0, j)),
            down_spec, down_spec, up_spec, up_spec,
            whole(normed[0]), whole(normed[1]), whole(unit), whole(scale), whole(gain), whole(rows),
            whole(down_rest), whole(total),
        ],
        out_specs=pl.BlockSpec((SUM_ROWS, LANES), lambda j: (0, 0)),
        out_shape=jax.ShapeDtypeStruct((SUM_ROWS, LANES), jnp.float32),
        scratch_shapes=[
            pltpu.VMEM((count, D_S), jnp.bfloat16),
            pltpu.VMEM((count, D_S), jnp.bfloat16),
            pltpu.VMEM((count, D_S), jnp.float32),
        ],
        compiler_params=pltpu.CompilerParams(vmem_limit_bytes=56 * 1024 * 1024),
        cost_estimate=pl.CostEstimate(
            flops=2 * count * D_S * (9 * S_HID + 2 * PIX_PAD), bytes_accessed=30 * 1024 * 1024, transcendentals=0
        ),
        name="trunk_backward",
    )(d_hidden, slope, *down, *up, *normed, unit, scale, gain, rows, down_rest, total)


def unpack_kernel(core, a_mine, a_theirs, b_mine, b_theirs, head, down, up, embed, gain, total):
    def unpack(a_low, a_high, b_low, b_high):
        half = SUM_ROWS // 2

        def take(low, high, start, count):
            stop = start + count
            parts = []
            if start < half:
                parts.append(low[start : min(stop, half), :])
            if stop > half:
                parts.append(high[max(start, half) - half : stop - half, :])
            parts = [part.astype(jnp.float32) for part in parts]
            return parts[0] if len(parts) == 1 else jnp.concatenate(parts, axis=0)

        for i in range(D_T // LANES):
            columns = slice(i * LANES, (i + 1) * LANES)
            head[:, columns] = take(a_low, a_high, i * D_S, D_S)
            up[:, columns] = take(b_low, b_high, UP_AT + i * D_S, D_S)
        at = D_S * D_T // LANES
        for i in range(2):
            down[:, i * LANES : (i + 1) * LANES] = take(a_low, a_high, at + i * S_HID, S_HID)
        down[:, 2 * LANES :] = take(b_low, b_high, 0, S_HID)
        for i in range(D_S // LANES):
            columns = slice(i * LANES, (i + 1) * LANES)
            embed[:, columns] = take(b_low, b_high, EMBED_AT + i * EMBED_ROWS, EMBED_ROWS)[:PIX]
        gain[...] = take(b_low, b_high, GAIN_AT, 16)[:8]
        total[...] = take(b_low, b_high, SUM_ROWS - 16, 16)[8:]

    @pl.when(core[0] == 0)
    def _():
        unpack(a_mine, a_theirs, b_mine, b_theirs)

    @pl.when(core[0] == 1)
    def _():
        unpack(a_theirs, a_mine, b_theirs, b_mine)


def unpack_sums(core, a_mine, a_theirs, b_mine, b_theirs):
    vmem = pl.BlockSpec(memory_space=pltpu.VMEM)
    shapes = [(D_S, D_T), (S_HID, D_S), (D_S, S_HID), (PIX, D_S), (8, LANES), (8, LANES)]
    return pl.pallas_call(
        unpack_kernel,
        in_specs=[pl.BlockSpec(memory_space=pltpu.SMEM)] + [vmem] * 4,
        out_specs=[vmem] * 6,
        out_shape=[jax.ShapeDtypeStruct(shape, jnp.float32) for shape in shapes],
        compiler_params=pltpu.CompilerParams(vmem_limit_bytes=56 * 1024 * 1024),
        cost_estimate=pl.CostEstimate(flops=0, bytes_accessed=12 * 1024 * 1024, transcendentals=0),
        name="unpack_sums",
    )(core.reshape(1), a_mine, a_theirs, b_mine, b_theirs)


def scatter_sum(sums, core):
    halves = sums.reshape(2, SUM_ROWS // 2, LANES)
    mine = lax.dynamic_index_in_dim(halves, core, 0, keepdims=False)
    other = lax.dynamic_index_in_dim(halves, 1 - core, 0, keepdims=False)
    mine = mine + core_swap(other)
    sent = mine.astype(jnp.bfloat16).reshape(RANKS, CHUNK, LANES)
    got = lax.all_to_all(sent, BOTH, 0, 0, axis_index_groups=core_groups(), tiled=True)
    return jnp.sum(got.astype(jnp.float32), axis=0)


def spread_chunk(chunk):
    spread = jnp.broadcast_to(chunk.astype(jnp.bfloat16)[None], (RANKS, CHUNK, LANES))
    half = lax.all_to_all(spread, BOTH, 0, 0, axis_index_groups=core_groups(), tiled=True)
    half = half.reshape(SUM_ROWS // 2, LANES)
    return half, core_swap(half)


def keep_total(chunk, core):
    rank = (lax.axis_index("student") // 2) * 8 + lax.axis_index("pool")
    owner = jnp.logical_and(core == 1, rank == RANKS - 1)
    whole = jnp.sum(chunk[CHUNK - 1, :3])
    first = lax.reduce_precision(whole, 8, 7)
    second = lax.reduce_precision(whole - first, 8, 7)
    lane = lax.broadcasted_iota(jnp.int32, (CHUNK, LANES), 1)
    row = jnp.where(lane == 0, first, jnp.where(lane == 1, second, whole - first - second))
    last = lax.broadcasted_iota(jnp.int32, (CHUNK, LANES), 0) == CHUNK - 1
    return jnp.where(jnp.logical_and(owner, last), row, chunk)


def on_device(
    pixels,
    keyframes,
    destination,
    student_embed,
    student_gain,
    student_up,
    student_down,
    student_head,
    teacher_embed,
    teacher_gain,
    teacher_project,
    teacher_output,
):
    pool_size = lax.axis_size("pool")

    def gathered(shard):
        return lax.all_gather(shard, "student", axis=0, tiled=True)

    embed_full = gathered(jnp.pad(teacher_embed[0].T, ((0, 0), (0, PIX_PAD - PIX))))
    project_full = gathered(teacher_project[0].T)
    output_full = gathered(teacher_output[0].T)

    teachers = jnp.arange(pool_size, dtype=jnp.int32)[:, None, None]
    chosen = [
        lax.dynamic_index_in_dim(pixels, keyframes[0, k], 0, keepdims=True) for k in range(2)
    ]
    outgoing = jnp.where(
        destination[0, 0] == teachers,
        chosen[0],
        jnp.where(destination[0, 1] == teachers, chosen[1], jnp.zeros((), jnp.bfloat16)),
    )
    outgoing = jnp.pad(outgoing, ((0, 0), (0, 0), (0, PIX_PAD - PIX)))
    arrived = lax.all_to_all(outgoing, "pool", split_axis=0, concat_axis=0, tiled=True)
    rows = arrived.reshape(pool_size * BLK, PIX_PAD)

    embed = jnp.pad(student_embed, ((0, PIX_PAD - PIX), (0, 0)))
    embed = halves_of(embed)
    lifted = bf16_dot(rows, embed[0], NN) + bf16_dot(rows, embed[1], NN)
    scale = rms_scale(lifted)
    unit = lifted * scale
    normed_s = halves_of(unit * student_gain)
    up = halves_of(student_up)
    down = halves_of(student_down)
    head = halves_of(student_head)
    pre = halved_dot(normed_s, up)
    cdf = 0.5 * (1.0 + lax.erf(pre * (2.0**-0.5)))
    act = halves_of(pre * cdf)
    slope = cdf + pre * jnp.exp(-0.5 * pre * pre) * ((2.0 * jnp.pi) ** -0.5)
    hidden = halves_of(lifted + halved_dot(act, down))
    student_out = halved_dot(hidden, head)

    embedded = bf16_dot(rows, embed_full, NT)
    normed = (embedded * rms_scale(embedded) * teacher_gain[0]).astype(jnp.bfloat16)
    mixed = bf16_dot(normed, project_full, NT).astype(jnp.bfloat16)
    context = attend(mixed)

    core = lax.rem(lax.axis_index("student"), 2)
    sums_a, down_rest, d_hidden, total = head_backward(
        context, embedded, output_full, student_out, hidden, act, head
    )
    chunk_a = scatter_sum(sums_a, core)
    sums_b = trunk_backward(
        d_hidden, slope, down, up, normed_s, unit, scale, student_gain[None], rows, down_rest, total
    )
    chunk_b = keep_total(scatter_sum(sums_b, core), core)
    head_sum, down_sum, up_sum, embed_sum, gain_sum, cosine_sum = unpack_sums(
        core, *spread_chunk(chunk_a), *spread_chunk(chunk_b)
    )
    gain_sum = gain_sum[: D_S // LANES].reshape(D_S)
    mean_distance = 1.0 - jnp.sum(cosine_sum[7, :3]) / (DEVICES * 2 * BLK)
    return (mean_distance, embed_sum, gain_sum, up_sum, down_sum, head_sum)


def solution(mesh):
    in_specs = (
        P(("student", "pool"), None, None),
        P(("student", "pool"), None),
        P(("student", "pool"), None),
        P(),
        P(),
        P(),
        P(),
        P(),
        P("pool", None, "student"),
        P("pool", None),
        P("pool", None, "student"),
        P("pool", None, "student"),
    )
    out_specs = (P(), P(), P(), P(), P(), P())
    return jax.shard_map(
        on_device, mesh=mesh, in_specs=in_specs, out_specs=out_specs, check_vma=False
    )
```

profile of v0, /device:TPU:1, one launch (start us, length us, event | category | flops | bytes accessed | tf_op | source)
XLA Modules:
  0.0 406.2 jit_solution(17558099064638040511)
XLA Ops:
  20.4 6.4 %all-to-all-start = ((bf16[8,128,640]{2,1,0:T(8,128)(2,1)}), bf16[8,128,640]{2,1,0:T(8,128)(2,1)S(1)}, u32[]{:S(2)}, u32[]{:S(2)}) async-start(bf16[8,128,640]{2,1,0:T(8,128)(2,1)} %pad.12), calls=%async_computation | async-start | bytes 2621440 | tf_op jit(solution)/shard_map/all_to_all | solution.py:384
  27.5 3.0 fusion.7
  31.2 3.6 fusion.8
  36.5 8.8 %all-to-all-done = bf16[8,128,640]{2,1,0:T(8,128)(2,1)S(1)} async-done(((bf16[8,128,640]{2,1,0:T(8,128)(2,1)}), bf16[8,128,640]{2,1,0:T(8,128)(2,1)S(1)}, u32[]{:S(2)}, u32[]{:S(2)}) %all-to-all-start) | async-done | bytes 1310752 | tf_op jit(solution)/shard_map/all_to_all | solution.py:384
  52.1 6.5 %fusion.4 = (f32[1024,1536]{1,0:T(8,128)}, bf16[1024,1536]{1,0:T(8,128)(2,1)S(1)}, bf16[1024,1536]{1,0:T(8,128)(2,1)}) fusion(bf16[1024,384]{1,0:T(8,128)(2,1)S(1)} %reduce-precision_convert_fusion.5.normed_hi, bf16[384,1536]{1,0:T(8,128)(2,1)S(1)} %copy-done.8, f32[1024,1536]{1,0:T(8,128)S(1)} %fusion.21, f32[1024,1536]{1,0:T(8,128)S(1)} %fusion.22), kind=kOutput, calls=%fused_computation.8 | convolution fusion | flops 1231552512 | bytes 27131904 | tf_op jit(solution)/shard_map/dot_general | solution.py:34
  58.6 2.9 fusion.23
  62.6 4.1 %fusion.24 = f32[1024,384]{1,0:T(8,128)S(1)} fusion(bf16[1024,1536]{1,0:T(8,128)(2,1)} %get-tuple-element.30.act_lo, bf16[1536,384]{1,0:T(8,128)(2,1)} %get-tuple-element.34.down_hi), kind=kOutput, calls=%fused_computation.67 | convolution fusion | flops 1207959552 | bytes 5898240 | tf_op jit(solution)/shard_map/dot_general | solution.py:34
  67.1 2.0 fusion.13
  72.8 4.5 %add_add_fusion.student_out = f32[1024,1536]{1,0:T(8,128)} fusion(f32[1024,1536]{1,0:T(8,128)S(1)} %fusion.25, f32[1024,1536]{1,0:T(8,128)S(1)} %fusion.26, bf16[1024,384]{1,0:T(8,128)(2,1)S(1)} %get-tuple-element.38.hidden_hi, bf16[384,1536]{1,0:T(8,128)(2,1)S(1)} %copy-done.9), kind=kOutput, calls=%fused_computation.9 | convolution fusion | flops 1211105280 | bytes 20840448 | tf_op jit(solution)/shard_map/dot_general | solution.py:34
  77.2 6.1 %multiply_reduce_fusion = (f32[1024]{0:T(1024)S(1)}, f32[1024,1536]{1,0:T(8,128)}) fusion(bf16[1024,640]{1,0:T(8,128)(2,1)S(1)} %bitcast.65, bf16[1536,640]{1,0:T(8,128)(2,1)} %all-gather.4.cloned.1.call-done), kind=kOutput, calls=%fused_computation.13 | convolution fusion | flops 2016410624 | bytes 9572352 | tf_op jit(solution)/shard_map/dot_general | solution.py:34
  83.3 78.1 %all-gather.6.cloned.1.call-done = bf16[4608,1536]{1,0:T(8,128)(2,1)} async-done(((bf16[288,1536]{1,0:T(8,128)(2,1)}), bf16[4608,1536]{1,0:T(8,128)(2,1)}) %all-gather.6.cloned.1.call-update) | async-done | bytes 14155792 | tf_op jit(solution)/shard_map/all_gather | solution.py:368
  161.4 19.7 %convolution_convert_fusion.mixed_ref = bf16[1024,4608]{1,0:T(8,128)(2,1)S(1)} fusion(bf16[4608,1536]{1,0:T(8,128)(2,1)} %all-gather.6.cloned.1.call-done, f32[1024,1536]{1,0:T(8,128)} %get-tuple-element.46.embedded, f32[1536]{0:T(1024)S(1)} %reduce.3, f32[1024]{0:T(1024)S(1)} %add_rsqrt_fusion.1), kind=kOutput, calls=%fused_computation | convolution fusion | flops 14504951808 | bytes 29894656 | tf_op jit(solution)/shard_map/dot_general | solution.py:34
  181.1 6.4 %attention.1.context = bf16[1024,1536]{1,0:T(8,128)(2,1)S(1)} custom-call(bf16[1024,4608]{1,0:T(8,128)(2,1)S(1)} %convolution_convert_fusion.mixed_ref), custom_call_target="tpu_custom_call" | custom-call | flops 1610612736 | bytes 12582912 | tf_op jit(solution)/shard_map/attention/pallas_call | solution.py:79
  189.2 30.4 %all-gather.8.cloned.1.call-done.output = bf16[1536,1536]{1,0:T(8,128)(2,1)} async-done(((bf16[96,1536]{1,0:T(8,128)(2,1)}), bf16[1536,1536]{1,0:T(8,128)(2,1)}) %all-gather.8.cloned.1.call-update) | async-done | bytes 4718608 | tf_op jit(solution)/shard_map/all_gather | solution.py:368
  219.6 31.4 %head_backward.1 = (f32[8192,128]{1,0:T(8,128)}, f32[1536,128]{1,0:T(8,128)}, f32[1024,384]{1,0:T(8,128)}, f32[8,128]{1,0:T(8,128)}) custom-call(bf16[1024,1536]{1,0:T(8,128)(2,1)} %copy-done, f32[1024,1536]{1,0:T(8,128)} %get-tuple-element.46.embedded, bf16[1536,1536]{1,0:T(8,128)(2,1)} %all-gather.8.cloned.1.call-done.output, ...), custom_call_target="tpu_custom_call" | custom-call | flops 15703474176 | bytes 41943040 | tf_op jit(solution)/shard_map/head_backward/pallas_call | solution.py:168
  251.0 3.1 dynamic-slice_bitcast_fusion.1
  254.3 29.8 %trunk_backward.1 = f32[8192,128]{1,0:T(8,128)} custom-call(f32[1024,384]{1,0:T(8,128)} %get-tuple-element.17.d_hidden, f32[1024,1536]{1,0:T(8,128)} %get-tuple-element.28.slope, bf16[1536,384]{1,0:T(8,128)(2,1)} %get-tuple-element.34.down_hi, bf16[1536,384]{1,0:T(8,128)(2,1)} %get-tuple-element.33.down_lo, bf16[384,1536]{1,0:T(8,128)(2,1)} %copy-done.2, ...), custom_call_target="tpu_custom_call" | custom-call | flops 11878268928 | bytes 31457280 | tf_op jit(solution)/shard_map/trunk_backward/pallas_call | solution.py:247
  284.1 3.0 dynamic-slice_bitcast_fusion
  287.4 2.8 fusion.11
  290.2 7.3 %all-to-all-start.1 = ((bf16[64,64,128]{2,1,0:T(8,128)(2,1)}), bf16[64,64,128]{2,1,0:T(8,128)(2,1)S(1)}, u32[]{:S(2)}, u32[]{:S(2)}) async-start(bf16[64,64,128]{2,1,0:T(8,128)(2,1)} %bitcast.17), calls=%async_computation.1 | async-start | bytes 2097152 | tf_op jit(solution)/shard_map/all_to_all | solution.py:328
  297.5 3.4 fusion.10
  300.9 13.7 %all-to-all-done.1 = bf16[64,64,128]{2,1,0:T(8,128)(2,1)S(1)} async-done(((bf16[64,64,128]{2,1,0:T(8,128)(2,1)}), bf16[64,64,128]{2,1,0:T(8,128)(2,1)S(1)}, u32[]{:S(2)}, u32[]{:S(2)}) %all-to-all-start.1) | async-done | bytes 1048608 | tf_op jit(solution)/shard_map/all_to_all | solution.py:328
  314.6 5.5 %all-to-all-start.3 = ((bf16[64,64,128]{2,1,0:T(8,128)(2,1)}), bf16[64,64,128]{2,1,0:T(8,128)(2,1)S(1)}, u32[]{:S(2)}, u32[]{:S(2)}) async-start(bf16[64,64,128]{2,1,0:T(8,128)(2,1)} %bitcast.23), calls=%async_computation.3 | async-start | bytes 2097152 | tf_op jit(solution)/shard_map/all_to_all | solution.py:328
  320.4 16.0 %all-to-all-done.3 = bf16[64,64,128]{2,1,0:T(8,128)(2,1)S(1)} async-done(((bf16[64,64,128]{2,1,0:T(8,128)(2,1)}), bf16[64,64,128]{2,1,0:T(8,128)(2,1)S(1)}, u32[]{:S(2)}, u32[]{:S(2)}) %all-to-all-start.3) | async-done | bytes 1048608 | tf_op jit(solution)/shard_map/all_to_all | solution.py:328
  337.6 5.8 %all-to-all-start.2 = ((bf16[64,64,128]{2,1,0:T(8,128)(2,1)}), bf16[64,64,128]{2,1,0:T(8,128)(2,1)S(1)}, u32[]{:S(2)}, u32[]{:S(2)}) async-start(bf16[64,64,128]{2,1,0:T(8,128)(2,1)} %broadcast_in_dim.78), calls=%async_computation.2 | async-start | bytes 2097152 | tf_op jit(solution)/shard_map/all_to_all | solution.py:334
  349.2 10.6 %all-to-all-done.2 = bf16[64,64,128]{2,1,0:T(8,128)(2,1)S(1)} async-done(((bf16[64,64,128]{2,1,0:T(8,128)(2,1)}), bf16[64,64,128]{2,1,0:T(8,128)(2,1)S(1)}, u32[]{:S(2)}, u32[]{:S(2)}) %all-to-all-start.2) | async-done | bytes 1048608 | tf_op jit(solution)/shard_map/all_to_all | solution.py:334
  361.1 4.7 %all-to-all-start.4 = ((bf16[64,64,128]{2,1,0:T(8,128)(2,1)}), bf16[64,64,128]{2,1,0:T(8,128)(2,1)S(1)}, u32[]{:S(2)}, u32[]{:S(2)}) async-start(bf16[64,64,128]{2,1,0:T(8,128)(2,1)} %broadcast_in_dim.83), calls=%async_computation.4 | async-start | bytes 2097152 | tf_op jit(solution)/shard_map/all_to_all | solution.py:334
  365.8 3.4 collective-permute-start.1
  369.2 12.3 %all-to-all-done.4 = bf16[64,64,128]{2,1,0:T(8,128)(2,1)S(1)} async-done(((bf16[64,64,128]{2,1,0:T(8,128)(2,1)}), bf16[64,64,128]{2,1,0:T(8,128)(2,1)S(1)}, u32[]{:S(2)}, u32[]{:S(2)}) %all-to-all-start.4) | async-done | bytes 1048608 | tf_op jit(solution)/shard_map/all_to_all | solution.py:334
  381.5 3.8 collective-permute-start.3
  385.3 2.3 collective-permute-done.3.b_theirs
  388.6 6.3 %unpack_sums.1 = (f32[384,1536]{1,0:T(8,128)}, f32[1536,384]{1,0:T(8,128)}, f32[384,1536]{1,0:T(8,128)}, f32[588,384]{1,0:T(8,128)}, f32[8,128]{1,0:T(8,128)}, /*index=5*/f32[8,128]{1,0:T(8,128)}) custom-call(s32[1]{0:T(128)} %bitcast.core, bf16[4096,128]{1,0:T(8,128)(2,1)} %bitcast.68, bf16[4096,128]{1,0:T(8,128)(2,1)} %copy-done.21, ...), custom_call_target="tpu_custom_call" | custom-call | bytes 12582912 | tf_op jit(solution)/shard_map/unpack_sums/pallas_call | solution.py:311
  (100 shorter events, 34.6 us)
Async XLA Ops:
  7.2 9.9 %copy-start.25 = (s32[1,2]{1,0:T(1,128)S(1)}, s32[1,2]{1,0:T(1,128)}, u32[]{:S(2)}) copy-start(s32[1,2]{1,0:T(1,128)} %param.14) | copy-start | bytes 28
  7.2 70.1 %all-gather.4.cloned.1.call-start = ((), (), s32[]{:S(2)}) async-start(), calls=%async_computation.5 | async-start | bytes 2088960 | tf_op jit(solution)/shard_map/all_gather | solution.py:368
  8.8 152.6 %all-gather.6.cloned.1.call-start = ((), (), s32[]{:S(2)}) async-start(), calls=%async_computation.6 | async-start | bytes 15040512 | tf_op jit(solution)/shard_map/all_gather | solution.py:368
  20.4 25.0 %all-to-all-start = ((bf16[8,128,640]{2,1,0:T(8,128)(2,1)}), bf16[8,128,640]{2,1,0:T(8,128)(2,1)S(1)}, u32[]{:S(2)}, u32[]{:S(2)}) async-start(bf16[8,128,640]{2,1,0:T(8,128)(2,1)} %pad.12), calls=%async_computation | async-start | bytes 2621440 | tf_op jit(solution)/shard_map/all_to_all | solution.py:384
  26.7 192.9 %all-gather.8.cloned.1.call-start = ((), (), s32[]{:S(2)}) async-start(), calls=%async_computation.7 | async-start | bytes 5013504 | tf_op jit(solution)/shard_map/all_gather | solution.py:368
  27.5 3.1 copy-start.23
  27.5 3.7 copy-start.24
  30.5 19.7 %copy-start.2 = (bf16[384,1536]{1,0:T(8,128)(2,1)}, bf16[384,1536]{1,0:T(8,128)(2,1)S(1)}, u32[]{:S(2)}) copy-start(bf16[384,1536]{1,0:T(8,128)(2,1)S(1)} %get-tuple-element.36.up_hi) | copy-start | bytes 3538948
  31.2 3.6 copy-start.17
  34.8 10.6 %copy-start.14 = (f32[588,384]{1,0:T(8,128)S(1)}, f32[588,384]{1,0:T(8,128)}, u32[]{:S(2)}) copy-start(f32[588,384]{1,0:T(8,128)} %param.15) | copy-start | bytes 2709508
  45.4 31.9 %copy-start.1 = (bf16[8,128,640]{2,1,0:T(8,128)(2,1)}, bf16[8,128,640]{2,1,0:T(8,128)(2,1)S(1)}, u32[]{:S(2)}) copy-start(bf16[8,128,640]{2,1,0:T(8,128)(2,1)S(1)} %all-to-all-done) | copy-start | bytes 3932164
  47.7 2.6 copy-start.5
  47.7 2.6 copy-start.13
  48.4 3.6 copy-start.4
  52.1 6.5 %copy-start.20 = (bf16[1536,384]{1,0:T(8,128)(2,1)S(1)}, bf16[1536,384]{1,0:T(8,128)(2,1)}, u32[]{:S(2)}) copy-start(bf16[1536,384]{1,0:T(8,128)(2,1)} %get-tuple-element.34.down_hi) | copy-start | bytes 3538948
  58.6 2.9 copy-start.15
  62.6 4.2 %copy-start.7 = (f32[1024,384]{1,0:T(8,128)S(1)}, f32[1024,384]{1,0:T(8,128)}, u32[]{:S(2)}) copy-start(f32[1024,384]{1,0:T(8,128)} %copy-done.6) | copy-start | bytes 4718596
  62.6 4.2 %copy-start.16 = (bf16[1024,1536]{1,0:T(8,128)(2,1)S(1)}, bf16[1024,1536]{1,0:T(8,128)(2,1)}, u32[]{:S(2)}) copy-start(bf16[1024,1536]{1,0:T(8,128)(2,1)} %copy-done.15) | copy-start | bytes 9437188
  62.6 4.2 %copy-start.19 = (bf16[1536,384]{1,0:T(8,128)(2,1)S(1)}, bf16[1536,384]{1,0:T(8,128)(2,1)}, u32[]{:S(2)}) copy-start(bf16[1536,384]{1,0:T(8,128)(2,1)} %get-tuple-element.33.down_lo) | copy-start | bytes 3538948
  62.6 4.5 %copy-start.26 = (f32[1024,384]{1,0:T(8,128)S(1)}, f32[1024,384]{1,0:T(8,128)}, u32[]{:S(2)}) copy-start(f32[1024,384]{1,0:T(8,128)} %fusion.23) | copy-start | bytes 4718596
  69.1 3.6 copy-start.12
  254.0 33.4 %collective-permute-start = (f32[4096,128]{1,0:T(8,128)}, f32[4096,128]{1,0:T(8,128)S(1)}, u32[]{:S(2)}, u32[]{:S(2)}) collective-permute-start(f32[4096,128]{1,0:T(8,128)} %dynamic-slice_bitcast_fusion.1), channel_id=1, source_target_pairs={{0,8},{1,9},{2,10},{3,11},{4,12},{5,13},{6,14},{7,15},{8,0},{9,1},... | collective-permute-start | bytes 6291464 | tf_op jit(solution)/shard_map/ppermute | solution.py:102
  287.1 10.4 %collective-permute-start.2 = (f32[4096,128]{1,0:T(8,128)}, f32[4096,128]{1,0:T(8,128)}, u32[]{:S(2)}, u32[]{:S(2)}) collective-permute-start(f32[4096,128]{1,0:T(8,128)} %dynamic-slice_bitcast_fusion), channel_id=1, source_target_pairs={{0,8},{1,9},{2,10},{3,11},{4,12},{5,13},{6,14},{7,15},{8,0},{9,1},... | collective-permute-start | bytes 6291464 | tf_op jit(solution)/shard_map/ppermute | solution.py:102
  290.2 24.5 %all-to-all-start.1 = ((bf16[64,64,128]{2,1,0:T(8,128)(2,1)}), bf16[64,64,128]{2,1,0:T(8,128)(2,1)S(1)}, u32[]{:S(2)}, u32[]{:S(2)}) async-start(bf16[64,64,128]{2,1,0:T(8,128)(2,1)} %bitcast.17), calls=%async_computation.1 | async-start | bytes 2097152 | tf_op jit(solution)/shard_map/all_to_all | solution.py:328
  314.6 21.8 %all-to-all-start.3 = ((bf16[64,64,128]{2,1,0:T(8,128)(2,1)}), bf16[64,64,128]{2,1,0:T(8,128)(2,1)S(1)}, u32[]{:S(2)}, u32[]{:S(2)}) async-start(bf16[64,64,128]{2,1,0:T(8,128)(2,1)} %bitcast.23), calls=%async_computation.3 | async-start | bytes 2097152 | tf_op jit(solution)/shard_map/all_to_all | solution.py:328
  337.6 22.2 %all-to-all-start.2 = ((bf16[64,64,128]{2,1,0:T(8,128)(2,1)}), bf16[64,64,128]{2,1,0:T(8,128)(2,1)S(1)}, u32[]{:S(2)}, u32[]{:S(2)}) async-start(bf16[64,64,128]{2,1,0:T(8,128)(2,1)} %broadcast_in_dim.78), calls=%async_computation.2 | async-start | bytes 2097152 | tf_op jit(solution)/shard_map/all_to_all | solution.py:334
  359.8 27.8 %copy-start.10 = (bf16[64,64,128]{2,1,0:T(8,128)(2,1)}, bf16[64,64,128]{2,1,0:T(8,128)(2,1)S(1)}, u32[]{:S(2)}) copy-start(bf16[64,64,128]{2,1,0:T(8,128)(2,1)S(1)} %all-to-all-done.2) | copy-start | bytes 3145732
  361.1 20.4 %all-to-all-start.4 = ((bf16[64,64,128]{2,1,0:T(8,128)(2,1)}), bf16[64,64,128]{2,1,0:T(8,128)(2,1)S(1)}, u32[]{:S(2)}, u32[]{:S(2)}) async-start(bf16[64,64,128]{2,1,0:T(8,128)(2,1)} %broadcast_in_dim.83), calls=%async_computation.4 | async-start | bytes 2097152 | tf_op jit(solution)/shard_map/all_to_all | solution.py:334
  365.8 19.5 %collective-permute-start.1 = (bf16[4096,128]{1,0:T(8,128)(2,1)S(1)}, bf16[4096,128]{1,0:T(8,128)(2,1)S(1)}, u32[]{:S(2)}, u32[]{:S(2)}) collective-permute-start(bf16[4096,128]{1,0:T(8,128)(2,1)S(1)} %bitcast.67), channel_id=1, source_target_pairs={{0,8},{1,9},{2,10},{3,11},{4,12},{5,13},{6,14},{7,15},{8,0},{9,1},... | collective-permute-start | bytes 3145736 | tf_op jit(solution)/shard_map/ppermute | solution.py:102
  381.5 6.1 %copy-start.11 = (bf16[64,64,128]{2,1,0:T(8,128)(2,1)}, bf16[64,64,128]{2,1,0:T(8,128)(2,1)S(1)}, u32[]{:S(2)}) copy-start(bf16[64,64,128]{2,1,0:T(8,128)(2,1)S(1)} %all-to-all-done.4) | copy-start | bytes 3145732
  381.5 6.1 %collective-permute-start.3 = (bf16[4096,128]{1,0:T(8,128)(2,1)S(1)}, bf16[4096,128]{1,0:T(8,128)(2,1)S(1)}, u32[]{:S(2)}, u32[]{:S(2)}) collective-permute-start(bf16[4096,128]{1,0:T(8,128)(2,1)S(1)} %bitcast.69), channel_id=1, source_target_pairs={{0,8},{1,9},{2,10},{3,11},{4,12},{5,13},{6,14},{7,15},{8,0},{9,1},... | collective-permute-start | bytes 3145736 | tf_op jit(solution)/shard_map/ppermute | solution.py:102
  385.3 2.3 copy-start.21
  (7 other events, 11.3 us)
Sparse Core Ops, SparseCore 0:
  10.4 52.2 all-gather.3
  65.1 96.2 all-gather.5
  163.8 55.7 all-gather.7
where the time goes:
time: 412 us; the launch traced here: 406 us
  waiting for transfers between devices  174 us (42%)
  Pallas kernels  73.8 us (18%)
  matrix products  54.9 us (13%)
  starting transfers between devices  37.6 us (9%)
  between operations  23.9 us (6%)
  local copies, waits for them, and re-layouts  22.1 us (5%)
  other arithmetic  20.2 us (5%)
    all_gather x3, waiting for transfers between devices, gathered(): return lax.all_gather(shard, 'student', axis=0, tiled=True)  109 us
    dot_general x13, matrix products, bf16_dot(): lax.dot_general(left, right, dims, preferred_element_type=jnp.float32)  54.9 us
    pallas_call x1, Pallas kernels, head_backward(): pl.pallas_call(head_kernel, grid=(rows // block,), in_specs=[by_row(D_T),...  31.4 us
    pallas_call x1, Pallas kernels, trunk_backward(): pl.pallas_call(trunk_kernel, grid=(S_HID // tile,), in_specs=[whole(d_hid...  29.8 us
    all_to_all x2, waiting for transfers between devices, scatter_sum(): lax.all_to_all(sent, BOTH, 0, 0, axis_index_groups=core_groups(), tiled=T...  29.7 us
    all_to_all x2, waiting for transfers between devices, spread_chunk(): lax.all_to_all(spread, BOTH, 0, 0, axis_index_groups=core_groups(), tiled...  22.9 us
    all_to_all x2, starting transfers between devices, scatter_sum(): lax.all_to_all(sent, BOTH, 0, 0, axis_index_groups=core_groups(), tiled=T...  12.9 us
    all_to_all x2, starting transfers between devices, spread_chunk(): lax.all_to_all(spread, BOTH, 0, 0, axis_index_groups=core_groups(), tiled...  10.5 us
  transfers between devices with their start and end apart: 12, of which 8 were waited for; matrix products, arithmetic and copies ran while one was open for 21% of the time, Pallas kernels for 9%

commit v1 on v0

--- a/solution.py
+++ b/solution.py
@@ -18,6 +18,14 @@
 D_T = 1536
 S_HID = 1536
 BLK = 128
+P_ROWS = 288
+O_ROWS = 96
+NEAR = 12
+FAR = 4
+CUT = 192
+REST = P_ROWS - CUT
+STUDENTS = 16
+EMBED_PACK = 48
 RANKS = DEVICES // 2
 CHUNK = 64
 SUM_ROWS = 2 * RANKS * CHUNK
@@ -46,18 +54,19 @@
     )
 
 
-def attention_kernel(mixed_ref, out_ref):
+def attend_block(mixed, at, out, base):
     lane = lax.broadcasted_iota(jnp.int32, (BLK, PAIR), 1)
     first = lane < HDIM
     zero = jnp.zeros((BLK, PAIR), jnp.bfloat16)
     ones = jnp.concatenate(
         [jnp.where(first, 1.0, 0.0), jnp.where(first, 0.0, 1.0)], axis=0
     ).astype(jnp.bfloat16)
+    rows = pl.ds(at, BLK)
     for pair in range(HEADS // 2):
-        at = pair * PAIR
-        queries = mixed_ref[:, at : at + PAIR]
-        keys = mixed_ref[:, D_T + at : D_T + at + PAIR]
-        values = mixed_ref[:, 2 * D_T + at : 2 * D_T + at + PAIR]
+        start = pair * PAIR
+        queries = mixed[rows, start : start + PAIR]
+        keys = mixed[rows, D_T + start : D_T + start + PAIR]
+        values = mixed[rows, 2 * D_T + start : 2 * D_T + start + PAIR]
         keys_two = jnp.concatenate(
             [jnp.where(first, keys, zero), jnp.where(first, zero, keys)], axis=0
         )
@@ -71,23 +80,125 @@
         right = jnp.exp((right - jnp.max(right, axis=1, keepdims=True)) * scale)
         weights = jnp.concatenate([left, right], axis=1).astype(jnp.bfloat16)
         summed = bf16_dot(weights, jnp.concatenate([values_two, ones], axis=1), NN)
-        out_ref[:, at : at + PAIR] = (summed[:, :PAIR] / summed[:, PAIR:]).astype(jnp.bfloat16)
-
-
-def attend(mixed):
-    rows, total = mixed.shape
+        out[rows, start : start + PAIR] = (summed[:, :PAIR] / summed[:, PAIR:]).astype(jnp.bfloat16)
+
+
+def shard_copies(plan, owners, target, semaphores, count):
+    copies = []
+    for i, (piece, start, rows, row) in enumerate(plan):
+        at = pl.multiple_of(owners[i] * count + row, 16)
+        copies.append(
+            pltpu.make_async_copy(
+                piece.at[pl.ds(start, rows)], target.at[pl.ds(at, rows)], semaphores.at[i]
+            )
+        )
+    return copies
+
+
+def teacher_kernel(owners, rows, gain, gathered, *rest):
+    pieces, rest = rest[: NEAR + FAR], rest[NEAR + FAR :]
+    embedded, context, embed, project, normed, mixed, semaphores, others = rest
+    wide = D_T // 2
+    first = [
+        pltpu.make_async_copy(
+            gathered.at[:, pl.ds(CUT, EMBED_PACK), pl.ds(i * wide, wide)], embed.at[:, i], others.at[i]
+        )
+        for i in range(2)
+    ]
+    for copy in first:
+        copy.start()
+    copies = [
+        pltpu.make_async_copy(
+            gathered.at[i, pl.ds(0, CUT)], project.at[pl.ds(i * P_ROWS, CUT)], others.at[2 + i]
+        )
+        for i in range(STUDENTS)
+    ]
+    plan = [(piece, 0, P_ROWS - CUT, CUT) for piece in pieces]
+    copies += shard_copies(plan, owners, project, semaphores, P_ROWS)
+    for copy in copies:
+        copy.start()
+    for copy in first:
+        copy.wait()
+    step = 2 * BLK
+
+    @pl.loop(0, rows.shape[0] // step)
+    def _(r):
+        at = pl.ds(pl.multiple_of(r * step, step), step)
+        weights = embed[...].reshape(D_T, wide)[:, :PIX_PAD]
+        product = bf16_dot(rows[at, :], weights, NT)
+        embedded[at, :] = product
+        normed[at, :] = (product * scale_of(product) * gain[...]).astype(jnp.bfloat16)
+
+    for copy in copies:
+        copy.wait()
+    tile = 512
+
+    @pl.loop(0, 3 * D_T // tile)
+    def _(n):
+        at = pl.ds(pl.multiple_of(n * tile, tile), tile)
+        mixed[:, at] = bf16_dot(normed[...], project[at, :], NT).astype(jnp.bfloat16)
+
+    @pl.loop(0, rows.shape[0] // BLK)
+    def _(b):
+        at = pl.multiple_of(b * BLK, BLK)
+        attend_block(mixed, at, context, at)
+
+
+def teach(owners, rows, gain, gathered, pieces):
+    count = rows.shape[0]
+    vmem = pl.BlockSpec(memory_space=pltpu.VMEM)
     return pl.pallas_call(
-        attention_kernel,
-        grid=(rows // BLK,),
-        in_specs=[pl.BlockSpec((BLK, total), lambda b: (b, 0))],
-        out_specs=pl.BlockSpec((BLK, D_T), lambda b: (b, 0)),
-        out_shape=jax.ShapeDtypeStruct((rows, D_T), jnp.bfloat16),
-        compiler_params=pltpu.CompilerParams(vmem_limit_bytes=32 * 1024 * 1024),
+        teacher_kernel,
+        in_specs=[pl.BlockSpec(memory_space=pltpu.SMEM)] + [vmem] * 2
+        + [pl.BlockSpec(memory_space=pl.ANY)] * (1 + NEAR + FAR),
+        out_specs=[vmem] * 2,
+        out_shape=[
+            jax.ShapeDtypeStruct((count, D_T), jnp.float32),
+            jax.ShapeDtypeStruct((count, D_T), jnp.bfloat16),
+        ],
+        scratch_shapes=[
+            pltpu.VMEM((STUDENTS, 2, EMBED_PACK, D_T // 2), jnp.bfloat16),
+            pltpu.VMEM((3 * D_T, D_T), jnp.bfloat16),
+            pltpu.VMEM((count, D_T), jnp.bfloat16),
+            pltpu.VMEM((count, 3 * D_T), jnp.bfloat16),
+            pltpu.SemaphoreType.DMA((NEAR + FAR,)),
+            pltpu.SemaphoreType.DMA((2 + STUDENTS,)),
+        ],
+        compiler_params=pltpu.CompilerParams(vmem_limit_bytes=58 * 1024 * 1024),
         cost_estimate=pl.CostEstimate(
-            flops=rows * BLK * D_T * 8, bytes_accessed=rows * D_T * 8, transcendentals=rows * BLK * HEADS
+            flops=2 * count * D_T * (PIX_PAD + 3 * D_T), bytes_accessed=30 * 1024 * 1024, transcendentals=0
         ),
-        name="attention",
-    )(mixed)
+        name="teacher",
+    )(owners, rows, gain, gathered, *pieces)
+
+
+def place(device):
+    student, pool = device // 8, device % 8
+    return [student // 4, student // 2 % 2, student % 2, pool]
+
+
+def moved(values, x=0, z=0, core=0):
+    pairs = []
+    for device in range(DEVICES):
+        at = place(device)
+        student = ((at[0] + x) % 4 * 2 + (at[1] ^ z)) * 2 + (at[2] ^ core)
+        pairs.append((device, student * 8 + at[3]))
+    return lax.ppermute(values, BOTH, pairs)
+
+
+def with_core(pieces):
+    return pieces + [moved(values, core=1) for values in pieces]
+
+
+def shard_owners():
+    x, z, core, _ = place(lax.axis_index("student") * 8)
+
+    def index(dx, dz, dc):
+        return (lax.rem(x + dx + 4, 4) * 2 + (z + dz) % 2) * 2 + (core + dc) % 2
+
+    near = [index(dx, dz, dc) for dc in range(2) for dx in (0, -1, 1) for dz in range(2)]
+    far = [index(2, dz, dc) for dc in range(2) for dz in range(2)]
+    return jnp.stack(near + far).astype(jnp.int32)
 
 
 def core_groups():
@@ -123,12 +234,35 @@
     return lax.rsqrt(jnp.mean(values * values, axis=1, keepdims=True) + EPSILON)
 
 
+def hand_over(core, sums, mine, other, done):
+    half = SUM_ROWS // 2
+    at = pl.multiple_of(core * half, half)
+    across = pl.multiple_of((1 - core) * half, half)
+    copies = [
+        pltpu.make_async_copy(sums.at[pl.ds(across, half)], other, done.at[0]),
+        pltpu.make_async_copy(sums.at[pl.ds(at, half)], mine, done.at[1]),
+    ]
+    for copy in copies:
+        copy.start()
+    for copy in copies:
+        copy.wait()
+
+
 def head_kernel(
-    context, embedded, output, student_out, hidden_hi, hidden_lo, act_hi, act_lo, head_hi, head_lo,
-    sums, down_rest, d_hidden_out, total,
+    core, owners, context, embedded, student_out, hidden_hi, hidden_lo, act_hi, act_lo, head_hi, head_lo,
+    *rest,
 ):
+    pieces, rest = rest[: NEAR + FAR], rest[NEAR + FAR :]
+    mine, other, down_rest, d_hidden_out, total, sums, output, semaphores, done = rest
+
     @pl.when(pl.program_id(0) == 0)
     def _():
+        plan = [(piece, REST if i < NEAR else 0, O_ROWS, 0) for i, piece in enumerate(pieces)]
+        copies = shard_copies(plan, owners, output, semaphores, O_ROWS)
+        for copy in copies:
+            copy.start()
+        for copy in copies:
+            copy.wait()
         sums[...] = jnp.zeros_like(sums)
         down_rest[...] = jnp.zeros_like(down_rest)
         total[...] = jnp.zeros_like(total)
@@ -154,8 +288,12 @@
         sums[at + i * S_HID : at + (i + 1) * S_HID, :] += grad_down[:, i * LANES : (i + 1) * LANES]
     down_rest[...] += grad_down[:, 2 * LANES :]
 
-
-def head_backward(context, embedded, output, student_out, hidden, act, head):
+    @pl.when(pl.program_id(0) == pl.num_programs(0) - 1)
+    def _():
+        hand_over(core[0], sums, mine, other, done)
+
+
+def head_backward(core, owners, context, embedded, student_out, hidden, act, head, pieces):
     rows = context.shape[0]
     block = 256
 
@@ -169,27 +307,38 @@
         head_kernel,
         grid=(rows // block,),
         in_specs=[
-            by_row(D_T), by_row(D_T), whole((D_T, D_T)), by_row(D_T), by_row(D_S), by_row(D_S),
+            pl.BlockSpec(memory_space=pltpu.SMEM),
+            pl.BlockSpec(memory_space=pltpu.SMEM),
+            by_row(D_T), by_row(D_T), by_row(D_T), by_row(D_S), by_row(D_S),
             by_row(S_HID), by_row(S_HID), whole((D_S, D_T)), whole((D_S, D_T)),
-        ],
-        out_specs=[whole((SUM_ROWS, LANES)), whole((S_HID, LANES)), by_row(D_S), whole((8, LANES))],
+        ]
+        + [pl.BlockSpec(memory_space=pl.ANY)] * (NEAR + FAR),
+        out_specs=[pl.BlockSpec(memory_space=pl.ANY)] * 2
+        + [whole((S_HID, LANES)), by_row(D_S), whole((8, LANES))],
         out_shape=[
-            jax.ShapeDtypeStruct((SUM_ROWS, LANES), jnp.float32),
+            jax.ShapeDtypeStruct((SUM_ROWS // 2, LANES), jnp.float32),
+            jax.ShapeDtypeStruct((SUM_ROWS // 2, LANES), jnp.float32),
             jax.ShapeDtypeStruct((S_HID, LANES), jnp.float32),
             jax.ShapeDtypeStruct((rows, D_S), jnp.float32),
             jax.ShapeDtypeStruct((8, LANES), jnp.float32),
+        ],
+        scratch_shapes=[
+            pltpu.VMEM((SUM_ROWS, LANES), jnp.float32),
+            pltpu.VMEM((D_T, D_T), jnp.bfloat16),
+            pltpu.SemaphoreType.DMA((NEAR + FAR,)),
+            pltpu.SemaphoreType.DMA((2,)),
         ],
         compiler_params=pltpu.CompilerParams(vmem_limit_bytes=56 * 1024 * 1024),
         cost_estimate=pl.CostEstimate(
             flops=2 * rows * D_T * (D_T + 9 * D_S), bytes_accessed=40 * 1024 * 1024, transcendentals=0
         ),
         name="head_backward",
-    )(context, embedded, output, student_out, *hidden, *act, *head)
+    )(core, owners, context, embedded, student_out, *hidden, *act, *head, *pieces)
 
 
 def trunk_kernel(
-    d_hidden, slope, down_hi, down_lo, up_hi, up_lo, normed_hi, normed_lo, unit, scale, gain, rows,
-    down_rest, total, sums, dh_hi, dh_lo, d_normed,
+    core, d_hidden, slope, down_hi, down_lo, up_hi, up_lo, normed_hi, normed_lo, unit, scale, gain, rows,
+    down_rest, total, mine, other, sums, dh_hi, dh_lo, d_normed, done,
 ):
     step = pl.program_id(0)
     tile = slope.shape[1]
@@ -233,9 +382,10 @@
             jnp.where(lane == 1, second.astype(jnp.float32), third.astype(jnp.float32)),
         )
         sums[SUM_ROWS - 1 :, :] = jnp.where(lane < 3, row, 0.0)
-
-
-def trunk_backward(d_hidden, slope, down, up, normed, unit, scale, gain, rows, down_rest, total):
+        hand_over(core[0], sums, mine, other, done)
+
+
+def trunk_backward(core, d_hidden, slope, down, up, normed, unit, scale, gain, rows, down_rest, total):
     count = d_hidden.shape[0]
     tile = 256
 
@@ -248,91 +398,91 @@
         trunk_kernel,
         grid=(S_HID // tile,),
         in_specs=[
+            pl.BlockSpec(memory_space=pltpu.SMEM),
             whole(d_hidden), pl.BlockSpec((count, tile), lambda j: (0, j)),
             down_spec, down_spec, up_spec, up_spec,
             whole(normed[0]), whole(normed[1]), whole(unit), whole(scale), whole(gain), whole(rows),
             whole(down_rest), whole(total),
         ],
-        out_specs=pl.BlockSpec((SUM_ROWS, LANES), lambda j: (0, 0)),
-        out_shape=jax.ShapeDtypeStruct((SUM_ROWS, LANES), jnp.float32),
+        out_specs=[pl.BlockSpec(memory_space=pl.ANY)] * 2,
+        out_shape=[jax.ShapeDtypeStruct((SUM_ROWS // 2, LANES), jnp.float32)] * 2,
         scratch_shapes=[
+            pltpu.VMEM((SUM_ROWS, LANES), jnp.float32),
             pltpu.VMEM((count, D_S), jnp.bfloat16),
             pltpu.VMEM((count, D_S), jnp.bfloat16),
             pltpu.VMEM((count, D_S), jnp.float32),
+            pltpu.SemaphoreType.DMA((2,)),
         ],
         compiler_params=pltpu.CompilerParams(vmem_limit_bytes=56 * 1024 * 1024),
         cost_estimate=pl.CostEstimate(
             flops=2 * count * D_S * (9 * S_HID + 2 * PIX_PAD), bytes_accessed=30 * 1024 * 1024, transcendentals=0
         ),
         name="trunk_backward",
-    )(d_hidden, slope, *down, *up, *normed, unit, scale, gain, rows, down_rest, total)
-
-
-def unpack_kernel(core, a_mine, a_theirs, b_mine, b_theirs, head, down, up, embed, gain, total):
-    def unpack(a_low, a_high, b_low, b_high):
-        half = SUM_ROWS // 2
-
-        def take(low, high, start, count):
-            stop = start + count
-            parts = []
-            if start < half:
-                parts.append(low[start : min(stop, half), :])
-            if stop > half:
-                parts.append(high[max(start, half) - half : stop - half, :])
-            parts = [part.astype(jnp.float32) for part in parts]
-            return parts[0] if len(parts) == 1 else jnp.concatenate(parts, axis=0)
+    )(core, d_hidden, slope, *down, *up, *normed, unit, scale, gain, rows, down_rest, total)
+
+
+def unpack_kernel(core, mine, theirs, head, down, up, embed, gain, total):
+    def unpack(low, high):
+        def take(part, start, count):
+            pieces, stop = [], start + count
+            while start < stop:
+                rank, row = start // CHUNK, start % CHUNK
+                ref = low if rank < RANKS else high
+                size = min(CHUNK - row, stop - start)
+                at = part * CHUNK + row
+                pieces.append(ref[rank % RANKS, at : at + size, :].astype(jnp.float32))
+                start += size
+            return pieces[0] if len(pieces) == 1 else jnp.concatenate(pieces, axis=0)
 
         for i in range(D_T // LANES):
             columns = slice(i * LANES, (i + 1) * LANES)
-            head[:, columns] = take(a_low, a_high, i * D_S, D_S)
-            up[:, columns] = take(b_low, b_high, UP_AT + i * D_S, D_S)
+            head[:, columns] = take(0, i * D_S, D_S)
+            up[:, columns] = take(1, UP_AT + i * D_S, D_S)
         at = D_S * D_T // LANES
         for i in range(2):
-            down[:, i * LANES : (i + 1) * LANES] = take(a_low, a_high, at + i * S_HID, S_HID)
-        down[:, 2 * LANES :] = take(b_low, b_high, 0, S_HID)
+            down[:, i * LANES : (i + 1) * LANES] = take(0, at + i * S_HID, S_HID)
+        down[:, 2 * LANES :] = take(1, 0, S_HID)
         for i in range(D_S // LANES):
             columns = slice(i * LANES, (i + 1) * LANES)
-            embed[:, columns] = take(b_low, b_high, EMBED_AT + i * EMBED_ROWS, EMBED_ROWS)[:PIX]
-        gain[...] = take(b_low, b_high, GAIN_AT, 16)[:8]
-        total[...] = take(b_low, b_high, SUM_ROWS - 16, 16)[8:]
+            embed[:, columns] = take(1, EMBED_AT + i * EMBED_ROWS, EMBED_ROWS)[:PIX]
+        gain[...] = take(1, GAIN_AT, 16)[:8]
+        total[...] = take(1, SUM_ROWS - 16, 16)[8:]
 
     @pl.when(core[0] == 0)
     def _():
-        unpack(a_mine, a_theirs, b_mine, b_theirs)
+        unpack(mine, theirs)
 
     @pl.when(core[0] == 1)
     def _():
-        unpack(a_theirs, a_mine, b_theirs, b_mine)
-
-
-def unpack_sums(core, a_mine, a_theirs, b_mine, b_theirs):
+        unpack(theirs, mine)
+
+
+def unpack_sums(core, mine, theirs):
     vmem = pl.BlockSpec(memory_space=pltpu.VMEM)
     shapes = [(D_S, D_T), (S_HID, D_S), (D_S, S_HID), (PIX, D_S), (8, LANES), (8, LANES)]
     return pl.pallas_call(
         unpack_kernel,
-        in_specs=[pl.BlockSpec(memory_space=pltpu.SMEM)] + [vmem] * 4,
+        in_specs=[pl.BlockSpec(memory_space=pltpu.SMEM)] + [vmem] * 2,
         out_specs=[vmem] * 6,
         out_shape=[jax.ShapeDtypeStruct(shape, jnp.float32) for shape in shapes],
         compiler_params=pltpu.CompilerParams(vmem_limit_bytes=56 * 1024 * 1024),
         cost_estimate=pl.CostEstimate(flops=0, bytes_accessed=12 * 1024 * 1024, transcendentals=0),
         name="unpack_sums",
-    )(core.reshape(1), a_mine, a_theirs, b_mine, b_theirs)
-
-
-def scatter_sum(sums, core):
-    halves = sums.reshape(2, SUM_ROWS // 2, LANES)
-    mine = lax.dynamic_index_in_dim(halves, core, 0, keepdims=False)
-    other = lax.dynamic_index_in_dim(halves, 1 - core, 0, keepdims=False)
-    mine = mine + core_swap(other)
-    sent = mine.astype(jnp.bfloat16).reshape(RANKS, CHUNK, LANES)
+    )(core, mine, theirs)
+
+
+def core_sum(mine, other):
+    return (mine + core_swap(other)).astype(jnp.bfloat16).reshape(RANKS, CHUNK, LANES)
+
+
+def chunk_sum(sent):
     got = lax.all_to_all(sent, BOTH, 0, 0, axis_index_groups=core_groups(), tiled=True)
     return jnp.sum(got.astype(jnp.float32), axis=0)
 
 
 def spread_chunk(chunk):
-    spread = jnp.broadcast_to(chunk.astype(jnp.bfloat16)[None], (RANKS, CHUNK, LANES))
+    spread = jnp.broadcast_to(chunk[None], (RANKS,) + chunk.shape)
     half = lax.all_to_all(spread, BOTH, 0, 0, axis_index_groups=core_groups(), tiled=True)
-    half = half.reshape(SUM_ROWS // 2, LANES)
     return half, core_swap(half)
 
 
@@ -364,12 +514,16 @@
 ):
     pool_size = lax.axis_size("pool")
 
-    def gathered(shard):
-        return lax.all_gather(shard, "student", axis=0, tiled=True)
-
-    embed_full = gathered(jnp.pad(teacher_embed[0].T, ((0, 0), (0, PIX_PAD - PIX))))
-    project_full = gathered(teacher_project[0].T)
-    output_full = gathered(teacher_output[0].T)
+    project = teacher_project[0].T
+    embed_shard = jnp.pad(teacher_embed[0].T, ((0, 0), (0, D_T // 2 - PIX)))
+    embed_shard = jnp.concatenate([embed_shard[:EMBED_PACK], embed_shard[EMBED_PACK:]], axis=1)
+    gathered = lax.all_gather(
+        jnp.concatenate([project[:CUT], embed_shard], axis=0), "student", axis=0, tiled=False
+    )
+    shard = jnp.concatenate([project[CUT:], teacher_output[0].T], axis=0)
+    first = [moved(shard, z=1), moved(shard, x=1), moved(shard, x=-1)]
+
+    owners = shard_owners()
 
     teachers = jnp.arange(pool_size, dtype=jnp.int32)[:, None, None]
     chosen = [
@@ -381,41 +535,50 @@
         jnp.where(destination[0, 1] == teachers, chosen[1], jnp.zeros((), jnp.bfloat16)),
     )
     outgoing = jnp.pad(outgoing, ((0, 0), (0, 0), (0, PIX_PAD - PIX)))
+    up, down, head = halves_of(student_up), halves_of(student_down), halves_of(student_head)
+    embed = halves_of(jnp.pad(student_embed, ((0, PIX_PAD - PIX), (0, 0))))
+    outgoing, up, down, head, embed, *first = lax.optimization_barrier(
+        (outgoing, up, down, head, embed, *first)
+    )
+    across, back, ahead = first
+    second = [
+        moved(across, x=1), moved(across, x=-1), moved(back[:REST], x=1), moved(ahead[REST:], x=-1)
+    ]
     arrived = lax.all_to_all(outgoing, "pool", split_axis=0, concat_axis=0, tiled=True)
     rows = arrived.reshape(pool_size * BLK, PIX_PAD)
 
-    embed = jnp.pad(student_embed, ((0, PIX_PAD - PIX), (0, 0)))
-    embed = halves_of(embed)
     lifted = bf16_dot(rows, embed[0], NN) + bf16_dot(rows, embed[1], NN)
     scale = rms_scale(lifted)
     unit = lifted * scale
     normed_s = halves_of(unit * student_gain)
-    up = halves_of(student_up)
-    down = halves_of(student_down)
-    head = halves_of(student_head)
     pre = halved_dot(normed_s, up)
     cdf = 0.5 * (1.0 + lax.erf(pre * (2.0**-0.5)))
     act = halves_of(pre * cdf)
     slope = cdf + pre * jnp.exp(-0.5 * pre * pre) * ((2.0 * jnp.pi) ** -0.5)
+    act, slope, *second = lax.optimization_barrier((act, slope, *second))
+    back_across, ahead_across, low_near, high_near = second
+    low = with_core([low_near, moved(back_across[:REST], x=1)])
+    high = with_core([high_near, moved(ahead_across[REST:], x=-1)])
+    near = with_core([shard, across, back, back_across, ahead, ahead_across])
     hidden = halves_of(lifted + halved_dot(act, down))
     student_out = halved_dot(hidden, head)
 
-    embedded = bf16_dot(rows, embed_full, NT)
-    normed = (embedded * rms_scale(embedded) * teacher_gain[0]).astype(jnp.bfloat16)
-    mixed = bf16_dot(normed, project_full, NT).astype(jnp.bfloat16)
-    context = attend(mixed)
-
+    embedded, context = teach(owners, rows, teacher_gain, gathered, near + low)
     core = lax.rem(lax.axis_index("student"), 2)
-    sums_a, down_rest, d_hidden, total = head_backward(
-        context, embedded, output_full, student_out, hidden, act, head
-    )
-    chunk_a = scatter_sum(sums_a, core)
+    core = core.reshape(1)
+    *sums_a, down_rest, d_hidden, total = head_backward(
+        core, owners, context, embedded, student_out, hidden, act, head, near + high
+    )
+    sent_a, d_hidden = lax.optimization_barrier((core_sum(*sums_a), d_hidden))
+    chunk_a = chunk_sum(sent_a)
     sums_b = trunk_backward(
-        d_hidden, slope, down, up, normed_s, unit, scale, student_gain[None], rows, down_rest, total
-    )
-    chunk_b = keep_total(scatter_sum(sums_b, core), core)
+        core, d_hidden, slope, down, up, normed_s, unit, scale, student_gain[None], rows, down_rest, total
+    )
+    chunk_a, *sums_b = lax.optimization_barrier((chunk_a, *sums_b))
+    chunk_b = keep_total(chunk_sum(core_sum(*sums_b)), core[0])
+    chunks = jnp.concatenate([chunk_a.astype(jnp.bfloat16), chunk_b.astype(jnp.bfloat16)], axis=0)
     head_sum, down_sum, up_sum, embed_sum, gain_sum, cosine_sum = unpack_sums(
-        core, *spread_chunk(chunk_a), *spread_chunk(chunk_b)
+        core, *spread_chunk(chunks)
     )
     gain_sum = gain_sum[: D_S // LANES].reshape(D_S)
     mean_distance = 1.0 - jnp.sum(cosine_sum[7, :3]) / (DEVICES * 2 * BLK)

time: 412 us -> 329 us (0.80)
  waiting for transfers between devices: 174 us -> 43.7 us
  blocking collectives: 0 us -> 32.1 us
  matrix products: 54.9 us -> 24.3 us
  Pallas kernels: 73.8 us -> 102 us
  starting transfers between devices: 37.6 us -> 54.7 us
    all_gather x3 -> x1, waiting for transfers between devices: 109 us -> 0.01 us  [on_device(): lax.all_gather(jnp.concatenate([project[:CUT], embed_shard], axis=0), 'st...]
    all_to_all x4 -> x2, waiting for transfers between devices: 52.6 us -> 17 us  [chunk_sum(): lax.all_to_all(sent, BOTH, 0, 0, axis_index_groups=core_groups(), tiled=T...]
    all_to_all x0 -> x1, blocking collectives: none -> 32.1 us  [spread_chunk(): lax.all_to_all(spread, BOTH, 0, 0, axis_index_groups=core_groups(), tiled...]
    dot_general x13 -> x11, matrix products: 54.9 us -> 24.3 us  [bf16_dot(): lax.dot_general(left, right, dims, preferred_element_type=jnp.float32)]
    pallas_call x3, Pallas kernels: 67.6 us -> 95.9 us  [the longest x1 33.4 us: head_backward(): pl.pallas_call(head_kernel, grid=(rows // block,), in_specs=[pl.BlockSpec...]
    ppermute x0 -> x19, starting transfers between devices: none -> 26.5 us  [moved(): return lax.ppermute(values, BOTH, pairs)]
    ppermute x0 -> x19, waiting for transfers between devices: none -> 15.8 us  [moved(): return lax.ppermute(values, BOTH, pairs)]
    all_to_all x1, waiting for transfers between devices: 8.81 us -> 0.29 us  [on_device(): lax.all_to_all(outgoing, 'pool', split_axis=0, concat_axis=0, tiled=True)]
  transfers between devices with their start and end apart: 12 -> 26, of which waited for: 8 -> 8; matrix products, arithmetic and copies ran while one was open for 21% -> 14% of each run, Pallas kernels for 9% -> 19%
where the time goes in v1:
time: 329 us; the launch traced here: 323 us
  Pallas kernels  102 us (31%)
  starting transfers between devices  54.7 us (17%)
  waiting for transfers between devices  43.7 us (13%)
  blocking collectives  32.1 us (10%)
  matrix products  24.3 us (7%)
  between operations  24.2 us (7%)
  local copies, waits for them, and re-layouts  23.3 us (7%)
  other arithmetic  18.7 us (6%)
    pallas_call x1, Pallas kernels, head_backward(): pl.pallas_call(head_kernel, grid=(rows // block,), in_specs=[pl.BlockSpec...  33.4 us
    pallas_call x1, Pallas kernels, teach(): pl.pallas_call(teacher_kernel, in_specs=[pl.BlockSpec(memory_space=pltpu....  32.9 us
    all_to_all x1, blocking collectives, spread_chunk(): lax.all_to_all(spread, BOTH, 0, 0, axis_index_groups=core_groups(), tiled...  32.1 us
    pallas_call x1, Pallas kernels, trunk_backward(): pl.pallas_call(trunk_kernel, grid=(S_HID // tile,), in_specs=[pl.BlockSpe...  29.5 us
    ppermute x19, starting transfers between devices, moved(): return lax.ppermute(values, BOTH, pairs)  26.5 us
    dot_general x11, matrix products, bf16_dot(): lax.dot_general(left, right, dims, preferred_element_type=jnp.float32)  24.3 us
    all_to_all x2, starting transfers between devices, chunk_sum(): lax.all_to_all(sent, BOTH, 0, 0, axis_index_groups=core_groups(), tiled=T...  18.7 us
    all_to_all x2, waiting for transfers between devices, chunk_sum(): lax.all_to_all(sent, BOTH, 0, 0, axis_index_groups=core_groups(), tiled=T...  17 us
  transfers between devices with their start and end apart: 26, of which 8 were waited for; matrix products, arithmetic and copies ran while one was open for 14% of the time, Pallas kernels for 19%

profile of v1, /device:TPU:1, one launch (start us, length us, event | category | flops | bytes accessed | tf_op | source)
XLA Modules:
  0.0 323.1 jit_solution(1406358799006678186)
XLA Ops:
  11.3 4.5 %collective-permute-start = (bf16[192,1536]{1,0:T(8,128)(2,1)S(1)}, bf16[192,1536]{1,0:T(8,128)(2,1)}, u32[]{:S(2)}, u32[]{:S(2)}) collective-permute-start(bf16[192,1536]{1,0:T(8,128)(2,1)S(1)} %pad_maximum_fusion.rest_0_), channel_id=1, source_target_pairs={{0,16},{1,17},{2,18},{3,19},{4,20},{5,21},{6,22},{7,23},{8,24},{9,... | collective-permute-start | bytes 1769480 | tf_op jit(solution)/shard_map/ppermute | solution.py:186
  29.1 2.4 fusion.5
  31.5 1.8 fusion.6
  34.2 4.7 %all-to-all-start = ((bf16[8,128,640]{2,1,0:T(8,128)(2,1)}), bf16[8,128,640]{2,1,0:T(8,128)(2,1)S(1)}, u32[]{:S(2)}, u32[]{:S(2)}) async-start(bf16[8,128,640]{2,1,0:T(8,128)(2,1)} %pad.12), calls=%async_computation | async-start | bytes 2621440 | tf_op jit(solution)/shard_map/all_to_all | solution.py:547
  39.0 5.4 %collective-permute-start.7 = (bf16[192,1536]{1,0:T(8,128)(2,1)}, bf16[192,1536]{1,0:T(8,128)(2,1)}, u32[]{:S(2)}, u32[]{:S(2)}) collective-permute-start(bf16[192,1536]{1,0:T(8,128)(2,1)} %copy-done.21), channel_id=1, source_target_pairs={{0,8},{1,9},{2,10},{3,11},{4,12},{5,13},{6,14},{7,15},{8,0},{9,1},... | collective-permute-start | bytes 1769480 | tf_op jit(solution)/shard_map/ppermute | solution.py:186
  45.9 2.6 collective-permute-start.4
  51.9 3.2 collective-permute-start.6
  58.1 1.8 fusion.14
  59.9 1.8 fusion.15
  61.7 5.3 %fusion.4 = (f32[1024,1536]{1,0:T(8,128)}, f32[1024,1536]{1,0:T(8,128)S(1)}) fusion(f32[1024,1536]{1,0:T(8,128)S(1)} %fusion.14, f32[1024,1536]{1,0:T(8,128)S(1)} %fusion.15, bf16[1024,384]{1,0:T(8,128)(2,1)S(1)} %reduce-precision_convert_fusion.5.normed_hi, bf16[384,1536]{1,0:T(8,128)(2,1)S(1)} %copy-done.7), kind=kOutput, calls=%fused_computation.7 | convolution fusion | flops 1223688192 | bytes 27131904 | tf_op jit(solution)/shard_map/dot_general | solution.py:42
  67.0 2.0 fusion
  69.0 10.4 %collective-permute-done.5.rest_12_ = bf16[96,1536]{1,0:T(8,128)(2,1)} collective-permute-done((bf16[96,1536]{1,0:T(8,128)(2,1)}, bf16[96,1536]{1,0:T(8,128)(2,1)}, u32[]{:S(2)}, u32[]{:S(2)}) %collective-permute-start.5) | collective-permute-done | bytes 294944 | tf_op jit(solution)/shard_map/ppermute | solution.py:186
  83.5 1.8 fusion.16
  87.1 1.9 fusion.9
  90.6 1.8 fusion.18
  93.4 1.8 fusion.19
  98.5 4.5 %add_add_fusion.student_out = f32[1024,1536]{1,0:T(8,128)} fusion(f32[1024,1536]{1,0:T(8,128)S(1)} %fusion.18, f32[1024,1536]{1,0:T(8,128)S(1)} %fusion.19, bf16[1024,384]{1,0:T(8,128)(2,1)S(1)} %reduce-precision_convert_fusion.4.hidden_hi, bf16[384,1536]{1,0:T(8,128)(2,1)S(1)} %copy-done.8), kind=kOutput, calls=%fused_computation.8 | convolution fusion | flops 1211105280 | bytes 20840448 | tf_op jit(solution)/shard_map/dot_general | solution.py:42
  103.7 4.5 %collective-permute-done.16.rest_13_ = bf16[96,1536]{1,0:T(8,128)(2,1)S(1)} collective-permute-done((bf16[96,1536]{1,0:T(8,128)(2,1)S(1)}, bf16[96,1536]{1,0:T(8,128)(2,1)S(1)}, u32[]{:S(2)}, u32[]{:S(2)}) %collective-permute-start.16) | collective-permute-done | bytes 294944 | tf_op jit(solution)/shard_map/ppermute | solution.py:186
  110.5 32.9 %teacher.1 = (f32[1024,1536]{1,0:T(8,128)}, bf16[1024,1536]{1,0:T(8,128)(2,1)}) custom-call(s32[16]{0:T(128)} %stack.67.owners, bf16[1024,640]{1,0:T(8,128)(2,1)} %bitcast.65, f32[1,1536]{1,0:T(1,128)} %gain.1, bf16[16,240,1536]{2,1,0:T(8,128)(2,1)} %bitcast.74, bf16[192,1536]{1,0:T(8,128)(2,1)} %copy-done.21, ...), custom_call_target="tpu_custom_call" | custom-call | flops 16508780544 | bytes 31457280 | tf_op jit(solution)/shard_map/teacher/pallas_call | solution.py:150
  144.3 33.4 %head_backward.1 = (f32[4096,128]{1,0:T(8,128)}, f32[4096,128]{1,0:T(8,128)}, f32[1536,128]{1,0:T(8,128)}, f32[1024,384]{1,0:T(8,128)}, f32[8,128]{1,0:T(8,128)}) custom-call(s32[1]{0:T(128)} %bitcast.core, s32[16]{0:T(128)} %stack.67.owners, bf16[1024,1536]{1,0:T(8,128)(2,1)} %get-tuple-element.56.context, f32[1024,1536]{1,0:T(8,128)} %get-tuple-element.57.embedded, ...), custom_call_target="tpu_custom_call" | custom-call | flops 15703474176 | bytes 41943040 | tf_op jit(solution)/shard_map/head_backward/pallas_call | solution.py:306
  179.4 2.8 collective-permute-done.19
  182.1 2.8 add_convert_fusion.1
  185.0 8.5 %all-to-all-start.1 = ((bf16[64,64,128]{2,1,0:T(8,128)(2,1)}), bf16[64,64,128]{2,1,0:T(8,128)(2,1)S(1)}, u32[]{:S(2)}, u32[]{:S(2)}) async-start(bf16[64,64,128]{2,1,0:T(8,128)(2,1)} %bitcast.32), calls=%async_computation.1 | async-start | bytes 2097152 | tf_op jit(solution)/shard_map/all_to_all | solution.py:479
  193.5 29.5 %trunk_backward.1 = (f32[4096,128]{1,0:T(8,128)}, f32[4096,128]{1,0:T(8,128)}) custom-call(s32[1]{0:T(128)} %bitcast.core, f32[1024,384]{1,0:T(8,128)} %get-tuple-element.69.d_hidden, f32[1024,1536]{1,0:T(8,128)} %get-tuple-element.70.slope, bf16[1536,384]{1,0:T(8,128)(2,1)} %get-tuple-element.59.down_hi, bf16[1536,384]{1,0:T(8,128)(2,1)} %get-tuple-element.61.down_lo, ...), custom_call_target="tpu_custom_call" | custom-call | flops 11878268928 | bytes 31457280 | tf_op jit(solution)/shard_map/trunk_backward/pallas_call | solution.py:397
  223.7 4.0 %collective-permute-done.20 = f32[4096,128]{1,0:T(8,128)S(1)} collective-permute-done((f32[4096,128]{1,0:T(8,128)}, f32[4096,128]{1,0:T(8,128)S(1)}, u32[]{:S(2)}, u32[]{:S(2)}) %collective-permute-start.20) | collective-permute-done | bytes 2097184 | tf_op jit(solution)/shard_map/ppermute | solution.py:213
  227.7 2.8 add_convert_fusion
  230.5 10.2 %all-to-all-start.2 = ((bf16[64,64,128]{2,1,0:T(8,128)(2,1)}), bf16[64,64,128]{2,1,0:T(8,128)(2,1)S(1)}, u32[]{:S(2)}, u32[]{:S(2)}) async-start(bf16[64,64,128]{2,1,0:T(8,128)(2,1)} %bitcast.34), calls=%async_computation.2 | async-start | bytes 2097152 | tf_op jit(solution)/shard_map/all_to_all | solution.py:479
  240.7 17.0 %all-to-all-done.2 = bf16[64,64,128]{2,1,0:T(8,128)(2,1)S(1)} async-done(((bf16[64,64,128]{2,1,0:T(8,128)(2,1)}), bf16[64,64,128]{2,1,0:T(8,128)(2,1)S(1)}, u32[]{:S(2)}, u32[]{:S(2)}) %all-to-all-start.2) | async-done | bytes 1048608 | tf_op jit(solution)/shard_map/all_to_all | solution.py:479
  264.0 32.1 %all_to_all.20.mine = bf16[64,128,128]{2,1,0:T(8,128)(2,1)S(1)} all-to-all(bf16[64,128,128]{2,1,0:T(8,128)(2,1)S(1)} %broadcast_in_dim.75), channel_id=1, replica_groups={{0,1,2,3,4,5,6,7,16,17,18,19,20,21,22,23,32,33,34,35,36,37,38,39,48,49,..., dimensions={0} | all-to-all | bytes 4194304 | tf_op jit(solution)/shard_map/all_to_all | solution.py:485
  296.1 4.1 %collective-permute-start.21 = (bf16[64,128,128]{2,1,0:T(8,128)(2,1)S(1)}, bf16[64,128,128]{2,1,0:T(8,128)(2,1)S(1)}, u32[]{:S(2)}, u32[]{:S(2)}) collective-permute-start(bf16[64,128,128]{2,1,0:T(8,128)(2,1)S(1)} %all_to_all.20.mine), channel_id=1, source_target_pairs={{0,8},{1,9},{2,10},{3,11},{4,12},{5,13},{6,14},{7,15},{8,0},{9,1},... | collective-permute-start | bytes 6291464 | tf_op jit(solution)/shard_map/ppermute | solution.py:213
  300.2 3.8 %collective-permute-done.21.theirs = bf16[64,128,128]{2,1,0:T(8,128)(2,1)S(1)} collective-permute-done((bf16[64,128,128]{2,1,0:T(8,128)(2,1)S(1)}, bf16[64,128,128]{2,1,0:T(8,128)(2,1)S(1)}, u32[]{:S(2)}, u32[]{:S(2)}) %collective-permute-start.21) | collective-permute-done | bytes 2097184 | tf_op jit(solution)/shard_map/ppermute | solution.py:213
  305.4 6.3 %unpack_sums.1 = (f32[384,1536]{1,0:T(8,128)}, f32[1536,384]{1,0:T(8,128)}, f32[384,1536]{1,0:T(8,128)}, f32[588,384]{1,0:T(8,128)}, f32[8,128]{1,0:T(8,128)}, /*index=5*/f32[8,128]{1,0:T(8,128)}) custom-call(s32[1]{0:T(128)} %bitcast.core, bf16[64,128,128]{2,1,0:T(8,128)(2,1)} %copy-done.3, bf16[64,128,128]{2,1,0:T(8,128)(2,1)} %copy-done.15), custom_call_target="tpu_custom_call" | custom-call | bytes 12582912 | tf_op jit(solution)/shard_map/unpack_sums/pallas_call | solution.py:463
  (154 shorter events, 46.6 us)
Async XLA Ops:
  7.2 102.5 %all-gather.3.cloned.1.call-start = ((), (), s32[]{:S(2)}) async-start(), calls=%async_computation.4 | async-start | bytes 12533760 | tf_op jit(solution)/shard_map/all_gather | solution.py:520
  11.3 14.8 %copy-start.21 = (bf16[192,1536]{1,0:T(8,128)(2,1)}, bf16[192,1536]{1,0:T(8,128)(2,1)S(1)}, u32[]{:S(2)}) copy-start(bf16[192,1536]{1,0:T(8,128)(2,1)S(1)} %pad_maximum_fusion.rest_0_) | copy-start | bytes 1769476
  11.3 22.0 %collective-permute-start = (bf16[192,1536]{1,0:T(8,128)(2,1)S(1)}, bf16[192,1536]{1,0:T(8,128)(2,1)}, u32[]{:S(2)}, u32[]{:S(2)}) collective-permute-start(bf16[192,1536]{1,0:T(8,128)(2,1)S(1)} %pad_maximum_fusion.rest_0_), channel_id=1, source_target_pairs={{0,16},{1,17},{2,18},{3,19},{4,20},{5,21},{6,22},{7,23},{8,24},{9,... | collective-permute-start | bytes 1769480 | tf_op jit(solution)/shard_map/ppermute | solution.py:186
  15.8 17.5 %collective-permute-start.1 = (bf16[192,1536]{1,0:T(8,128)(2,1)S(1)}, bf16[192,1536]{1,0:T(8,128)(2,1)S(1)}, u32[]{:S(2)}, u32[]{:S(2)}) collective-permute-start(bf16[192,1536]{1,0:T(8,128)(2,1)S(1)} %pad_maximum_fusion.rest_0_), channel_id=1, source_target_pairs={{0,32},{1,33},{2,34},{3,35},{4,36},{5,37},{6,38},{7,39},{8,40},{9,... | collective-permute-start | bytes 1769480 | tf_op jit(solution)/shard_map/ppermute | solution.py:186
  17.0 17.2 %collective-permute-start.2 = (bf16[192,1536]{1,0:T(8,128)(2,1)S(1)}, bf16[192,1536]{1,0:T(8,128)(2,1)}, u32[]{:S(2)}, u32[]{:S(2)}) collective-permute-start(bf16[192,1536]{1,0:T(8,128)(2,1)S(1)} %pad_maximum_fusion.rest_0_), channel_id=1, source_target_pairs={{0,96},{1,97},{2,98},{3,99},{4,100},{5,101},{6,102},{7,103},{8,104... | collective-permute-start | bytes 1769480 | tf_op jit(solution)/shard_map/ppermute | solution.py:186
  31.5 28.4 %copy-start.1 = (bf16[384,1536]{1,0:T(8,128)(2,1)}, bf16[384,1536]{1,0:T(8,128)(2,1)S(1)}, u32[]{:S(2)}) copy-start(bf16[384,1536]{1,0:T(8,128)(2,1)S(1)} %get-tuple-element.50.up_hi) | copy-start | bytes 3538948
  34.2 21.2 %all-to-all-start = ((bf16[8,128,640]{2,1,0:T(8,128)(2,1)}), bf16[8,128,640]{2,1,0:T(8,128)(2,1)S(1)}, u32[]{:S(2)}, u32[]{:S(2)}) async-start(bf16[8,128,640]{2,1,0:T(8,128)(2,1)} %pad.12), calls=%async_computation | async-start | bytes 2621440 | tf_op jit(solution)/shard_map/all_to_all | solution.py:547
  39.0 56.3 %collective-permute-start.7 = (bf16[192,1536]{1,0:T(8,128)(2,1)}, bf16[192,1536]{1,0:T(8,128)(2,1)}, u32[]{:S(2)}, u32[]{:S(2)}) collective-permute-start(bf16[192,1536]{1,0:T(8,128)(2,1)} %copy-done.21), channel_id=1, source_target_pairs={{0,8},{1,9},{2,10},{3,11},{4,12},{5,13},{6,14},{7,15},{8,0},{9,1},... | collective-permute-start | bytes 1769480 | tf_op jit(solution)/shard_map/ppermute | solution.py:186
  45.0 35.7 %collective-permute-start.3 = (bf16[192,1536]{1,0:T(8,128)(2,1)}, bf16[192,1536]{1,0:T(8,128)(2,1)}, u32[]{:S(2)}, u32[]{:S(2)}) collective-permute-start(bf16[192,1536]{1,0:T(8,128)(2,1)} %collective-permute-done.rest_1_), channel_id=1, source_target_pairs={{0,32},{1,33},{2,34},{3,35},{4,36},{5,37},{6,38},{7,39},{8,40},{9,... | collective-permute-start | bytes 1769480 | tf_op jit(solution)/shard_map/ppermute | solution.py:186
  45.9 35.2 %collective-permute-start.4 = (bf16[192,1536]{1,0:T(8,128)(2,1)}, bf16[192,1536]{1,0:T(8,128)(2,1)}, u32[]{:S(2)}, u32[]{:S(2)}) collective-permute-start(bf16[192,1536]{1,0:T(8,128)(2,1)} %collective-permute-done.rest_1_), channel_id=1, source_target_pairs={{0,96},{1,97},{2,98},{3,99},{4,100},{5,101},{6,102},{7,103},{8,104... | collective-permute-start | bytes 1769480 | tf_op jit(solution)/shard_map/ppermute | solution.py:186
  50.2 29.2 %collective-permute-start.5 = (bf16[96,1536]{1,0:T(8,128)(2,1)}, bf16[96,1536]{1,0:T(8,128)(2,1)}, u32[]{:S(2)}, u32[]{:S(2)}) collective-permute-start(bf16[96,1536]{1,0:T(8,128)(2,1)} %slice.53), channel_id=1, source_target_pairs={{0,32},{1,33},{2,34},{3,35},{4,36},{5,37},{6,38},{7,39},{8,40},{9,... | collective-permute-start | bytes 884744 | tf_op jit(solution)/shard_map/ppermute | solution.py:186
  51.9 28.7 %collective-permute-start.6 = (bf16[96,1536]{1,0:T(8,128)(2,1)}, bf16[96,1536]{1,0:T(8,128)(2,1)}, u32[]{:S(2)}, u32[]{:S(2)}) collective-permute-start(bf16[96,1536]{1,0:T(8,128)(2,1)} %slice.54), channel_id=1, source_target_pairs={{0,96},{1,97},{2,98},{3,99},{4,100},{5,101},{6,102},{7,103},{8,104... | collective-permute-start | bytes 884744 | tf_op jit(solution)/shard_map/ppermute | solution.py:186
  67.0 16.5 %copy-start.18 = (bf16[1536,384]{1,0:T(8,128)(2,1)S(1)}, bf16[1536,384]{1,0:T(8,128)(2,1)}, u32[]{:S(2)}) copy-start(bf16[1536,384]{1,0:T(8,128)(2,1)} %get-tuple-element.59.down_hi) | copy-start | bytes 3538948
  69.0 16.3 %copy-start.10 = (bf16[1024,1536]{1,0:T(8,128)(2,1)}, bf16[1024,1536]{1,0:T(8,128)(2,1)S(1)}, u32[]{:S(2)}) copy-start(bf16[1024,1536]{1,0:T(8,128)(2,1)S(1)} %get-tuple-element.60.act_lo) | copy-start | bytes 9437188
  69.0 18.1 %copy-start.11 = (bf16[1024,1536]{1,0:T(8,128)(2,1)}, bf16[1024,1536]{1,0:T(8,128)(2,1)S(1)}, u32[]{:S(2)}) copy-start(bf16[1024,1536]{1,0:T(8,128)(2,1)S(1)} %get-tuple-element.58.act_hi) | copy-start | bytes 9437188
  79.4 16.6 %collective-permute-start.8 = (bf16[192,1536]{1,0:T(8,128)(2,1)}, bf16[192,1536]{1,0:T(8,128)(2,1)S(1)}, u32[]{:S(2)}, u32[]{:S(2)}) collective-permute-start(bf16[192,1536]{1,0:T(8,128)(2,1)} %collective-permute-done.rest_1_), channel_id=1, source_target_pairs={{0,8},{1,9},{2,10},{3,11},{4,12},{5,13},{6,14},{7,15},{8,0},{9,1},... | collective-permute-start | bytes 1769480 | tf_op jit(solution)/shard_map/ppermute | solution.py:186
  80.6 15.5 %collective-permute-start.9 = (bf16[192,1536]{1,0:T(8,128)(2,1)S(1)}, bf16[192,1536]{1,0:T(8,128)(2,1)S(1)}, u32[]{:S(2)}, u32[]{:S(2)}) collective-permute-start(bf16[192,1536]{1,0:T(8,128)(2,1)S(1)} %copy-done.24), channel_id=1, source_target_pairs={{0,8},{1,9},{2,10},{3,11},{4,12},{5,13},{6,14},{7,15},{8,0},{9,1},... | collective-permute-start | bytes 1769480 | tf_op jit(solution)/shard_map/ppermute | solution.py:186
  80.7 15.9 %collective-permute-start.11 = (bf16[192,1536]{1,0:T(8,128)(2,1)}, bf16[192,1536]{1,0:T(8,128)(2,1)S(1)}, u32[]{:S(2)}, u32[]{:S(2)}) collective-permute-start(bf16[192,1536]{1,0:T(8,128)(2,1)} %collective-permute-done.2.rest_4_), channel_id=1, source_target_pairs={{0,8},{1,9},{2,10},{3,11},{4,12},{5,13},{6,14},{7,15},{8,0},{9,1},... | collective-permute-start | bytes 1769480 | tf_op jit(solution)/shard_map/ppermute | solution.py:186
  82.1 16.0 %collective-permute-start.13 = (bf16[96,1536]{1,0:T(8,128)(2,1)S(1)}, bf16[96,1536]{1,0:T(8,128)(2,1)S(1)}, u32[]{:S(2)}, u32[]{:S(2)}) collective-permute-start(bf16[96,1536]{1,0:T(8,128)(2,1)S(1)} %slice.55), channel_id=1, source_target_pairs={{0,32},{1,33},{2,34},{3,35},{4,36},{5,37},{6,38},{7,39},{8,40},{9,... | collective-permute-start | bytes 884744 | tf_op jit(solution)/shard_map/ppermute | solution.py:186
  95.2 13.7 %collective-permute-start.10 = (bf16[192,1536]{1,0:T(8,128)(2,1)}, bf16[192,1536]{1,0:T(8,128)(2,1)S(1)}, u32[]{:S(2)}, u32[]{:S(2)}) collective-permute-start(bf16[192,1536]{1,0:T(8,128)(2,1)} %collective-permute-done.3.rest_3_), channel_id=1, source_target_pairs={{0,8},{1,9},{2,10},{3,11},{4,12},{5,13},{6,14},{7,15},{8,0},{9,1},... | collective-permute-start | bytes 1769480 | tf_op jit(solution)/shard_map/ppermute | solution.py:186
  96.0 13.6 %collective-permute-start.12 = (bf16[192,1536]{1,0:T(8,128)(2,1)}, bf16[192,1536]{1,0:T(8,128)(2,1)}, u32[]{:S(2)}, u32[]{:S(2)}) collective-permute-start(bf16[192,1536]{1,0:T(8,128)(2,1)} %collective-permute-done.4.rest_5_), channel_id=1, source_target_pairs={{0,8},{1,9},{2,10},{3,11},{4,12},{5,13},{6,14},{7,15},{8,0},{9,1},... | collective-permute-start | bytes 1769480 | tf_op jit(solution)/shard_map/ppermute | solution.py:186
  96.1 6.8 %collective-permute-start.14 = (bf16[96,1536]{1,0:T(8,128)(2,1)}, bf16[96,1536]{1,0:T(8,128)(2,1)S(1)}, u32[]{:S(2)}, u32[]{:S(2)}) collective-permute-start(bf16[96,1536]{1,0:T(8,128)(2,1)} %collective-permute-done.5.rest_12_), channel_id=1, source_target_pairs={{0,8},{1,9},{2,10},{3,11},{4,12},{5,13},{6,14},{7,15},{8,0},{9,1},... | collective-permute-start | bytes 884744 | tf_op jit(solution)/shard_map/ppermute | solution.py:186
  96.5 11.6 %collective-permute-start.16 = (bf16[96,1536]{1,0:T(8,128)(2,1)S(1)}, bf16[96,1536]{1,0:T(8,128)(2,1)S(1)}, u32[]{:S(2)}, u32[]{:S(2)}) collective-permute-start(bf16[96,1536]{1,0:T(8,128)(2,1)S(1)} %slice.56), channel_id=1, source_target_pairs={{0,96},{1,97},{2,98},{3,99},{4,100},{5,101},{6,102},{7,103},{8,104... | collective-permute-start | bytes 884744 | tf_op jit(solution)/shard_map/ppermute | solution.py:186
  98.1 10.8 %collective-permute-start.15 = (bf16[96,1536]{1,0:T(8,128)(2,1)S(1)}, bf16[96,1536]{1,0:T(8,128)(2,1)S(1)}, u32[]{:S(2)}, u32[]{:S(2)}) collective-permute-start(bf16[96,1536]{1,0:T(8,128)(2,1)S(1)} %collective-permute-done.13.rest_13_), channel_id=1, source_target_pairs={{0,8},{1,9},{2,10},{3,11},{4,12},{5,13},{6,14},{7,15},{8,0},{9,1},... | collective-permute-start | bytes 884744 | tf_op jit(solution)/shard_map/ppermute | solution.py:186
  103.0 40.4 %collective-permute-start.17 = (bf16[96,1536]{1,0:T(8,128)(2,1)}, bf16[96,1536]{1,0:T(8,128)(2,1)S(1)}, u32[]{:S(2)}, u32[]{:S(2)}) collective-permute-start(bf16[96,1536]{1,0:T(8,128)(2,1)} %collective-permute-done.6.rest_12_), channel_id=1, source_target_pairs={{0,8},{1,9},{2,10},{3,11},{4,12},{5,13},{6,14},{7,15},{8,0},{9,1},... | collective-permute-start | bytes 884744 | tf_op jit(solution)/shard_map/ppermute | solution.py:186
  108.2 35.2 %copy-start.33 = (bf16[96,1536]{1,0:T(8,128)(2,1)}, bf16[96,1536]{1,0:T(8,128)(2,1)S(1)}, u32[]{:S(2)}) copy-start(bf16[96,1536]{1,0:T(8,128)(2,1)S(1)} %collective-permute-done.16.rest_13_) | copy-start | bytes 884740
  108.2 35.2 %collective-permute-start.18 = (bf16[96,1536]{1,0:T(8,128)(2,1)S(1)}, bf16[96,1536]{1,0:T(8,128)(2,1)S(1)}, u32[]{:S(2)}, u32[]{:S(2)}) collective-permute-start(bf16[96,1536]{1,0:T(8,128)(2,1)S(1)} %collective-permute-done.16.rest_13_), channel_id=1, source_target_pairs={{0,8},{1,9},{2,10},{3,11},{4,12},{5,13},{6,14},{7,15},{8,0},{9,1},... | collective-permute-start | bytes 884744 | tf_op jit(solution)/shard_map/ppermute | solution.py:186
  177.7 4.5 %collective-permute-start.19 = (f32[4096,128]{1,0:T(8,128)}, f32[4096,128]{1,0:T(8,128)S(1)}, u32[]{:S(2)}, u32[]{:S(2)}) collective-permute-start(f32[4096,128]{1,0:T(8,128)} %get-tuple-element.66), channel_id=1, source_target_pairs={{0,8},{1,9},{2,10},{3,11},{4,12},{5,13},{6,14},{7,15},{8,0},{9,1},... | collective-permute-start | bytes 6291464 | tf_op jit(solution)/shard_map/ppermute | solution.py:213
  185.0 38.1 %all-to-all-start.1 = ((bf16[64,64,128]{2,1,0:T(8,128)(2,1)}), bf16[64,64,128]{2,1,0:T(8,128)(2,1)S(1)}, u32[]{:S(2)}, u32[]{:S(2)}) async-start(bf16[64,64,128]{2,1,0:T(8,128)(2,1)} %bitcast.32), calls=%async_computation.1 | async-start | bytes 2097152 | tf_op jit(solution)/shard_map/all_to_all | solution.py:479
  223.2 4.5 %collective-permute-start.20 = (f32[4096,128]{1,0:T(8,128)}, f32[4096,128]{1,0:T(8,128)S(1)}, u32[]{:S(2)}, u32[]{:S(2)}) collective-permute-start(f32[4096,128]{1,0:T(8,128)} %get-tuple-element.77), channel_id=1, source_target_pairs={{0,8},{1,9},{2,10},{3,11},{4,12},{5,13},{6,14},{7,15},{8,0},{9,1},... | collective-permute-start | bytes 6291464 | tf_op jit(solution)/shard_map/ppermute | solution.py:213
  230.5 27.2 %all-to-all-start.2 = ((bf16[64,64,128]{2,1,0:T(8,128)(2,1)}), bf16[64,64,128]{2,1,0:T(8,128)(2,1)S(1)}, u32[]{:S(2)}, u32[]{:S(2)}) async-start(bf16[64,64,128]{2,1,0:T(8,128)(2,1)} %bitcast.34), calls=%async_computation.2 | async-start | bytes 2097152 | tf_op jit(solution)/shard_map/all_to_all | solution.py:479
  296.1 7.9 %collective-permute-start.21 = (bf16[64,128,128]{2,1,0:T(8,128)(2,1)S(1)}, bf16[64,128,128]{2,1,0:T(8,128)(2,1)S(1)}, u32[]{:S(2)}, u32[]{:S(2)}) collective-permute-start(bf16[64,128,128]{2,1,0:T(8,128)(2,1)S(1)} %all_to_all.20.mine), channel_id=1, source_target_pairs={{0,8},{1,9},{2,10},{3,11},{4,12},{5,13},{6,14},{7,15},{8,0},{9,1},... | collective-permute-start | bytes 6291464 | tf_op jit(solution)/shard_map/ppermute | solution.py:213
  (32 other events, 130.1 us)
Sparse Core Ops, SparseCore 0:
  11.0 95.7 all-gather.2

commit v2 on v1

--- a/solution.py
+++ b/solution.py
@@ -223,6 +223,14 @@
     return high, (values - high.astype(jnp.float32)).astype(jnp.bfloat16)
 
 
+def three_parts(value, lane):
+    first = value.astype(jnp.bfloat16).astype(jnp.float32)
+    second = (value - first).astype(jnp.bfloat16).astype(jnp.float32)
+    third = value - first - second
+    row = jnp.where(lane == 0, first, jnp.where(lane == 1, second, third))
+    return jnp.where(lane < 3, row, 0.0)
+
+
 def dot_three(left, right, dims):
     at_left, at_right = dims[0][0][0], dims[0][1][0]
     wide = jnp.concatenate([left[0], left[1], left[0]], axis=at_left)
@@ -372,22 +380,14 @@
             start = EMBED_AT + i * EMBED_ROWS
             sums[start : start + EMBED_ROWS, :] = grad_embed[:EMBED_ROWS, columns]
             sums[GAIN_AT + i : GAIN_AT + i + 1, :] = grad_gain[:, columns]
-        first, rest = cut(total[0:1, :])
-        first = first.astype(jnp.float32)
-        second, third = cut(total[0:1, :] - first)
         lane = lax.broadcasted_iota(jnp.int32, (1, LANES), 1)
-        row = jnp.where(
-            lane == 0,
-            first,
-            jnp.where(lane == 1, second.astype(jnp.float32), third.astype(jnp.float32)),
-        )
-        sums[SUM_ROWS - 1 :, :] = jnp.where(lane < 3, row, 0.0)
+        sums[SUM_ROWS - 1 :, :] = three_parts(total[0:1, :], lane)
         hand_over(core[0], sums, mine, other, done)
 
 
 def trunk_backward(core, d_hidden, slope, down, up, normed, unit, scale, gain, rows, down_rest, total):
     count = d_hidden.shape[0]
-    tile = 256
+    tile = 512
 
     def whole(values):
         return pl.BlockSpec(values.shape, lambda j: (0, 0))
@@ -421,7 +421,7 @@
     )(core, d_hidden, slope, *down, *up, *normed, unit, scale, gain, rows, down_rest, total)
 
 
-def unpack_kernel(core, mine, theirs, head, down, up, embed, gain, total):
+def unpack_kernel(core, mine, theirs, head, down, up, embed, gain, mean_distance):
     def unpack(low, high):
         def take(part, start, count):
             pieces, stop = [], start + count
@@ -445,8 +445,12 @@
         for i in range(D_S // LANES):
             columns = slice(i * LANES, (i + 1) * LANES)
             embed[:, columns] = take(1, EMBED_AT + i * EMBED_ROWS, EMBED_ROWS)[:PIX]
-        gain[...] = take(1, GAIN_AT, 16)[:8]
-        total[...] = take(1, SUM_ROWS - 16, 16)[8:]
+        gains = take(1, GAIN_AT, 16)
+        for i in range(D_S // LANES):
+            gain[:, i * LANES : (i + 1) * LANES] = gains[i : i + 1]
+        lane = lax.broadcasted_iota(jnp.int32, (1, LANES), 1)
+        cosines = jnp.where(lane < 3, take(1, SUM_ROWS - 16, 16)[15:], 0.0)
+        mean_distance[...] = 1.0 - jnp.sum(cosines, axis=1, keepdims=True) / (DEVICES * 2 * BLK)
 
     @pl.when(core[0] == 0)
     def _():
@@ -459,7 +463,7 @@
 
 def unpack_sums(core, mine, theirs):
     vmem = pl.BlockSpec(memory_space=pltpu.VMEM)
-    shapes = [(D_S, D_T), (S_HID, D_S), (D_S, S_HID), (PIX, D_S), (8, LANES), (8, LANES)]
+    shapes = [(D_S, D_T), (S_HID, D_S), (D_S, S_HID), (PIX, D_S), (1, D_S), (1, 1)]
     return pl.pallas_call(
         unpack_kernel,
         in_specs=[pl.BlockSpec(memory_space=pltpu.SMEM)] + [vmem] * 2,
@@ -471,31 +475,35 @@
     )(core, mine, theirs)
 
 
-def core_sum(mine, other):
-    return (mine + core_swap(other)).astype(jnp.bfloat16).reshape(RANKS, CHUNK, LANES)
-
-
-def chunk_sum(sent):
-    got = lax.all_to_all(sent, BOTH, 0, 0, axis_index_groups=core_groups(), tiled=True)
-    return jnp.sum(got.astype(jnp.float32), axis=0)
-
-
-def spread_chunk(chunk):
-    spread = jnp.broadcast_to(chunk[None], (RANKS,) + chunk.shape)
-    half = lax.all_to_all(spread, BOTH, 0, 0, axis_index_groups=core_groups(), tiled=True)
-    return half, core_swap(half)
-
-
-def keep_total(chunk, core):
-    rank = (lax.axis_index("student") // 2) * 8 + lax.axis_index("pool")
-    owner = jnp.logical_and(core == 1, rank == RANKS - 1)
-    whole = jnp.sum(chunk[CHUNK - 1, :3])
-    first = lax.reduce_precision(whole, 8, 7)
-    second = lax.reduce_precision(whole - first, 8, 7)
-    lane = lax.broadcasted_iota(jnp.int32, (CHUNK, LANES), 1)
-    row = jnp.where(lane == 0, first, jnp.where(lane == 1, second, whole - first - second))
-    last = lax.broadcasted_iota(jnp.int32, (CHUNK, LANES), 0) == CHUNK - 1
-    return jnp.where(jnp.logical_and(owner, last), row, chunk)
+def core_sum(mine, theirs):
+    return (mine + theirs).astype(jnp.bfloat16).reshape(RANKS, CHUNK, LANES)
+
+
+def to_all_ranks(values):
+    return lax.all_to_all(values, BOTH, 0, 0, axis_index_groups=core_groups(), tiled=True)
+
+
+def chunk_kernel(owner, got, spread):
+    chunk = jnp.sum(got[...].astype(jnp.float32), axis=0)
+    lane = lax.broadcasted_iota(jnp.int32, (1, LANES), 1)
+    parts = chunk[2 * CHUNK - 1 :, :]
+    whole = jnp.sum(jnp.where(lane < 3, parts, 0.0), axis=1, keepdims=True)
+    last = jnp.where(owner[0] == 1, three_parts(whole, lane), parts)
+    rounded = jnp.concatenate([chunk[: 2 * CHUNK - 1, :], last], axis=0).astype(jnp.bfloat16)
+    spread[...] = jnp.broadcast_to(rounded[None], spread.shape)
+
+
+def add_chunk(owner, got):
+    vmem = pl.BlockSpec(memory_space=pltpu.VMEM)
+    return pl.pallas_call(
+        chunk_kernel,
+        in_specs=[pl.BlockSpec(memory_space=pltpu.SMEM), vmem],
+        out_specs=vmem,
+        out_shape=jax.ShapeDtypeStruct(got.shape, jnp.bfloat16),
+        compiler_params=pltpu.CompilerParams(vmem_limit_bytes=32 * 1024 * 1024),
+        cost_estimate=pl.CostEstimate(flops=0, bytes_accessed=4 * 1024 * 1024, transcendentals=0),
+        name="add_chunk",
+    )(owner, got)
 
 
 def on_device(
@@ -569,20 +577,20 @@
     *sums_a, down_rest, d_hidden, total = head_backward(
         core, owners, context, embedded, student_out, hidden, act, head, near + high
     )
-    sent_a, d_hidden = lax.optimization_barrier((core_sum(*sums_a), d_hidden))
-    chunk_a = chunk_sum(sent_a)
+    theirs_a = core_swap(sums_a[1])
     sums_b = trunk_backward(
         core, d_hidden, slope, down, up, normed_s, unit, scale, student_gain[None], rows, down_rest, total
     )
-    chunk_a, *sums_b = lax.optimization_barrier((chunk_a, *sums_b))
-    chunk_b = keep_total(chunk_sum(core_sum(*sums_b)), core[0])
-    chunks = jnp.concatenate([chunk_a.astype(jnp.bfloat16), chunk_b.astype(jnp.bfloat16)], axis=0)
-    head_sum, down_sum, up_sum, embed_sum, gain_sum, cosine_sum = unpack_sums(
-        core, *spread_chunk(chunks)
-    )
-    gain_sum = gain_sum[: D_S // LANES].reshape(D_S)
-    mean_distance = 1.0 - jnp.sum(cosine_sum[7, :3]) / (DEVICES * 2 * BLK)
-    return (mean_distance, embed_sum, gain_sum, up_sum, down_sum, head_sum)
+    rank = lax.axis_index("student") // 2 * 8 + lax.axis_index("pool")
+    owner = jnp.logical_and(core == 1, rank == RANKS - 1).astype(jnp.int32)
+    theirs_a, *sums_b = lax.optimization_barrier((theirs_a, *sums_b))
+    sent = [core_sum(sums_a[0], theirs_a), core_sum(sums_b[0], core_swap(sums_b[1]))]
+    got = to_all_ranks(jnp.concatenate(sent, axis=1))
+    half = to_all_ranks(add_chunk(owner, got))
+    head_sum, down_sum, up_sum, embed_sum, gain_sum, mean_distance = unpack_sums(
+        core, half, core_swap(half)
+    )
+    return (mean_distance.reshape(()), embed_sum, gain_sum.reshape(D_S), up_sum, down_sum, head_sum)
 
 
 def solution(mesh):

time: 329 us -> 310 us (0.942)
  starting transfers between devices: 54.7 us -> 44.6 us
  waiting for transfers between devices: 43.7 us -> 50.5 us
  Pallas kernels: 102 us -> 95.5 us
  between operations: 24.2 us -> 18.8 us
  other arithmetic: 18.7 us -> 15.2 us
    all_to_all x2 -> x1, waiting for transfers between devices: 17 us -> 27.4 us  [to_all_ranks(): lax.all_to_all(values, BOTH, 0, 0, axis_index_groups=core_groups(), tiled...]
    all_to_all x2 -> x1, starting transfers between devices: 18.7 us -> 9.21 us  [to_all_ranks(): lax.all_to_all(values, BOTH, 0, 0, axis_index_groups=core_groups(), tiled...]
    pallas_call x1, Pallas kernels: 29.5 us -> 22.3 us  [trunk_backward(): pl.pallas_call(trunk_kernel, grid=(S_HID // tile,), in_specs=[pl.BlockSpe...]
    ppermute x3, waiting for transfers between devices: 10.5 us -> 5.83 us  [core_swap(): return lax.ppermute(values, BOTH, pairs)]
    convert_element_type x3 -> x2, other arithmetic: 6.32 us -> 2.15 us  [core_sum(): return (mine + theirs).astype(jnp.bfloat16).reshape(RANKS, CHUNK, LANES)]
    unnamed x76 -> x74, local copies, waits for them, and re-layouts: 7.54 us -> 6.95 us
  transfers between devices with their start and end apart: 26 -> 25, of which waited for: 8 -> 7; matrix products, arithmetic and copies ran while one was open for 14% -> 16% of each run, Pallas kernels for 19% -> 18%
where the time goes in v2:
time: 310 us; the launch traced here: 304 us
  Pallas kernels  95.5 us (31%)
  waiting for transfers between devices  50.5 us (16%)
  starting transfers between devices  44.6 us (14%)
  blocking collectives  34.5 us (11%)
  matrix products  24.4 us (8%)
  local copies, waits for them, and re-layouts  21 us (7%)
  between operations  18.8 us (6%)
  other arithmetic  15.2 us (5%)
    all_to_all x1, blocking collectives, to_all_ranks(): lax.all_to_all(values, BOTH, 0, 0, axis_index_groups=core_groups(), tiled...  34.5 us
    pallas_call x1, Pallas kernels, head_backward(): pl.pallas_call(head_kernel, grid=(rows // block,), in_specs=[pl.BlockSpec...  33.4 us
    pallas_call x1, Pallas kernels, teach(): pl.pallas_call(teacher_kernel, in_specs=[pl.BlockSpec(memory_space=pltpu....  32.9 us
    all_to_all x1, waiting for transfers between devices, to_all_ranks(): lax.all_to_all(values, BOTH, 0, 0, axis_index_groups=core_groups(), tiled...  27.4 us
    ppermute x19, starting transfers between devices, moved(): return lax.ppermute(values, BOTH, pairs)  26.6 us
    dot_general x11, matrix products, bf16_dot(): lax.dot_general(left, right, dims, preferred_element_type=jnp.float32)  24.4 us
    pallas_call x1, Pallas kernels, trunk_backward(): pl.pallas_call(trunk_kernel, grid=(S_HID // tile,), in_specs=[pl.BlockSpe...  22.3 us
    ppermute x19, waiting for transfers between devices, moved(): return lax.ppermute(values, BOTH, pairs)  17.2 us
  transfers between devices with their start and end apart: 25, of which 7 were waited for; matrix products, arithmetic and copies ran while one was open for 16% of the time, Pallas kernels for 18%

profile of v2, /device:TPU:1, one launch (start us, length us, event | category | flops | bytes accessed | tf_op | source)
XLA Modules:
  0.0 304.3 jit_solution(5134267285894292792)
XLA Ops:
  12.1 4.4 %collective-permute-start = (bf16[192,1536]{1,0:T(8,128)(2,1)}, bf16[192,1536]{1,0:T(8,128)(2,1)}, u32[]{:S(2)}, u32[]{:S(2)}) collective-permute-start(bf16[192,1536]{1,0:T(8,128)(2,1)} %pad_maximum_fusion.1.rest_0_), channel_id=1, source_target_pairs={{0,16},{1,17},{2,18},{3,19},{4,20},{5,21},{6,22},{7,23},{8,24},{9,... | collective-permute-start | bytes 1769480 | tf_op jit(solution)/shard_map/ppermute | solution.py:186
  29.8 2.4 fusion.5
  32.2 1.9 fusion.6
  36.2 4.1 %all-to-all-start = ((bf16[8,128,640]{2,1,0:T(8,128)(2,1)}), bf16[8,128,640]{2,1,0:T(8,128)(2,1)S(1)}, u32[]{:S(2)}, u32[]{:S(2)}) async-start(bf16[8,128,640]{2,1,0:T(8,128)(2,1)} %pad.12), calls=%async_computation | async-start | bytes 2621440 | tf_op jit(solution)/shard_map/all_to_all | solution.py:555
  40.4 6.0 %collective-permute-start.7 = (bf16[192,1536]{1,0:T(8,128)(2,1)}, bf16[192,1536]{1,0:T(8,128)(2,1)}, u32[]{:S(2)}, u32[]{:S(2)}) collective-permute-start(bf16[192,1536]{1,0:T(8,128)(2,1)} %pad_maximum_fusion.1.rest_0_), channel_id=1, source_target_pairs={{0,8},{1,9},{2,10},{3,11},{4,12},{5,13},{6,14},{7,15},{8,0},{9,1},... | collective-permute-start | bytes 1769480 | tf_op jit(solution)/shard_map/ppermute | solution.py:186
  47.8 2.7 collective-permute-start.4
  52.1 1.7 slice.45
  53.8 3.2 %collective-permute-start.6 = (bf16[96,1536]{1,0:T(8,128)(2,1)}, bf16[96,1536]{1,0:T(8,128)(2,1)}, u32[]{:S(2)}, u32[]{:S(2)}) collective-permute-start(bf16[96,1536]{1,0:T(8,128)(2,1)} %slice.45), channel_id=1, source_target_pairs={{0,96},{1,97},{2,98},{3,99},{4,100},{5,101},{6,102},{7,103},{8,104... | collective-permute-start | bytes 884744 | tf_op jit(solution)/shard_map/ppermute | solution.py:186
  59.5 1.8 fusion.14
  61.3 1.8 fusion.15
  63.2 5.3 %fusion.4 = (f32[1024,1536]{1,0:T(8,128)}, f32[1024,1536]{1,0:T(8,128)S(1)}) fusion(f32[1024,1536]{1,0:T(8,128)S(1)} %fusion.14, f32[1024,1536]{1,0:T(8,128)S(1)} %fusion.15, bf16[1024,384]{1,0:T(8,128)(2,1)S(1)} %reduce-precision_convert_fusion.5.normed_hi, bf16[384,1536]{1,0:T(8,128)(2,1)S(1)} %copy-done.7), kind=kOutput, calls=%fused_computation.7 | convolution fusion | flops 1223688192 | bytes 27131904 | tf_op jit(solution)/shard_map/dot_general | solution.py:42
  68.4 2.0 fusion
  70.4 11.8 %collective-permute-done.5.rest_12_ = bf16[96,1536]{1,0:T(8,128)(2,1)} collective-permute-done((bf16[96,1536]{1,0:T(8,128)(2,1)}, bf16[96,1536]{1,0:T(8,128)(2,1)}, u32[]{:S(2)}, u32[]{:S(2)}) %collective-permute-start.5) | collective-permute-done | bytes 294944 | tf_op jit(solution)/shard_map/ppermute | solution.py:186
  85.4 1.8 fusion.16
  87.2 1.8 fusion.17
  89.0 1.9 fusion.9
  92.6 1.8 fusion.18
  95.4 1.8 fusion.19
  98.6 2.1 collective-permute-start.16
  101.1 4.5 %add_add_fusion.student_out = f32[1024,1536]{1,0:T(8,128)} fusion(f32[1024,1536]{1,0:T(8,128)S(1)} %fusion.18, f32[1024,1536]{1,0:T(8,128)S(1)} %fusion.19, bf16[1024,384]{1,0:T(8,128)(2,1)S(1)} %reduce-precision_convert_fusion.4.hidden_hi, bf16[384,1536]{1,0:T(8,128)(2,1)S(1)} %copy-done.8), kind=kOutput, calls=%fused_computation.8 | convolution fusion | flops 1211105280 | bytes 20840448 | tf_op jit(solution)/shard_map/dot_general | solution.py:42
  105.9 3.2 %collective-permute-done.16.rest_13_ = bf16[96,1536]{1,0:T(8,128)(2,1)S(1)} collective-permute-done((bf16[96,1536]{1,0:T(8,128)(2,1)S(1)}, bf16[96,1536]{1,0:T(8,128)(2,1)S(1)}, u32[]{:S(2)}, u32[]{:S(2)}) %collective-permute-start.16) | collective-permute-done | bytes 294944 | tf_op jit(solution)/shard_map/ppermute | solution.py:186
  111.4 32.9 %teacher.1 = (f32[1024,1536]{1,0:T(8,128)}, bf16[1024,1536]{1,0:T(8,128)(2,1)}) custom-call(s32[16]{0:T(128)} %stack.67.owners, bf16[1024,640]{1,0:T(8,128)(2,1)} %bitcast.65, f32[1,1536]{1,0:T(1,128)} %gain.1, bf16[16,240,1536]{2,1,0:T(8,128)(2,1)} %bitcast.76, bf16[192,1536]{1,0:T(8,128)(2,1)} %pad_maximum_fusion.1.rest_0_, ...), custom_call_target="tpu_custom_call" | custom-call | flops 16508780544 | bytes 31457280 | tf_op jit(solution)/shard_map/teacher/pallas_call | solution.py:150
  145.2 33.4 %head_backward.1 = (f32[4096,128]{1,0:T(8,128)}, f32[4096,128]{1,0:T(8,128)}, f32[1536,128]{1,0:T(8,128)}, f32[1024,384]{1,0:T(8,128)}, f32[8,128]{1,0:T(8,128)}) custom-call(s32[1]{0:T(128)} %bitcast.core, s32[16]{0:T(128)} %stack.67.owners, bf16[1024,1536]{1,0:T(8,128)(2,1)} %get-tuple-element.54.context, f32[1024,1536]{1,0:T(8,128)} %get-tuple-element.55.embedded, ...), custom_call_target="tpu_custom_call" | custom-call | flops 15703474176 | bytes 41943040 | tf_op jit(solution)/shard_map/head_backward/pallas_call | solution.py:314
  180.6 22.3 %trunk_backward.1 = (f32[4096,128]{1,0:T(8,128)}, f32[4096,128]{1,0:T(8,128)}) custom-call(s32[1]{0:T(128)} %bitcast.core, f32[1024,384]{1,0:T(8,128)} %get-tuple-element.65.d_hidden, f32[1024,1536]{1,0:T(8,128)} %get-tuple-element.66.slope, bf16[1536,384]{1,0:T(8,128)(2,1)} %get-tuple-element.57.down_hi, bf16[1536,384]{1,0:T(8,128)(2,1)} %get-tuple-element.59.down_lo, ...), custom_call_target="tpu_custom_call" | custom-call | flops 11878268928 | bytes 31457280 | tf_op jit(solution)/shard_map/trunk_backward/pallas_call | solution.py:397
  203.4 1.9 add_convert_fusion.1
  205.4 2.0 collective-permute-done.20
  209.1 9.2 %all-to-all-start.1 = ((bf16[64,128,128]{2,1,0:T(8,128)(2,1)}), bf16[64,128,128]{2,1,0:T(8,128)(2,1)S(1)}, u32[]{:S(2)}, u32[]{:S(2)}) async-start(bf16[64,128,128]{2,1,0:T(8,128)(2,1)} %pad_maximum_fusion), calls=%async_computation.1 | async-start | bytes 4194304 | tf_op jit(solution)/shard_map/all_to_all | solution.py:483
  218.3 27.4 %all-to-all-done.1.got = bf16[64,128,128]{2,1,0:T(8,128)(2,1)S(1)} async-done(((bf16[64,128,128]{2,1,0:T(8,128)(2,1)}), bf16[64,128,128]{2,1,0:T(8,128)(2,1)S(1)}, u32[]{:S(2)}, u32[]{:S(2)}) %all-to-all-start.1) | async-done | bytes 2097184 | tf_op jit(solution)/shard_map/all_to_all | solution.py:483
  246.3 34.5 %all_to_all.15.mine = bf16[64,128,128]{2,1,0:T(8,128)(2,1)S(1)} all-to-all(bf16[64,128,128]{2,1,0:T(8,128)(2,1)S(1)} %add_chunk.1), channel_id=1, replica_groups={{0,1,2,3,4,5,6,7,16,17,18,19,20,21,22,23,32,33,34,35,36,37,38,39,48,49,..., dimensions={0} | all-to-all | bytes 4194304 | tf_op jit(solution)/shard_map/all_to_all | solution.py:483
  280.8 3.7 %collective-permute-start.21 = (bf16[64,128,128]{2,1,0:T(8,128)(2,1)S(1)}, bf16[64,128,128]{2,1,0:T(8,128)(2,1)S(1)}, u32[]{:S(2)}, u32[]{:S(2)}) collective-permute-start(bf16[64,128,128]{2,1,0:T(8,128)(2,1)S(1)} %all_to_all.15.mine), channel_id=1, source_target_pairs={{0,8},{1,9},{2,10},{3,11},{4,12},{5,13},{6,14},{7,15},{8,0},{9,1},... | collective-permute-start | bytes 6291464 | tf_op jit(solution)/shard_map/ppermute | solution.py:213
  284.5 3.8 %collective-permute-done.21.theirs = bf16[64,128,128]{2,1,0:T(8,128)(2,1)S(1)} collective-permute-done((bf16[64,128,128]{2,1,0:T(8,128)(2,1)S(1)}, bf16[64,128,128]{2,1,0:T(8,128)(2,1)S(1)}, u32[]{:S(2)}, u32[]{:S(2)}) %collective-permute-start.21) | collective-permute-done | bytes 2097184 | tf_op jit(solution)/shard_map/ppermute | solution.py:213
  289.6 6.4 %unpack_sums.1 = (f32[384,1536]{1,0:T(8,128)}, f32[1536,384]{1,0:T(8,128)}, f32[384,1536]{1,0:T(8,128)}, f32[588,384]{1,0:T(8,128)}, f32[1,384]{1,0:T(1,128)}, /*index=5*/f32[1,1]{1,0:T(1,128)}) custom-call(s32[1]{0:T(128)} %bitcast.core, bf16[64,128,128]{2,1,0:T(8,128)(2,1)} %copy-done.3, bf16[64,128,128]{2,1,0:T(8,128)(2,1)} %copy-done.17), custom_call_target="tpu_custom_call" | custom-call | bytes 12582912 | tf_op jit(solution)/shard_map/unpack_sums/pallas_call | solution.py:467
  (142 shorter events, 40.1 us)
Async XLA Ops:
  7.2 103.4 %all-gather.3.cloned.1.call-start = ((), (), s32[]{:S(2)}) async-start(), calls=%async_computation.3 | async-start | bytes 12533760 | tf_op jit(solution)/shard_map/all_gather | solution.py:528
  10.2 14.5 %copy-start.26 = (s32[1,2]{1,0:T(1,128)S(1)}, s32[1,2]{1,0:T(1,128)}, u32[]{:S(2)}) copy-start(s32[1,2]{1,0:T(1,128)} %param.14) | copy-start | bytes 28
  12.1 22.0 %collective-permute-start = (bf16[192,1536]{1,0:T(8,128)(2,1)}, bf16[192,1536]{1,0:T(8,128)(2,1)}, u32[]{:S(2)}, u32[]{:S(2)}) collective-permute-start(bf16[192,1536]{1,0:T(8,128)(2,1)} %pad_maximum_fusion.1.rest_0_), channel_id=1, source_target_pairs={{0,16},{1,17},{2,18},{3,19},{4,20},{5,21},{6,22},{7,23},{8,24},{9,... | collective-permute-start | bytes 1769480 | tf_op jit(solution)/shard_map/ppermute | solution.py:186
  16.5 18.6 %collective-permute-start.1 = (bf16[192,1536]{1,0:T(8,128)(2,1)}, bf16[192,1536]{1,0:T(8,128)(2,1)}, u32[]{:S(2)}, u32[]{:S(2)}) collective-permute-start(bf16[192,1536]{1,0:T(8,128)(2,1)} %pad_maximum_fusion.1.rest_0_), channel_id=1, source_target_pairs={{0,32},{1,33},{2,34},{3,35},{4,36},{5,37},{6,38},{7,39},{8,40},{9,... | collective-permute-start | bytes 1769480 | tf_op jit(solution)/shard_map/ppermute | solution.py:186
  17.7 18.5 %collective-permute-start.2 = (bf16[192,1536]{1,0:T(8,128)(2,1)}, bf16[192,1536]{1,0:T(8,128)(2,1)}, u32[]{:S(2)}, u32[]{:S(2)}) collective-permute-start(bf16[192,1536]{1,0:T(8,128)(2,1)} %pad_maximum_fusion.1.rest_0_), channel_id=1, source_target_pairs={{0,96},{1,97},{2,98},{3,99},{4,100},{5,101},{6,102},{7,103},{8,104... | collective-permute-start | bytes 1769480 | tf_op jit(solution)/shard_map/ppermute | solution.py:186
  32.2 29.1 %copy-start.1 = (bf16[384,1536]{1,0:T(8,128)(2,1)}, bf16[384,1536]{1,0:T(8,128)(2,1)S(1)}, u32[]{:S(2)}) copy-start(bf16[384,1536]{1,0:T(8,128)(2,1)S(1)} %get-tuple-element.48.up_hi) | copy-start | bytes 3538948
  36.2 20.8 %all-to-all-start = ((bf16[8,128,640]{2,1,0:T(8,128)(2,1)}), bf16[8,128,640]{2,1,0:T(8,128)(2,1)S(1)}, u32[]{:S(2)}, u32[]{:S(2)}) async-start(bf16[8,128,640]{2,1,0:T(8,128)(2,1)} %pad.12), calls=%async_computation | async-start | bytes 2621440 | tf_op jit(solution)/shard_map/all_to_all | solution.py:555
  40.4 56.8 %collective-permute-start.7 = (bf16[192,1536]{1,0:T(8,128)(2,1)}, bf16[192,1536]{1,0:T(8,128)(2,1)}, u32[]{:S(2)}, u32[]{:S(2)}) collective-permute-start(bf16[192,1536]{1,0:T(8,128)(2,1)} %pad_maximum_fusion.1.rest_0_), channel_id=1, source_target_pairs={{0,8},{1,9},{2,10},{3,11},{4,12},{5,13},{6,14},{7,15},{8,0},{9,1},... | collective-permute-start | bytes 1769480 | tf_op jit(solution)/shard_map/ppermute | solution.py:186
  47.0 36.2 %collective-permute-start.3 = (bf16[192,1536]{1,0:T(8,128)(2,1)}, bf16[192,1536]{1,0:T(8,128)(2,1)}, u32[]{:S(2)}, u32[]{:S(2)}) collective-permute-start(bf16[192,1536]{1,0:T(8,128)(2,1)} %collective-permute-done.rest_1_), channel_id=1, source_target_pairs={{0,32},{1,33},{2,34},{3,35},{4,36},{5,37},{6,38},{7,39},{8,40},{9,... | collective-permute-start | bytes 1769480 | tf_op jit(solution)/shard_map/ppermute | solution.py:186
  47.8 36.0 %collective-permute-start.4 = (bf16[192,1536]{1,0:T(8,128)(2,1)}, bf16[192,1536]{1,0:T(8,128)(2,1)}, u32[]{:S(2)}, u32[]{:S(2)}) collective-permute-start(bf16[192,1536]{1,0:T(8,128)(2,1)} %collective-permute-done.rest_1_), channel_id=1, source_target_pairs={{0,96},{1,97},{2,98},{3,99},{4,100},{5,101},{6,102},{7,103},{8,104... | collective-permute-start | bytes 1769480 | tf_op jit(solution)/shard_map/ppermute | solution.py:186
  52.1 30.1 %collective-permute-start.5 = (bf16[96,1536]{1,0:T(8,128)(2,1)}, bf16[96,1536]{1,0:T(8,128)(2,1)}, u32[]{:S(2)}, u32[]{:S(2)}) collective-permute-start(bf16[96,1536]{1,0:T(8,128)(2,1)} %slice.44), channel_id=1, source_target_pairs={{0,32},{1,33},{2,34},{3,35},{4,36},{5,37},{6,38},{7,39},{8,40},{9,... | collective-permute-start | bytes 884744 | tf_op jit(solution)/shard_map/ppermute | solution.py:186
  53.8 29.4 %collective-permute-start.6 = (bf16[96,1536]{1,0:T(8,128)(2,1)}, bf16[96,1536]{1,0:T(8,128)(2,1)}, u32[]{:S(2)}, u32[]{:S(2)}) collective-permute-start(bf16[96,1536]{1,0:T(8,128)(2,1)} %slice.45), channel_id=1, source_target_pairs={{0,96},{1,97},{2,98},{3,99},{4,100},{5,101},{6,102},{7,103},{8,104... | collective-permute-start | bytes 884744 | tf_op jit(solution)/shard_map/ppermute | solution.py:186
  68.4 16.9 %copy-start.20 = (bf16[1536,384]{1,0:T(8,128)(2,1)S(1)}, bf16[1536,384]{1,0:T(8,128)(2,1)}, u32[]{:S(2)}) copy-start(bf16[1536,384]{1,0:T(8,128)(2,1)} %get-tuple-element.57.down_hi) | copy-start | bytes 3538948
  70.4 16.7 %copy-start.10 = (bf16[1024,1536]{1,0:T(8,128)(2,1)}, bf16[1024,1536]{1,0:T(8,128)(2,1)S(1)}, u32[]{:S(2)}) copy-start(bf16[1024,1536]{1,0:T(8,128)(2,1)S(1)} %get-tuple-element.58.act_lo) | copy-start | bytes 9437188
  70.4 18.5 %copy-start.11 = (bf16[1024,1536]{1,0:T(8,128)(2,1)}, bf16[1024,1536]{1,0:T(8,128)(2,1)S(1)}, u32[]{:S(2)}) copy-start(bf16[1024,1536]{1,0:T(8,128)(2,1)S(1)} %get-tuple-element.56.act_hi) | copy-start | bytes 9437188
  82.3 15.8 %collective-permute-start.8 = (bf16[192,1536]{1,0:T(8,128)(2,1)}, bf16[192,1536]{1,0:T(8,128)(2,1)S(1)}, u32[]{:S(2)}, u32[]{:S(2)}) collective-permute-start(bf16[192,1536]{1,0:T(8,128)(2,1)} %collective-permute-done.rest_1_), channel_id=1, source_target_pairs={{0,8},{1,9},{2,10},{3,11},{4,12},{5,13},{6,14},{7,15},{8,0},{9,1},... | collective-permute-start | bytes 1769480 | tf_op jit(solution)/shard_map/ppermute | solution.py:186
  83.2 14.9 %collective-permute-start.9 = (bf16[192,1536]{1,0:T(8,128)(2,1)}, bf16[192,1536]{1,0:T(8,128)(2,1)S(1)}, u32[]{:S(2)}, u32[]{:S(2)}) collective-permute-start(bf16[192,1536]{1,0:T(8,128)(2,1)} %collective-permute-done.1.rest_2_), channel_id=1, source_target_pairs={{0,8},{1,9},{2,10},{3,11},{4,12},{5,13},{6,14},{7,15},{8,0},{9,1},... | collective-permute-start | bytes 1769480 | tf_op jit(solution)/shard_map/ppermute | solution.py:186
  83.2 15.3 %collective-permute-start.11 = (bf16[192,1536]{1,0:T(8,128)(2,1)}, bf16[192,1536]{1,0:T(8,128)(2,1)S(1)}, u32[]{:S(2)}, u32[]{:S(2)}) collective-permute-start(bf16[192,1536]{1,0:T(8,128)(2,1)} %collective-permute-done.2.rest_4_), channel_id=1, source_target_pairs={{0,8},{1,9},{2,10},{3,11},{4,12},{5,13},{6,14},{7,15},{8,0},{9,1},... | collective-permute-start | bytes 1769480 | tf_op jit(solution)/shard_map/ppermute | solution.py:186
  84.7 15.9 %collective-permute-start.13 = (bf16[96,1536]{1,0:T(8,128)(2,1)S(1)}, bf16[96,1536]{1,0:T(8,128)(2,1)S(1)}, u32[]{:S(2)}, u32[]{:S(2)}) collective-permute-start(bf16[96,1536]{1,0:T(8,128)(2,1)S(1)} %slice.46), channel_id=1, source_target_pairs={{0,32},{1,33},{2,34},{3,35},{4,36},{5,37},{6,38},{7,39},{8,40},{9,... | collective-permute-start | bytes 884744 | tf_op jit(solution)/shard_map/ppermute | solution.py:186
  97.2 12.7 %collective-permute-start.10 = (bf16[192,1536]{1,0:T(8,128)(2,1)}, bf16[192,1536]{1,0:T(8,128)(2,1)S(1)}, u32[]{:S(2)}, u32[]{:S(2)}) collective-permute-start(bf16[192,1536]{1,0:T(8,128)(2,1)} %collective-permute-done.3.rest_3_), channel_id=1, source_target_pairs={{0,8},{1,9},{2,10},{3,11},{4,12},{5,13},{6,14},{7,15},{8,0},{9,1},... | collective-permute-start | bytes 1769480 | tf_op jit(solution)/shard_map/ppermute | solution.py:186
  98.0 12.5 %collective-permute-start.12 = (bf16[192,1536]{1,0:T(8,128)(2,1)}, bf16[192,1536]{1,0:T(8,128)(2,1)}, u32[]{:S(2)}, u32[]{:S(2)}) collective-permute-start(bf16[192,1536]{1,0:T(8,128)(2,1)} %collective-permute-done.4.rest_5_), channel_id=1, source_target_pairs={{0,8},{1,9},{2,10},{3,11},{4,12},{5,13},{6,14},{7,15},{8,0},{9,1},... | collective-permute-start | bytes 1769480 | tf_op jit(solution)/shard_map/ppermute | solution.py:186
  98.1 7.5 %collective-permute-start.14 = (bf16[96,1536]{1,0:T(8,128)(2,1)}, bf16[96,1536]{1,0:T(8,128)(2,1)S(1)}, u32[]{:S(2)}, u32[]{:S(2)}) collective-permute-start(bf16[96,1536]{1,0:T(8,128)(2,1)} %collective-permute-done.5.rest_12_), channel_id=1, source_target_pairs={{0,8},{1,9},{2,10},{3,11},{4,12},{5,13},{6,14},{7,15},{8,0},{9,1},... | collective-permute-start | bytes 884744 | tf_op jit(solution)/shard_map/ppermute | solution.py:186
  98.6 10.5 %collective-permute-start.16 = (bf16[96,1536]{1,0:T(8,128)(2,1)S(1)}, bf16[96,1536]{1,0:T(8,128)(2,1)S(1)}, u32[]{:S(2)}, u32[]{:S(2)}) collective-permute-start(bf16[96,1536]{1,0:T(8,128)(2,1)S(1)} %slice.47), channel_id=1, source_target_pairs={{0,96},{1,97},{2,98},{3,99},{4,100},{5,101},{6,102},{7,103},{8,104... | collective-permute-start | bytes 884744 | tf_op jit(solution)/shard_map/ppermute | solution.py:186
  100.6 9.2 %collective-permute-start.15 = (bf16[96,1536]{1,0:T(8,128)(2,1)S(1)}, bf16[96,1536]{1,0:T(8,128)(2,1)S(1)}, u32[]{:S(2)}, u32[]{:S(2)}) collective-permute-start(bf16[96,1536]{1,0:T(8,128)(2,1)S(1)} %collective-permute-done.13.rest_13_), channel_id=1, source_target_pairs={{0,8},{1,9},{2,10},{3,11},{4,12},{5,13},{6,14},{7,15},{8,0},{9,1},... | collective-permute-start | bytes 884744 | tf_op jit(solution)/shard_map/ppermute | solution.py:186
  105.6 38.7 %collective-permute-start.17 = (bf16[96,1536]{1,0:T(8,128)(2,1)}, bf16[96,1536]{1,0:T(8,128)(2,1)S(1)}, u32[]{:S(2)}, u32[]{:S(2)}) collective-permute-start(bf16[96,1536]{1,0:T(8,128)(2,1)} %collective-permute-done.6.rest_12_), channel_id=1, source_target_pairs={{0,8},{1,9},{2,10},{3,11},{4,12},{5,13},{6,14},{7,15},{8,0},{9,1},... | collective-permute-start | bytes 884744 | tf_op jit(solution)/shard_map/ppermute | solution.py:186
  109.1 35.2 %copy-start.32 = (bf16[96,1536]{1,0:T(8,128)(2,1)}, bf16[96,1536]{1,0:T(8,128)(2,1)S(1)}, u32[]{:S(2)}) copy-start(bf16[96,1536]{1,0:T(8,128)(2,1)S(1)} %collective-permute-done.16.rest_13_) | copy-start | bytes 884740
  109.1 35.2 %collective-permute-start.18 = (bf16[96,1536]{1,0:T(8,128)(2,1)S(1)}, bf16[96,1536]{1,0:T(8,128)(2,1)S(1)}, u32[]{:S(2)}, u32[]{:S(2)}) collective-permute-start(bf16[96,1536]{1,0:T(8,128)(2,1)S(1)} %collective-permute-done.16.rest_13_), channel_id=1, source_target_pairs={{0,8},{1,9},{2,10},{3,11},{4,12},{5,13},{6,14},{7,15},{8,0},{9,1},... | collective-permute-start | bytes 884744 | tf_op jit(solution)/shard_map/ppermute | solution.py:186
  178.6 24.2 %collective-permute-start.19 = (f32[4096,128]{1,0:T(8,128)}, f32[4096,128]{1,0:T(8,128)}, u32[]{:S(2)}, u32[]{:S(2)}) collective-permute-start(f32[4096,128]{1,0:T(8,128)} %get-tuple-element.64), channel_id=1, source_target_pairs={{0,8},{1,9},{2,10},{3,11},{4,12},{5,13},{6,14},{7,15},{8,0},{9,1},... | collective-permute-start | bytes 6291464 | tf_op jit(solution)/shard_map/ppermute | solution.py:213
  180.5 22.8 %copy-start.15 = (f32[4096,128]{1,0:T(8,128)S(1)}, f32[4096,128]{1,0:T(8,128)}, u32[]{:S(2)}) copy-start(f32[4096,128]{1,0:T(8,128)} %get-tuple-element.63) | copy-start | bytes 6291460
  202.8 4.6 %collective-permute-start.20 = (f32[4096,128]{1,0:T(8,128)}, f32[4096,128]{1,0:T(8,128)S(1)}, u32[]{:S(2)}, u32[]{:S(2)}) collective-permute-start(f32[4096,128]{1,0:T(8,128)} %get-tuple-element.73), channel_id=1, source_target_pairs={{0,8},{1,9},{2,10},{3,11},{4,12},{5,13},{6,14},{7,15},{8,0},{9,1},... | collective-permute-start | bytes 6291464 | tf_op jit(solution)/shard_map/ppermute | solution.py:213
  209.1 36.6 %all-to-all-start.1 = ((bf16[64,128,128]{2,1,0:T(8,128)(2,1)}), bf16[64,128,128]{2,1,0:T(8,128)(2,1)S(1)}, u32[]{:S(2)}, u32[]{:S(2)}) async-start(bf16[64,128,128]{2,1,0:T(8,128)(2,1)} %pad_maximum_fusion), calls=%async_computation.1 | async-start | bytes 4194304 | tf_op jit(solution)/shard_map/all_to_all | solution.py:483
  280.8 7.5 %collective-permute-start.21 = (bf16[64,128,128]{2,1,0:T(8,128)(2,1)S(1)}, bf16[64,128,128]{2,1,0:T(8,128)(2,1)S(1)}, u32[]{:S(2)}, u32[]{:S(2)}) collective-permute-start(bf16[64,128,128]{2,1,0:T(8,128)(2,1)S(1)} %all_to_all.15.mine), channel_id=1, source_target_pairs={{0,8},{1,9},{2,10},{3,11},{4,12},{5,13},{6,14},{7,15},{8,0},{9,1},... | collective-permute-start | bytes 6291464 | tf_op jit(solution)/shard_map/ppermute | solution.py:213
  (30 other events, 109.5 us)
Sparse Core Ops, SparseCore 0:
  11.0 95.9 all-gather.2

commit v3 on v2

v3 whole, which is shorter than its diff:
```python
import jax
import jax.numpy as jnp
from jax import lax
from jax.experimental import pallas as pl
from jax.experimental.pallas import tpu as pltpu
from jax.sharding import PartitionSpec as P

HEADS = 24
HDIM = 64
EPSILON = 1e-06
BOTH = ("student", "pool")
DEVICES = 128
PAIR = 2 * HDIM
LANES = 128
PIX = 588
PIX_PAD = 640
D_S = 384
D_T = 1536
S_HID = 1536
BLK = 128
P_ROWS = 288
O_ROWS = 96
NEAR = 12
FAR = 4
CUT = 192
REST = P_ROWS - CUT
STUDENTS = 16
EMBED_PACK = 48
RANKS = DEVICES // 2
CHUNK = 64
SUM_ROWS = 2 * RANKS * CHUNK
EMBED_ROWS = 592
UP_AT = S_HID
EMBED_AT = UP_AT + D_S * S_HID // LANES
GAIN_AT = EMBED_AT + (D_S // LANES) * EMBED_ROWS
NT = (((1,), (1,)), ((), ()))
TN = (((0,), (0,)), ((), ()))
NN = (((1,), (0,)), ((), ()))


def bf16_dot(left, right, dims):
    return lax.dot_general(left, right, dims, preferred_element_type=jnp.float32)


def rms_scale(values):
    return lax.rsqrt(jnp.mean(values * values, axis=-1, keepdims=True) + EPSILON)


def halved_dot(left, right):
    return (
        bf16_dot(left[0], right[0], NN)
        + bf16_dot(left[1], right[0], NN)
        + bf16_dot(left[0], right[1], NN)
    )


def attend_block(mixed, at, out):
    lane = lax.broadcasted_iota(jnp.int32, (BLK, PAIR), 1)
    first = lane < HDIM
    zero = jnp.zeros((BLK, PAIR), jnp.bfloat16)
    ones = jnp.concatenate(
        [jnp.where(first, 1.0, 0.0), jnp.where(first, 0.0, 1.0)], axis=0
    ).astype(jnp.bfloat16)
    rows = pl.ds(at, BLK)
    for pair in range(HEADS // 2):
        start = pair * PAIR
        queries = mixed[rows, start : start + PAIR]
        keys = mixed[rows, D_T + start : D_T + start + PAIR]
        values = mixed[rows, 2 * D_T + start : 2 * D_T + start + PAIR]
        keys_two = jnp.concatenate(
            [jnp.where(first, keys, zero), jnp.where(first, zero, keys)], axis=0
        )
        values_two = jnp.concatenate(
            [jnp.where(first, values, zero), jnp.where(first, zero, values)], axis=0
        )
        scores = bf16_dot(queries, keys_two, NT)
        left, right = scores[:, :BLK], scores[:, BLK:]
        scale = HDIM ** (-0.5)
        left = jnp.exp((left - jnp.max(left, axis=1, keepdims=True)) * scale)
        right = jnp.exp((right - jnp.max(right, axis=1, keepdims=True)) * scale)
        weights = jnp.concatenate([left, right], axis=1).astype(jnp.bfloat16)
        summed = bf16_dot(weights, jnp.concatenate([values_two, ones], axis=1), NN)
        out[rows, start : start + PAIR] = (summed[:, :PAIR] / summed[:, PAIR:]).astype(jnp.bfloat16)


def shard_copies(plan, owners, target, semaphores, count):
    copies = []
    for i, (piece, start, rows, row) in enumerate(plan):
        at = pl.multiple_of(owners[i] * count + row, 16)
        copies.append(
            pltpu.make_async_copy(
                piece.at[pl.ds(start, rows)], target.at[pl.ds(at, rows)], semaphores.at[i]
            )
        )
    return copies


def place(device):
    student, pool = device // 8, device % 8
    return [student // 4, student // 2 % 2, student % 2, pool]


def moved(values, x=0, z=0, core=0):
    pairs = []
    for device in range(DEVICES):
        at = place(device)
        student = ((at[0] + x) % 4 * 2 + (at[1] ^ z)) * 2 + (at[2] ^ core)
        pairs.append((device, student * 8 + at[3]))
    return lax.ppermute(values, BOTH, pairs)


def with_core(pieces):
    return pieces + [moved(values, core=1) for values in pieces]


def shard_owners():
    x, z, core, _ = place(lax.axis_index("student") * 8)

    def index(dx, dz, dc):
        return (lax.rem(x + dx + 4, 4) * 2 + (z + dz) % 2) * 2 + (core + dc) % 2

    near = [index(dx, dz, dc) for dc in range(2) for dx in (0, -1, 1) for dz in range(2)]
    far = [index(2, dz, dc) for dc in range(2) for dz in range(2)]
    return jnp.stack(near + far).astype(jnp.int32)


def core_groups():
    groups = [[], []]
    for device in range(DEVICES):
        groups[(device // 8) % 2].append(device)
    return groups


def core_swap(values):
    pairs = [(d, d ^ 8) for d in range(DEVICES)]
    return lax.ppermute(values, BOTH, pairs)


def halves_of(values):
    high = lax.reduce_precision(values, 8, 7)
    return high.astype(jnp.bfloat16), (values - high).astype(jnp.bfloat16)


def cut(values):
    high = values.astype(jnp.bfloat16)
    return high, (values - high.astype(jnp.float32)).astype(jnp.bfloat16)


def three_parts(value, lane):
    first = value.astype(jnp.bfloat16).astype(jnp.float32)
    second = (value - first).astype(jnp.bfloat16).astype(jnp.float32)
    third = value - first - second
    row = jnp.where(lane == 0, first, jnp.where(lane == 1, second, third))
    return jnp.where(lane < 3, row, 0.0)


def dot_three(left, right, dims):
    at_left, at_right = dims[0][0][0], dims[0][1][0]
    wide = jnp.concatenate([left[0], left[1], left[0]], axis=at_left)
    other = jnp.concatenate([right[0], right[0], right[1]], axis=at_right)
    return bf16_dot(wide, other, dims)


def scale_of(values):
    return lax.rsqrt(jnp.mean(values * values, axis=1, keepdims=True) + EPSILON)


def hand_over(core, sums, mine, other, done):
    half = SUM_ROWS // 2
    at = pl.multiple_of(core * half, half)
    across = pl.multiple_of((1 - core) * half, half)
    copies = [
        pltpu.make_async_copy(sums.at[pl.ds(across, half)], other, done.at[0]),
        pltpu.make_async_copy(sums.at[pl.ds(at, half)], mine, done.at[1]),
    ]
    for copy in copies:
        copy.start()
    for copy in copies:
        copy.wait()


def project_rows(refs, owners, scopes):
    rows, gain, gathered, pieces, embedded, mixed, semaphores, others = refs
    embed, project, normed = scopes
    wide = D_T // 2
    first = [
        pltpu.make_async_copy(
            gathered.at[:, pl.ds(CUT, EMBED_PACK), pl.ds(i * wide, wide)], embed.at[:, i], others.at[i]
        )
        for i in range(2)
    ]
    for copy in first:
        copy.start()
    copies = [
        pltpu.make_async_copy(
            gathered.at[i, pl.ds(0, CUT)], project.at[pl.ds(i * P_ROWS, CUT)], others.at[2 + i]
        )
        for i in range(STUDENTS)
    ]
    plan = [(piece, 0, REST, CUT) for piece in pieces]
    copies += shard_copies(plan, owners, project, semaphores, P_ROWS)
    for copy in copies:
        copy.start()
    for copy in first:
        copy.wait()
    step = 2 * BLK

    @pl.loop(0, rows.shape[0] // step)
    def _(r):
        at = pl.ds(pl.multiple_of(r * step, step), step)
        weights = embed[...].reshape(D_T, wide)[:, :PIX_PAD]
        product = bf16_dot(rows[at, :], weights, NT)
        embedded[at, :] = product
        normed[at, :] = (product * scale_of(product) * gain[...]).astype(jnp.bfloat16)

    for copy in copies:
        copy.wait()
    tile = 512

    @pl.loop(0, 3 * D_T // tile)
    def _(n):
        at = pl.ds(pl.multiple_of(n * tile, tile), tile)
        mixed[:, at] = bf16_dot(normed[...], project[at, :], NT).astype(jnp.bfloat16)


def teacher_kernel(core, project_owners, output_owners, rows, gain, gathered, *rest):
    pieces, rest = rest[: NEAR + FAR], rest[NEAR + FAR :]
    high, rest = rest[:FAR], rest[FAR:]
    sources, rest = rest[:7], rest[7:]
    mine, other, down_rest, d_hidden_out, total, embedded, context, mixed, *semaphores = rest
    project_done, others, output_done, sources_done, done = semaphores
    count, block = rows.shape[0], 2 * BLK

    def project(*scopes):
        refs = rows, gain, gathered, pieces, embedded, mixed, project_done, others
        project_rows(refs, project_owners, scopes)

    pl.run_scoped(
        project,
        pltpu.VMEM((STUDENTS, 2, EMBED_PACK, D_T // 2), jnp.bfloat16),
        pltpu.VMEM((3 * D_T, D_T), jnp.bfloat16),
        pltpu.VMEM((count, D_T), jnp.bfloat16),
    )

    def compare(output, sums, *held):
        plan = [(piece, REST if i < NEAR else 0, O_ROWS, 0) for i, piece in enumerate(pieces[:NEAR] + high)]
        copies = shard_copies(plan, output_owners, output, output_done, O_ROWS)
        copies += [
            pltpu.make_async_copy(source, target, sources_done.at[i])
            for i, (source, target) in enumerate(zip(sources, held))
        ]
        for copy in copies:
            copy.start()
        sums[...] = jnp.zeros_like(sums)
        down_rest[...] = jnp.zeros_like(down_rest)
        total[...] = jnp.zeros_like(total)

        @pl.loop(0, count // BLK)
        def _(b):
            attend_block(mixed, pl.multiple_of(b * BLK, BLK), context)

        for copy in copies:
            copy.wait()
        student_out, hidden_hi, hidden_lo, act_hi, act_lo, head_hi, head_lo = held

        @pl.loop(0, count // block)
        def _(r):
            at = pl.ds(pl.multiple_of(r * block, block), block)
            finished = embedded[at, :] + bf16_dot(context[at, :], output[...], NT)
            features = (finished * scale_of(finished)).astype(jnp.bfloat16).astype(jnp.float32)
            out = student_out[at, :]
            dot_mean = jnp.mean(out * features, axis=1, keepdims=True)
            out_scale, feature_scale = scale_of(out), scale_of(features)
            both = out_scale * feature_scale
            total[...] += jnp.sum(dot_mean * both)
            along = both * (-1.0 / D_T)
            back = both * dot_mean * out_scale * out_scale * (1.0 / D_T)
            d_out = cut(along * features + back * out)
            grad_head = dot_three((hidden_hi[at, :], hidden_lo[at, :]), d_out, TN)
            for i in range(D_T // LANES):
                sums[i * D_S : (i + 1) * D_S, :] += grad_head[:, i * LANES : (i + 1) * LANES]
            d_hidden = dot_three(d_out, (head_hi[...], head_lo[...]), NT)
            d_hidden_out[at, :] = d_hidden
            grad_down = dot_three((act_hi[at, :], act_lo[at, :]), cut(d_hidden), TN)
            start = D_S * D_T // LANES
            for i in range(2):
                columns = slice(i * LANES, (i + 1) * LANES)
                sums[start + i * S_HID : start + (i + 1) * S_HID, :] += grad_down[:, columns]
            down_rest[...] += grad_down[:, 2 * LANES :]

        hand_over(core[0], sums, mine, other, done)

    pl.run_scoped(
        compare,
        pltpu.VMEM((D_T, D_T), jnp.bfloat16),
        pltpu.VMEM((SUM_ROWS, LANES), jnp.float32),
        *[pltpu.VMEM(source.shape, source.dtype) for source in sources],
    )


def teacher_and_head(core, owners, rows, gain, gathered, pieces, high, student_out, hidden, act, head):
    count = rows.shape[0]
    smem, vmem, anywhere = [
        pl.BlockSpec(memory_space=space) for space in (pltpu.SMEM, pltpu.VMEM, pl.ANY)
    ]
    sources = (student_out, *hidden, *act, *head)
    return pl.pallas_call(
        teacher_kernel,
        in_specs=[smem] * 3 + [vmem] * 2 + [anywhere] * (1 + len(pieces) + len(high) + len(sources)),
        out_specs=[anywhere] * 2 + [vmem] * 3,
        out_shape=[
            jax.ShapeDtypeStruct((SUM_ROWS // 2, LANES), jnp.float32),
            jax.ShapeDtypeStruct((SUM_ROWS // 2, LANES), jnp.float32),
            jax.ShapeDtypeStruct((S_HID, LANES), jnp.float32),
            jax.ShapeDtypeStruct((count, D_S), jnp.float32),
            jax.ShapeDtypeStruct((8, LANES), jnp.float32),
        ],
        scratch_shapes=[
            pltpu.VMEM((count, D_T), jnp.float32),
            pltpu.VMEM((count, D_T), jnp.bfloat16),
            pltpu.VMEM((count, 3 * D_T), jnp.bfloat16),
            pltpu.SemaphoreType.DMA((NEAR + FAR,)),
            pltpu.SemaphoreType.DMA((2 + STUDENTS,)),
            pltpu.SemaphoreType.DMA((NEAR + FAR,)),
            pltpu.SemaphoreType.DMA((len(sources),)),
            pltpu.SemaphoreType.DMA((2,)),
        ],
        compiler_params=pltpu.CompilerParams(vmem_limit_bytes=60 * 1024 * 1024),
        cost_estimate=pl.CostEstimate(
            flops=2 * count * D_T * (PIX_PAD + 4 * D_T + 9 * D_S),
            bytes_accessed=50 * 1024 * 1024,
            transcendentals=0,
        ),
        name="teacher_and_head",
    )(core, owners, owners, rows, gain, gathered, *pieces, *high, *sources)


def trunk_kernel(
    core, d_hidden, slope, down_hi, down_lo, up_hi, up_lo, normed_hi, normed_lo, lifted, gain, rows,
    down_rest, total, mine, other, sums, dh_hi, dh_lo, d_normed, done,
):
    step = pl.program_id(0)
    tile = slope.shape[1]

    @pl.when(step == 0)
    def _():
        dh_hi[...], dh_lo[...] = cut(d_hidden[...])
        d_normed[...] = jnp.zeros_like(d_normed)
        sums[:UP_AT, :] = down_rest[...]
        sums[GAIN_AT:, :] = jnp.zeros((SUM_ROWS - GAIN_AT, LANES), jnp.float32)

    d_act = dot_three((dh_hi[...], dh_lo[...]), (down_hi[...], down_lo[...]), NT)
    d_pre = cut(d_act * slope[...])
    grad_up = dot_three((normed_hi[...], normed_lo[...]), d_pre, TN)
    at = pl.multiple_of(UP_AT + step * (tile // LANES) * D_S, LANES)
    for i in range(tile // LANES):
        sums[pl.ds(at + i * D_S, D_S), :] = grad_up[:, i * LANES : (i + 1) * LANES]
    d_normed[...] += dot_three(d_pre, (up_hi[...], up_lo[...]), NT)

    @pl.when(step == pl.num_programs(0) - 1)
    def _():
        d_out = d_normed[...]
        scale = scale_of(lifted[...])
        across = lifted[...] * scale
        grad_gain = jnp.sum(d_out * across, axis=0, keepdims=True)
        d_unit = d_out * gain[...]
        inner = jnp.mean(d_unit * across, axis=1, keepdims=True)
        d_lifted = cut(d_hidden[...] + scale * (d_unit - across * inner))
        grad_embed = bf16_dot(rows[...], d_lifted[0], TN) + bf16_dot(rows[...], d_lifted[1], TN)
        for i in range(D_S // LANES):
            columns = slice(i * LANES, (i + 1) * LANES)
            start = EMBED_AT + i * EMBED_ROWS
            sums[start : start + EMBED_ROWS, :] = grad_embed[:EMBED_ROWS, columns]
            sums[GAIN_AT + i : GAIN_AT + i + 1, :] = grad_gain[:, columns]
        lane = lax.broadcasted_iota(jnp.int32, (1, LANES), 1)
        sums[SUM_ROWS - 1 :, :] = three_parts(total[0:1, :], lane)
        hand_over(core[0], sums, mine, other, done)


def trunk_backward(core, d_hidden, slope, down, up, normed, lifted, gain, rows, down_rest, total):
    count = d_hidden.shape[0]
    tile = 512

    def whole(values):
        return pl.BlockSpec(values.shape, lambda j: (0, 0))

    down_spec = pl.BlockSpec((tile, D_S), lambda j: (j, 0))
    up_spec = pl.BlockSpec((D_S, tile), lambda j: (0, j))
    return pl.pallas_call(
        trunk_kernel,
        grid=(S_HID // tile,),
        in_specs=[
            pl.BlockSpec(memory_space=pltpu.SMEM),
            whole(d_hidden), pl.BlockSpec((count, tile), lambda j: (0, j)),
            down_spec, down_spec, up_spec, up_spec,
            whole(normed[0]), whole(normed[1]), whole(lifted), whole(gain), whole(rows),
            whole(down_rest), whole(total),
        ],
        out_specs=[pl.BlockSpec(memory_space=pl.ANY)] * 2,
        out_shape=[jax.ShapeDtypeStruct((SUM_ROWS // 2, LANES), jnp.float32)] * 2,
        scratch_shapes=[
            pltpu.VMEM((SUM_ROWS, LANES), jnp.float32),
            pltpu.VMEM((count, D_S), jnp.bfloat16),
            pltpu.VMEM((count, D_S), jnp.bfloat16),
            pltpu.VMEM((count, D_S), jnp.float32),
            pltpu.SemaphoreType.DMA((2,)),
        ],
        compiler_params=pltpu.CompilerParams(vmem_limit_bytes=56 * 1024 * 1024),
        cost_estimate=pl.CostEstimate(
            flops=2 * count * D_S * (9 * S_HID + 2 * PIX_PAD), bytes_accessed=30 * 1024 * 1024, transcendentals=0
        ),
        name="trunk_backward",
    )(core, d_hidden, slope, *down, *up, *normed, lifted, gain, rows, down_rest, total)


def unpack_kernel(
    core, mine_hbm, theirs_hbm, head_hbm, down_hbm, up_hbm, embed_hbm, gain, mean_distance,
    mine, theirs, head, down, up, embed, semaphores,
):
    arrivals = [
        pltpu.make_async_copy(mine_hbm, mine, semaphores.at[0]),
        pltpu.make_async_copy(theirs_hbm, theirs, semaphores.at[1]),
    ]
    results = [
        pltpu.make_async_copy(source, target, semaphores.at[2 + i])
        for i, (source, target) in enumerate(
            [(head, head_hbm), (down, down_hbm), (up, up_hbm), (embed, embed_hbm)]
        )
    ]
    for copy in arrivals:
        copy.start()
    for copy in arrivals:
        copy.wait()

    def take(halves, part, start, count):
        pieces, stop = [], start + count
        while start < stop:
            rank, row = start // CHUNK, start % CHUNK
            size = min(CHUNK - row, stop - start)
            at = part * CHUNK + row
            pieces.append(halves[rank // RANKS][rank % RANKS, at : at + size, :].astype(jnp.float32))
            start += size
        return pieces[0] if len(pieces) == 1 else jnp.concatenate(pieces, axis=0)

    def strip(i):
        return slice(i * LANES, (i + 1) * LANES)

    def unpack_head(halves):
        for i in range(D_T // LANES):
            head[:, strip(i)] = take(halves, 0, i * D_S, D_S)

    def unpack_down(halves):
        at = D_S * D_T // LANES
        for i in range(2):
            down[:, strip(i)] = take(halves, 0, at + i * S_HID, S_HID)
        down[:, 2 * LANES :] = take(halves, 1, 0, S_HID)

    def unpack_up(halves):
        for i in range(S_HID // LANES):
            up[:, strip(i)] = take(halves, 1, UP_AT + i * D_S, D_S)

    def unpack_rest(halves):
        for i in range(D_S // LANES):
            embed[:, strip(i)] = take(halves, 1, EMBED_AT + i * EMBED_ROWS, EMBED_ROWS)[:PIX]
        gains = take(halves, 1, GAIN_AT, 16)
        for i in range(D_S // LANES):
            gain[:, strip(i)] = gains[i : i + 1]
        lane = lax.broadcasted_iota(jnp.int32, (1, LANES), 1)
        cosines = jnp.where(lane < 3, take(halves, 1, SUM_ROWS - 16, 16)[15:], 0.0)
        mean_distance[0] = 1.0 - jnp.sum(cosines) * (1.0 / (DEVICES * 2 * BLK))

    for unpack, copy in zip([unpack_head, unpack_down, unpack_up, unpack_rest], results):

        @pl.when(core[0] == 0)
        def _():
            unpack((mine, theirs))

        @pl.when(core[0] == 1)
        def _():
            unpack((theirs, mine))

        copy.start()
    for copy in results:
        copy.wait()


def unpack_sums(core, mine, theirs):
    smem, vmem, anywhere = [
        pl.BlockSpec(memory_space=space) for space in (pltpu.SMEM, pltpu.VMEM, pl.ANY)
    ]
    shapes = [(D_S, D_T), (S_HID, D_S), (D_S, S_HID), (PIX, D_S)]
    return pl.pallas_call(
        unpack_kernel,
        in_specs=[smem, anywhere, anywhere],
        out_specs=[anywhere] * 4 + [vmem, smem],
        out_shape=[jax.ShapeDtypeStruct(shape, jnp.float32) for shape in shapes + [(1, D_S), (1,)]],
        scratch_shapes=[pltpu.VMEM(mine.shape, mine.dtype)] * 2
        + [pltpu.VMEM(shape, jnp.float32) for shape in shapes]
        + [pltpu.SemaphoreType.DMA((6,))],
        compiler_params=pltpu.CompilerParams(vmem_limit_bytes=56 * 1024 * 1024),
        cost_estimate=pl.CostEstimate(flops=0, bytes_accessed=12 * 1024 * 1024, transcendentals=0),
        name="unpack_sums",
    )(core, mine, theirs)


def core_sum(mine, theirs):
    return (mine + theirs).astype(jnp.bfloat16).reshape(RANKS, CHUNK, LANES)


def to_all_ranks(values):
    return lax.all_to_all(values, BOTH, 0, 0, axis_index_groups=core_groups(), tiled=True)


def chunk_kernel(owner, got, spread):
    chunk = jnp.sum(got[...].astype(jnp.float32), axis=0)
    lane = lax.broadcasted_iota(jnp.int32, (1, LANES), 1)
    parts = chunk[2 * CHUNK - 1 :, :]
    whole = jnp.sum(jnp.where(lane < 3, parts, 0.0), axis=1, keepdims=True)
    last = jnp.where(owner[0] == 1, three_parts(whole, lane), parts)
    rounded = jnp.concatenate([chunk[: 2 * CHUNK - 1, :], last], axis=0).astype(jnp.bfloat16)
    spread[...] = jnp.broadcast_to(rounded[None], spread.shape)


def add_chunk(owner, got):
    vmem = pl.BlockSpec(memory_space=pltpu.VMEM)
    return pl.pallas_call(
        chunk_kernel,
        in_specs=[pl.BlockSpec(memory_space=pltpu.SMEM), vmem],
        out_specs=vmem,
        out_shape=jax.ShapeDtypeStruct(got.shape, jnp.bfloat16),
        compiler_params=pltpu.CompilerParams(vmem_limit_bytes=32 * 1024 * 1024),
        cost_estimate=pl.CostEstimate(flops=0, bytes_accessed=4 * 1024 * 1024, transcendentals=0),
        name="add_chunk",
    )(owner, got)


def on_device(
    pixels,
    keyframes,
    destination,
    student_embed,
    student_gain,
    student_up,
    student_down,
    student_head,
    teacher_embed,
    teacher_gain,
    teacher_project,
    teacher_output,
):
    pool_size = lax.axis_size("pool")

    project = teacher_project[0].T
    embed_shard = jnp.pad(teacher_embed[0].T, ((0, 0), (0, D_T // 2 - PIX)))
    embed_shard = jnp.concatenate([embed_shard[:EMBED_PACK], embed_shard[EMBED_PACK:]], axis=1)
    gathered = lax.all_gather(
        jnp.concatenate([project[:CUT], embed_shard], axis=0), "student", axis=0, tiled=False
    )
    shard = jnp.concatenate([project[CUT:], teacher_output[0].T], axis=0)
    first = [moved(shard, z=1), moved(shard, x=1), moved(shard, x=-1)]

    owners = shard_owners()

    teachers = jnp.arange(pool_size, dtype=jnp.int32)[:, None, None]
    chosen = [
        lax.dynamic_index_in_dim(pixels, keyframes[0, k], 0, keepdims=True) for k in range(2)
    ]
    outgoing = jnp.where(
        destination[0, 0] == teachers,
        chosen[0],
        jnp.where(destination[0, 1] == teachers, chosen[1], jnp.zeros((), jnp.bfloat16)),
    )
    outgoing = jnp.pad(outgoing, ((0, 0), (0, 0), (0, PIX_PAD - PIX)))
    up, down, head = halves_of(student_up), halves_of(student_down), halves_of(student_head)
    embed = halves_of(jnp.pad(student_embed, ((0, PIX_PAD - PIX), (0, 0))))
    outgoing, up, down, head, embed, gain, *first = lax.optimization_barrier(
        (outgoing, up, down, head, embed, student_gain[None], *first)
    )
    across, back, ahead = first
    second = [
        moved(across, x=1), moved(across, x=-1), moved(back[:REST], x=1), moved(ahead[REST:], x=-1)
    ]
    arrived = lax.all_to_all(outgoing, "pool", split_axis=0, concat_axis=0, tiled=True)
    rows = arrived.reshape(pool_size * BLK, PIX_PAD)

    lifted = bf16_dot(rows, embed[0], NN) + bf16_dot(rows, embed[1], NN)
    normed_s = halves_of(lifted * rms_scale(lifted) * student_gain)
    pre = halved_dot(normed_s, up)
    cdf = 0.5 * (1.0 + lax.erf(pre * (2.0**-0.5)))
    act = halves_of(pre * cdf)
    slope = cdf + pre * jnp.exp(-0.5 * pre * pre) * ((2.0 * jnp.pi) ** -0.5)
    act, slope, *second = lax.optimization_barrier((act, slope, *second))
    back_across, ahead_across, low_near, high_near = second
    third = [moved(back_across[:REST], x=1), moved(ahead_across[REST:], x=-1)]
    near = with_core([shard, across, back, back_across, ahead, ahead_across])
    hidden = halves_of(lifted + halved_dot(act, down))
    student_out = halved_dot(hidden, head)
    student_out, *third = lax.optimization_barrier((student_out, *third))
    low = with_core([low_near, third[0]])
    high = with_core([high_near, third[1]])

    core = lax.rem(lax.axis_index("student"), 2).reshape(1)
    *sums_a, down_rest, d_hidden, total = teacher_and_head(
        core, owners, rows, teacher_gain, gathered, near + low, high, student_out, hidden, act, head
    )
    theirs_a = core_swap(sums_a[1])
    sums_b = trunk_backward(
        core, d_hidden, slope, down, up, normed_s, lifted, gain, rows, down_rest, total
    )
    rank = lax.axis_index("student") // 2 * 8 + lax.axis_index("pool")
    owner = jnp.logical_and(core == 1, rank == RANKS - 1).astype(jnp.int32)
    theirs_a, *sums_b = lax.optimization_barrier((theirs_a, *sums_b))
    sent = [core_sum(sums_a[0], theirs_a), core_sum(sums_b[0], core_swap(sums_b[1]))]
    got = to_all_ranks(jnp.concatenate(sent, axis=1))
    half = to_all_ranks(add_chunk(owner, got))
    head_sum, down_sum, up_sum, embed_sum, gain_sum, mean_distance = unpack_sums(
        core, half, core_swap(half)
    )
    return (mean_distance.reshape(()), embed_sum, gain_sum.reshape(D_S), up_sum, down_sum, head_sum)


def solution(mesh):
    in_specs = (
        P(("student", "pool"), None, None),
        P(("student", "pool"), None),
        P(("student", "pool"), None),
        P(),
        P(),
        P(),
        P(),
        P(),
        P("pool", None, "student"),
        P("pool", None),
        P("pool", None, "student"),
        P("pool", None, "student"),
    )
    out_specs = (P(), P(), P(), P(), P(), P())
    return jax.shard_map(
        on_device, mesh=mesh, in_specs=in_specs, out_specs=out_specs, check_vma=False
    )
```

time: 310 us -> 297 us (0.958)
  Pallas kernels: 95.5 us -> 87.2 us
  local copies, waits for them, and re-layouts: 21 us -> 17.9 us
    ppermute x19, waiting for transfers between devices: 17.2 us -> 7.31 us  [moved(): return lax.ppermute(values, BOTH, pairs)]
    pallas_call x3 -> x2, Pallas kernels: 72.7 us -> 64.4 us  [the longest x1 58.1 us: teacher_and_head(): pl.pallas_call(teacher_kernel, in_specs=[smem] * 3 + [vmem] * 2 + [anywhe...]
    all_gather x1, waiting for transfers between devices: 0.01 us -> 4.09 us  [on_device(): lax.all_gather(jnp.concatenate([project[:CUT], embed_shard], axis=0), 'st...]
    all_to_all x1, waiting for transfers between devices: 0.01 us -> 4.07 us  [on_device(): lax.all_to_all(outgoing, 'pool', split_axis=0, concat_axis=0, tiled=True)]
    unnamed x74 -> x80, local copies, waits for them, and re-layouts: 6.95 us -> 4.96 us
    convert_element_type x7 -> x6, other arithmetic: 6.98 us -> 6.83 us  [halves_of(): return (high.astype(jnp.bfloat16), (values - high).astype(jnp.bfloat16))]
  transfers between devices with their start and end apart: 25 -> 25, of which waited for: 7 -> 10; matrix products, arithmetic and copies ran while one was open for 16% -> 15% of each run, Pallas kernels for 18% -> 8%
where the time goes in v3:
time: 297 us; the launch traced here: 291 us
  Pallas kernels  87.2 us (29%)
  waiting for transfers between devices  50.6 us (17%)
  starting transfers between devices  45.3 us (15%)
  blocking collectives  34.5 us (12%)
  matrix products  24.3 us (8%)
  between operations  18.7 us (6%)
  local copies, waits for them, and re-layouts  17.9 us (6%)
  other arithmetic  12.6 us (4%)
    pallas_call x1, Pallas kernels, teacher_and_head(): pl.pallas_call(teacher_kernel, in_specs=[smem] * 3 + [vmem] * 2 + [anywhe...  58.1 us
    all_to_all x1, blocking collectives, to_all_ranks(): lax.all_to_all(values, BOTH, 0, 0, axis_index_groups=core_groups(), tiled...  34.5 us
    all_to_all x1, waiting for transfers between devices, to_all_ranks(): lax.all_to_all(values, BOTH, 0, 0, axis_index_groups=core_groups(), tiled...  27.4 us
    ppermute x19, starting transfers between devices, moved(): return lax.ppermute(values, BOTH, pairs)  25.8 us
    dot_general x11, matrix products, bf16_dot(): lax.dot_general(left, right, dims, preferred_element_type=jnp.float32)  24.3 us
    pallas_call x1, Pallas kernels, trunk_backward(): pl.pallas_call(trunk_kernel, grid=(S_HID // tile,), in_specs=[pl.BlockSpe...  22.3 us
    all_to_all x1, starting transfers between devices, to_all_ranks(): lax.all_to_all(values, BOTH, 0, 0, axis_index_groups=core_groups(), tiled...  10.1 us
    ppermute x3, waiting for transfers between devices, core_swap(): return lax.ppermute(values, BOTH, pairs)  7.68 us
  transfers between devices with their start and end apart: 25, of which 10 were waited for; matrix products, arithmetic and copies ran while one was open for 15% of the time, Pallas kernels for 8%

profile of v3, /device:TPU:1, one launch (start us, length us, event | category | flops | bytes accessed | tf_op | source)
XLA Modules:
  0.0 291.2 jit_solution(17570371473675833130)
XLA Ops:
  11.3 3.4 %collective-permute-start.2 = (bf16[192,1536]{1,0:T(8,128)(2,1)S(1)}, bf16[192,1536]{1,0:T(8,128)(2,1)}, u32[]{:S(2)}, u32[]{:S(2)}) collective-permute-start(bf16[192,1536]{1,0:T(8,128)(2,1)S(1)} %pad_maximum_fusion.1.rest_0_), channel_id=1, source_target_pairs={{0,96},{1,97},{2,98},{3,99},{4,100},{5,101},{6,102},{7,103},{8,104... | collective-permute-start | bytes 1769480 | tf_op jit(solution)/shard_map/ppermute | solution.py:109
  14.7 3.6 %collective-permute-start = (bf16[192,1536]{1,0:T(8,128)(2,1)S(1)}, bf16[192,1536]{1,0:T(8,128)(2,1)}, u32[]{:S(2)}, u32[]{:S(2)}) collective-permute-start(bf16[192,1536]{1,0:T(8,128)(2,1)S(1)} %pad_maximum_fusion.1.rest_0_), channel_id=1, source_target_pairs={{0,16},{1,17},{2,18},{3,19},{4,20},{5,21},{6,22},{7,23},{8,24},{9,... | collective-permute-start | bytes 1769480 | tf_op jit(solution)/shard_map/ppermute | solution.py:109
  29.4 2.5 fusion.5
  32.0 1.8 fusion.6
  34.6 4.7 %all-to-all-start = ((bf16[8,128,640]{2,1,0:T(8,128)(2,1)}), bf16[8,128,640]{2,1,0:T(8,128)(2,1)S(1)}, u32[]{:S(2)}, u32[]{:S(2)}) async-start(bf16[8,128,640]{2,1,0:T(8,128)(2,1)} %pad.12), calls=%async_computation | async-start | bytes 2621440 | tf_op jit(solution)/shard_map/all_to_all | solution.py:583
  39.3 4.1 %collective-permute-start.7 = (bf16[192,1536]{1,0:T(8,128)(2,1)}, bf16[192,1536]{1,0:T(8,128)(2,1)}, u32[]{:S(2)}, u32[]{:S(2)}) collective-permute-start(bf16[192,1536]{1,0:T(8,128)(2,1)} %copy-done.23), channel_id=1, source_target_pairs={{0,8},{1,9},{2,10},{3,11},{4,12},{5,13},{6,14},{7,15},{8,0},{9,1},... | collective-permute-start | bytes 1769480 | tf_op jit(solution)/shard_map/ppermute | solution.py:109
  43.4 3.3 %collective-permute-start.4 = (bf16[192,1536]{1,0:T(8,128)(2,1)}, bf16[192,1536]{1,0:T(8,128)(2,1)}, u32[]{:S(2)}, u32[]{:S(2)}) collective-permute-start(bf16[192,1536]{1,0:T(8,128)(2,1)} %collective-permute-done.rest_1_), channel_id=1, source_target_pairs={{0,96},{1,97},{2,98},{3,99},{4,100},{5,101},{6,102},{7,103},{8,104... | collective-permute-start | bytes 1769480 | tf_op jit(solution)/shard_map/ppermute | solution.py:109
  48.4 1.7 slice.45
  50.1 2.7 collective-permute-start.6
  53.3 4.1 %all-to-all-done = bf16[8,128,640]{2,1,0:T(8,128)(2,1)S(1)} async-done(((bf16[8,128,640]{2,1,0:T(8,128)(2,1)}), bf16[8,128,640]{2,1,0:T(8,128)(2,1)S(1)}, u32[]{:S(2)}, u32[]{:S(2)}) %all-to-all-start) | async-done | bytes 1310752 | tf_op jit(solution)/shard_map/all_to_all | solution.py:583
  59.7 1.8 fusion.15
  61.5 1.8 fusion.14
  63.4 5.3 %fusion.4 = (f32[1024,1536]{1,0:T(8,128)}, f32[1024,1536]{1,0:T(8,128)S(1)}) fusion(f32[1024,1536]{1,0:T(8,128)S(1)} %fusion.14, f32[1024,1536]{1,0:T(8,128)S(1)} %fusion.15, bf16[1024,384]{1,0:T(8,128)(2,1)S(1)} %get-tuple-element.97.normed_hi, bf16[384,1536]{1,0:T(8,128)(2,1)S(1)} %copy-done.7), kind=kOutput, calls=%fused_computation.7 | convolution fusion | flops 1223688192 | bytes 27131904 | tf_op jit(solution)/shard_map/dot_general | solution.py:42
  68.6 2.0 fusion
  70.6 4.4 %collective-permute-done.6.rest_16_ = bf16[96,1536]{1,0:T(8,128)(2,1)} collective-permute-done((bf16[96,1536]{1,0:T(8,128)(2,1)}, bf16[96,1536]{1,0:T(8,128)(2,1)}, u32[]{:S(2)}, u32[]{:S(2)}) %collective-permute-start.6) | collective-permute-done | bytes 294944 | tf_op jit(solution)/shard_map/ppermute | solution.py:109
  77.9 2.3 collective-permute-start.11
  83.8 1.8 fusion.17
  85.6 1.8 fusion.16
  87.5 1.9 fusion.9
  91.0 1.8 fusion.18
  92.8 1.8 fusion.19
  95.8 4.4 %add_add_fusion.rest_20_ = f32[1024,1536]{1,0:T(8,128)} fusion(f32[1024,1536]{1,0:T(8,128)S(1)} %fusion.18, f32[1024,1536]{1,0:T(8,128)S(1)} %fusion.19, bf16[1024,384]{1,0:T(8,128)(2,1)S(1)} %reduce-precision_convert_fusion.4.rest_21_, bf16[384,1536]{1,0:T(8,128)(2,1)S(1)} %copy-done.8), kind=kOutput, calls=%fused_computation.8 | convolution fusion | flops 1211105280 | bytes 20840448 | tf_op jit(solution)/shard_map/dot_general | solution.py:42
  103.6 4.1 %all-gather.3.cloned.1.call-done = bf16[3840,1536]{1,0:T(8,128)(2,1)} async-done(((bf16[240,1536]{1,0:T(8,128)(2,1)}), bf16[3840,1536]{1,0:T(8,128)(2,1)}) %all-gather.3.cloned.1.call-update) | async-done | bytes 11796496 | tf_op jit(solution)/shard_map/all_gather | solution.py:556
  107.8 58.1 %teacher_and_head.1 = (f32[4096,128]{1,0:T(8,128)}, f32[4096,128]{1,0:T(8,128)}, f32[1536,128]{1,0:T(8,128)}, f32[1024,384]{1,0:T(8,128)}, f32[8,128]{1,0:T(8,128)}) custom-call(s32[1]{0:T(128)} %bitcast.core, s32[16]{0:T(128)} %stack.67.project_owners.output_owners, s32[16]{0:T(128)} %stack.67.project_owners.output_owners, bf16[1024,640]{1,0:T(8,128)(2,1)} %bitcast.64, ...), custom_call_target="tpu_custom_call" | custom-call | flops 32212254720 | bytes 52428800 | tf_op jit(solution)/shard_map/teacher_and_head/pallas_call | solution.py:307
  166.4 22.3 %trunk_backward.1 = (f32[4096,128]{1,0:T(8,128)}, f32[4096,128]{1,0:T(8,128)}) custom-call(s32[1]{0:T(128)} %bitcast.core, f32[1024,384]{1,0:T(8,128)} %get-tuple-element.68.d_hidden, f32[1024,1536]{1,0:T(8,128)} %get-tuple-element.69.slope, bf16[1536,384]{1,0:T(8,128)(2,1)} %get-tuple-element.57.down_hi, bf16[1536,384]{1,0:T(8,128)(2,1)} %get-tuple-element.59.down_lo, ...), custom_call_target="tpu_custom_call" | custom-call | flops 11878268928 | bytes 31457280 | tf_op jit(solution)/shard_map/trunk_backward/pallas_call | solution.py:389
  189.3 3.9 %collective-permute-done.20 = f32[4096,128]{1,0:T(8,128)S(1)} collective-permute-done((f32[4096,128]{1,0:T(8,128)}, f32[4096,128]{1,0:T(8,128)S(1)}, u32[]{:S(2)}, u32[]{:S(2)}) %collective-permute-start.20) | collective-permute-done | bytes 2097184 | tf_op jit(solution)/shard_map/ppermute | solution.py:136
  195.0 10.1 %all-to-all-start.1 = ((bf16[64,128,128]{2,1,0:T(8,128)(2,1)}), bf16[64,128,128]{2,1,0:T(8,128)(2,1)S(1)}, u32[]{:S(2)}, u32[]{:S(2)}) async-start(bf16[64,128,128]{2,1,0:T(8,128)(2,1)} %pad_maximum_fusion), calls=%async_computation.1 | async-start | bytes 4194304 | tf_op jit(solution)/shard_map/all_to_all | solution.py:511
  205.2 27.4 %all-to-all-done.1.got = bf16[64,128,128]{2,1,0:T(8,128)(2,1)S(1)} async-done(((bf16[64,128,128]{2,1,0:T(8,128)(2,1)}), bf16[64,128,128]{2,1,0:T(8,128)(2,1)S(1)}, u32[]{:S(2)}, u32[]{:S(2)}) %all-to-all-start.1) | async-done | bytes 2097184 | tf_op jit(solution)/shard_map/all_to_all | solution.py:511
  233.1 34.5 %all_to_all.15.mine_hbm = bf16[64,128,128]{2,1,0:T(8,128)(2,1)S(1)} all-to-all(bf16[64,128,128]{2,1,0:T(8,128)(2,1)S(1)} %add_chunk.1), channel_id=1, replica_groups={{0,1,2,3,4,5,6,7,16,17,18,19,20,21,22,23,32,33,34,35,36,37,38,39,48,49,..., dimensions={0} | all-to-all | bytes 4194304 | tf_op jit(solution)/shard_map/all_to_all | solution.py:511
  267.6 3.7 %collective-permute-start.21 = (bf16[64,128,128]{2,1,0:T(8,128)(2,1)S(1)}, bf16[64,128,128]{2,1,0:T(8,128)(2,1)S(1)}, u32[]{:S(2)}, u32[]{:S(2)}) collective-permute-start(bf16[64,128,128]{2,1,0:T(8,128)(2,1)S(1)} %all_to_all.15.mine_hbm), channel_id=1, source_target_pairs={{0,8},{1,9},{2,10},{3,11},{4,12},{5,13},{6,14},{7,15},{8,0},{9,1},... | collective-permute-start | bytes 6291464 | tf_op jit(solution)/shard_map/ppermute | solution.py:136
  271.3 3.8 %collective-permute-done.21.theirs_hbm = bf16[64,128,128]{2,1,0:T(8,128)(2,1)S(1)} collective-permute-done((bf16[64,128,128]{2,1,0:T(8,128)(2,1)S(1)}, bf16[64,128,128]{2,1,0:T(8,128)(2,1)S(1)}, u32[]{:S(2)}, u32[]{:S(2)}) %collective-permute-start.21) | collective-permute-done | bytes 2097184 | tf_op jit(solution)/shard_map/ppermute | solution.py:136
  276.5 6.4 %unpack_sums.1 = (f32[384,1536]{1,0:T(8,128)}, f32[1536,384]{1,0:T(8,128)}, f32[384,1536]{1,0:T(8,128)}, f32[588,384]{1,0:T(8,128)}, f32[1,384]{1,0:T(1,128)}, /*index=5*/f32[1]{0:T(128)}) custom-call(s32[1]{0:T(128)} %bitcast.core, bf16[64,128,128]{2,1,0:T(8,128)(2,1)} %copy-done.3, bf16[64,128,128]{2,1,0:T(8,128)(2,1)} %copy-done.17), custom_call_target="tpu_custom_call" | custom-call | bytes 12582912 | tf_op jit(solution)/shard_map/unpack_sums/pallas_call | solution.py:492
  (145 shorter events, 35.4 us)
Async XLA Ops:
  7.2 100.6 %all-gather.3.cloned.1.call-start = ((), (), s32[]{:S(2)}) async-start(), calls=%async_computation.3 | async-start | bytes 12533760 | tf_op jit(solution)/shard_map/all_gather | solution.py:556
  11.3 16.4 %copy-start.23 = (bf16[192,1536]{1,0:T(8,128)(2,1)}, bf16[192,1536]{1,0:T(8,128)(2,1)S(1)}, u32[]{:S(2)}) copy-start(bf16[192,1536]{1,0:T(8,128)(2,1)S(1)} %pad_maximum_fusion.1.rest_0_) | copy-start | bytes 1769476
  11.3 22.4 %collective-permute-start.2 = (bf16[192,1536]{1,0:T(8,128)(2,1)S(1)}, bf16[192,1536]{1,0:T(8,128)(2,1)}, u32[]{:S(2)}, u32[]{:S(2)}) collective-permute-start(bf16[192,1536]{1,0:T(8,128)(2,1)S(1)} %pad_maximum_fusion.1.rest_0_), channel_id=1, source_target_pairs={{0,96},{1,97},{2,98},{3,99},{4,100},{5,101},{6,102},{7,103},{8,104... | collective-permute-start | bytes 1769480 | tf_op jit(solution)/shard_map/ppermute | solution.py:109
  14.7 19.1 %collective-permute-start.1 = (bf16[192,1536]{1,0:T(8,128)(2,1)S(1)}, bf16[192,1536]{1,0:T(8,128)(2,1)S(1)}, u32[]{:S(2)}, u32[]{:S(2)}) collective-permute-start(bf16[192,1536]{1,0:T(8,128)(2,1)S(1)} %pad_maximum_fusion.1.rest_0_), channel_id=1, source_target_pairs={{0,32},{1,33},{2,34},{3,35},{4,36},{5,37},{6,38},{7,39},{8,40},{9,... | collective-permute-start | bytes 1769480 | tf_op jit(solution)/shard_map/ppermute | solution.py:109
  14.7 19.6 %collective-permute-start = (bf16[192,1536]{1,0:T(8,128)(2,1)S(1)}, bf16[192,1536]{1,0:T(8,128)(2,1)}, u32[]{:S(2)}, u32[]{:S(2)}) collective-permute-start(bf16[192,1536]{1,0:T(8,128)(2,1)S(1)} %pad_maximum_fusion.1.rest_0_), channel_id=1, source_target_pairs={{0,16},{1,17},{2,18},{3,19},{4,20},{5,21},{6,22},{7,23},{8,24},{9,... | collective-permute-start | bytes 1769480 | tf_op jit(solution)/shard_map/ppermute | solution.py:109
  32.0 29.6 %copy-start.1 = (bf16[384,1536]{1,0:T(8,128)(2,1)}, bf16[384,1536]{1,0:T(8,128)(2,1)S(1)}, u32[]{:S(2)}) copy-start(bf16[384,1536]{1,0:T(8,128)(2,1)S(1)} %get-tuple-element.50.up_hi) | copy-start | bytes 3538948
  34.6 22.8 %all-to-all-start = ((bf16[8,128,640]{2,1,0:T(8,128)(2,1)}), bf16[8,128,640]{2,1,0:T(8,128)(2,1)S(1)}, u32[]{:S(2)}, u32[]{:S(2)}) async-start(bf16[8,128,640]{2,1,0:T(8,128)(2,1)} %pad.12), calls=%async_computation | async-start | bytes 2621440 | tf_op jit(solution)/shard_map/all_to_all | solution.py:583
  39.3 55.3 %collective-permute-start.7 = (bf16[192,1536]{1,0:T(8,128)(2,1)}, bf16[192,1536]{1,0:T(8,128)(2,1)}, u32[]{:S(2)}, u32[]{:S(2)}) collective-permute-start(bf16[192,1536]{1,0:T(8,128)(2,1)} %copy-done.23), channel_id=1, source_target_pairs={{0,8},{1,9},{2,10},{3,11},{4,12},{5,13},{6,14},{7,15},{8,0},{9,1},... | collective-permute-start | bytes 1769480 | tf_op jit(solution)/shard_map/ppermute | solution.py:109
  43.4 36.7 %collective-permute-start.4 = (bf16[192,1536]{1,0:T(8,128)(2,1)}, bf16[192,1536]{1,0:T(8,128)(2,1)}, u32[]{:S(2)}, u32[]{:S(2)}) collective-permute-start(bf16[192,1536]{1,0:T(8,128)(2,1)} %collective-permute-done.rest_1_), channel_id=1, source_target_pairs={{0,96},{1,97},{2,98},{3,99},{4,100},{5,101},{6,102},{7,103},{8,104... | collective-permute-start | bytes 1769480 | tf_op jit(solution)/shard_map/ppermute | solution.py:109
  46.7 33.5 %collective-permute-start.3 = (bf16[192,1536]{1,0:T(8,128)(2,1)}, bf16[192,1536]{1,0:T(8,128)(2,1)}, u32[]{:S(2)}, u32[]{:S(2)}) collective-permute-start(bf16[192,1536]{1,0:T(8,128)(2,1)} %collective-permute-done.rest_1_), channel_id=1, source_target_pairs={{0,32},{1,33},{2,34},{3,35},{4,36},{5,37},{6,38},{7,39},{8,40},{9,... | collective-permute-start | bytes 1769480 | tf_op jit(solution)/shard_map/ppermute | solution.py:109
  50.1 25.0 %collective-permute-start.6 = (bf16[96,1536]{1,0:T(8,128)(2,1)}, bf16[96,1536]{1,0:T(8,128)(2,1)}, u32[]{:S(2)}, u32[]{:S(2)}) collective-permute-start(bf16[96,1536]{1,0:T(8,128)(2,1)} %slice.45), channel_id=1, source_target_pairs={{0,96},{1,97},{2,98},{3,99},{4,100},{5,101},{6,102},{7,103},{8,104... | collective-permute-start | bytes 884744 | tf_op jit(solution)/shard_map/ppermute | solution.py:109
  52.8 25.1 %collective-permute-start.5 = (bf16[96,1536]{1,0:T(8,128)(2,1)}, bf16[96,1536]{1,0:T(8,128)(2,1)}, u32[]{:S(2)}, u32[]{:S(2)}) collective-permute-start(bf16[96,1536]{1,0:T(8,128)(2,1)} %slice.44), channel_id=1, source_target_pairs={{0,32},{1,33},{2,34},{3,35},{4,36},{5,37},{6,38},{7,39},{8,40},{9,... | collective-permute-start | bytes 884744 | tf_op jit(solution)/shard_map/ppermute | solution.py:109
  59.3 28.1 %copy-start.6 = (f32[1024,384]{1,0:T(8,128)}, f32[1024,384]{1,0:T(8,128)S(1)}, u32[]{:S(2)}) copy-start(f32[1024,384]{1,0:T(8,128)S(1)} %get-tuple-element.109.lifted) | copy-start | bytes 4718596
  68.6 15.2 %copy-start.20 = (bf16[1536,384]{1,0:T(8,128)(2,1)S(1)}, bf16[1536,384]{1,0:T(8,128)(2,1)}, u32[]{:S(2)}) copy-start(bf16[1536,384]{1,0:T(8,128)(2,1)} %get-tuple-element.57.down_hi) | copy-start | bytes 3538948
  70.6 15.0 %copy-start.10 = (bf16[1024,1536]{1,0:T(8,128)(2,1)}, bf16[1024,1536]{1,0:T(8,128)(2,1)S(1)}, u32[]{:S(2)}) copy-start(bf16[1024,1536]{1,0:T(8,128)(2,1)S(1)} %get-tuple-element.58.rest_24_) | copy-start | bytes 9437188
  70.6 16.8 %copy-start.11 = (bf16[1024,1536]{1,0:T(8,128)(2,1)}, bf16[1024,1536]{1,0:T(8,128)(2,1)S(1)}, u32[]{:S(2)}) copy-start(bf16[1024,1536]{1,0:T(8,128)(2,1)S(1)} %get-tuple-element.56.rest_23_) | copy-start | bytes 9437188
  75.1 20.1 %collective-permute-start.9 = (bf16[192,1536]{1,0:T(8,128)(2,1)S(1)}, bf16[192,1536]{1,0:T(8,128)(2,1)S(1)}, u32[]{:S(2)}, u32[]{:S(2)}) collective-permute-start(bf16[192,1536]{1,0:T(8,128)(2,1)S(1)} %copy-done.26), channel_id=1, source_target_pairs={{0,8},{1,9},{2,10},{3,11},{4,12},{5,13},{6,14},{7,15},{8,0},{9,1},... | collective-permute-start | bytes 1769480 | tf_op jit(solution)/shard_map/ppermute | solution.py:109
  77.9 22.4 %collective-permute-start.11 = (bf16[192,1536]{1,0:T(8,128)(2,1)}, bf16[192,1536]{1,0:T(8,128)(2,1)S(1)}, u32[]{:S(2)}, u32[]{:S(2)}) collective-permute-start(bf16[192,1536]{1,0:T(8,128)(2,1)} %collective-permute-done.2.rest_4_), channel_id=1, source_target_pairs={{0,8},{1,9},{2,10},{3,11},{4,12},{5,13},{6,14},{7,15},{8,0},{9,1},... | collective-permute-start | bytes 1769480 | tf_op jit(solution)/shard_map/ppermute | solution.py:109
  82.1 13.2 %collective-permute-start.14 = (bf16[96,1536]{1,0:T(8,128)(2,1)S(1)}, bf16[96,1536]{1,0:T(8,128)(2,1)S(1)}, u32[]{:S(2)}, u32[]{:S(2)}) collective-permute-start(bf16[96,1536]{1,0:T(8,128)(2,1)S(1)} %slice.47), channel_id=1, source_target_pairs={{0,96},{1,97},{2,98},{3,99},{4,100},{5,101},{6,102},{7,103},{8,104... | collective-permute-start | bytes 884744 | tf_op jit(solution)/shard_map/ppermute | solution.py:109
  82.3 13.4 %collective-permute-start.13 = (bf16[96,1536]{1,0:T(8,128)(2,1)S(1)}, bf16[96,1536]{1,0:T(8,128)(2,1)S(1)}, u32[]{:S(2)}, u32[]{:S(2)}) collective-permute-start(bf16[96,1536]{1,0:T(8,128)(2,1)S(1)} %slice.46), channel_id=1, source_target_pairs={{0,32},{1,33},{2,34},{3,35},{4,36},{5,37},{6,38},{7,39},{8,40},{9,... | collective-permute-start | bytes 884744 | tf_op jit(solution)/shard_map/ppermute | solution.py:109
  94.6 6.2 %collective-permute-start.8 = (bf16[192,1536]{1,0:T(8,128)(2,1)}, bf16[192,1536]{1,0:T(8,128)(2,1)S(1)}, u32[]{:S(2)}, u32[]{:S(2)}) collective-permute-start(bf16[192,1536]{1,0:T(8,128)(2,1)} %collective-permute-done.rest_1_), channel_id=1, source_target_pairs={{0,8},{1,9},{2,10},{3,11},{4,12},{5,13},{6,14},{7,15},{8,0},{9,1},... | collective-permute-start | bytes 1769480 | tf_op jit(solution)/shard_map/ppermute | solution.py:109
  95.2 8.4 %collective-permute-start.10 = (bf16[192,1536]{1,0:T(8,128)(2,1)}, bf16[192,1536]{1,0:T(8,128)(2,1)S(1)}, u32[]{:S(2)}, u32[]{:S(2)}) collective-permute-start(bf16[192,1536]{1,0:T(8,128)(2,1)} %collective-permute-done.3.rest_3_), channel_id=1, source_target_pairs={{0,8},{1,9},{2,10},{3,11},{4,12},{5,13},{6,14},{7,15},{8,0},{9,1},... | collective-permute-start | bytes 1769480 | tf_op jit(solution)/shard_map/ppermute | solution.py:109
  95.3 8.3 %collective-permute-start.12 = (bf16[192,1536]{1,0:T(8,128)(2,1)}, bf16[192,1536]{1,0:T(8,128)(2,1)S(1)}, u32[]{:S(2)}, u32[]{:S(2)}) collective-permute-start(bf16[192,1536]{1,0:T(8,128)(2,1)} %collective-permute-done.4.rest_5_), channel_id=1, source_target_pairs={{0,8},{1,9},{2,10},{3,11},{4,12},{5,13},{6,14},{7,15},{8,0},{9,1},... | collective-permute-start | bytes 1769480 | tf_op jit(solution)/shard_map/ppermute | solution.py:109
  95.7 5.2 %collective-permute-start.15 = (bf16[96,1536]{1,0:T(8,128)(2,1)}, bf16[96,1536]{1,0:T(8,128)(2,1)S(1)}, u32[]{:S(2)}, u32[]{:S(2)}) collective-permute-start(bf16[96,1536]{1,0:T(8,128)(2,1)} %collective-permute-done.5.rest_12_), channel_id=1, source_target_pairs={{0,8},{1,9},{2,10},{3,11},{4,12},{5,13},{6,14},{7,15},{8,0},{9,1},... | collective-permute-start | bytes 884744 | tf_op jit(solution)/shard_map/ppermute | solution.py:109
  100.3 2.1 collective-permute-start.17
  100.8 2.3 collective-permute-start.16
  101.0 2.6 collective-permute-start.18
  165.8 22.9 %collective-permute-start.19 = (f32[4096,128]{1,0:T(8,128)}, f32[4096,128]{1,0:T(8,128)S(1)}, u32[]{:S(2)}, u32[]{:S(2)}) collective-permute-start(f32[4096,128]{1,0:T(8,128)} %get-tuple-element.67), channel_id=1, source_target_pairs={{0,8},{1,9},{2,10},{3,11},{4,12},{5,13},{6,14},{7,15},{8,0},{9,1},... | collective-permute-start | bytes 6291464 | tf_op jit(solution)/shard_map/ppermute | solution.py:136
  166.4 22.7 %copy-start.15 = (f32[4096,128]{1,0:T(8,128)S(1)}, f32[4096,128]{1,0:T(8,128)}, u32[]{:S(2)}) copy-start(f32[4096,128]{1,0:T(8,128)} %get-tuple-element.66) | copy-start | bytes 6291460
  188.7 4.5 %collective-permute-start.20 = (f32[4096,128]{1,0:T(8,128)}, f32[4096,128]{1,0:T(8,128)S(1)}, u32[]{:S(2)}, u32[]{:S(2)}) collective-permute-start(f32[4096,128]{1,0:T(8,128)} %get-tuple-element.77), channel_id=1, source_target_pairs={{0,8},{1,9},{2,10},{3,11},{4,12},{5,13},{6,14},{7,15},{8,0},{9,1},... | collective-permute-start | bytes 6291464 | tf_op jit(solution)/shard_map/ppermute | solution.py:136
  195.0 37.6 %all-to-all-start.1 = ((bf16[64,128,128]{2,1,0:T(8,128)(2,1)}), bf16[64,128,128]{2,1,0:T(8,128)(2,1)S(1)}, u32[]{:S(2)}, u32[]{:S(2)}) async-start(bf16[64,128,128]{2,1,0:T(8,128)(2,1)} %pad_maximum_fusion), calls=%async_computation.1 | async-start | bytes 4194304 | tf_op jit(solution)/shard_map/all_to_all | solution.py:511
  267.6 7.5 %collective-permute-start.21 = (bf16[64,128,128]{2,1,0:T(8,128)(2,1)S(1)}, bf16[64,128,128]{2,1,0:T(8,128)(2,1)S(1)}, u32[]{:S(2)}, u32[]{:S(2)}) collective-permute-start(bf16[64,128,128]{2,1,0:T(8,128)(2,1)S(1)} %all_to_all.15.mine_hbm), channel_id=1, source_target_pairs={{0,8},{1,9},{2,10},{3,11},{4,12},{5,13},{6,14},{7,15},{8,0},{9,1},... | collective-permute-start | bytes 6291464 | tf_op jit(solution)/shard_map/ppermute | solution.py:136
  (33 other events, 156.1 us)
Sparse Core Ops, SparseCore 0:
  11.0 96.7 all-gather.2

commit v4 on v3

--- a/solution.py
+++ b/solution.py
@@ -464,7 +464,7 @@
             embed[:, strip(i)] = take(halves, 1, EMBED_AT + i * EMBED_ROWS, EMBED_ROWS)[:PIX]
         gains = take(halves, 1, GAIN_AT, 16)
         for i in range(D_S // LANES):
-            gain[:, strip(i)] = gains[i : i + 1]
+            gain[strip(i)] = gains[i]
         lane = lax.broadcasted_iota(jnp.int32, (1, LANES), 1)
         cosines = jnp.where(lane < 3, take(halves, 1, SUM_ROWS - 16, 16)[15:], 0.0)
         mean_distance[0] = 1.0 - jnp.sum(cosines) * (1.0 / (DEVICES * 2 * BLK))
@@ -493,11 +493,11 @@
         unpack_kernel,
         in_specs=[smem, anywhere, anywhere],
         out_specs=[anywhere] * 4 + [vmem, smem],
-        out_shape=[jax.ShapeDtypeStruct(shape, jnp.float32) for shape in shapes + [(1, D_S), (1,)]],
+        out_shape=[jax.ShapeDtypeStruct(shape, jnp.float32) for shape in shapes + [(D_S,), (1,)]],
         scratch_shapes=[pltpu.VMEM(mine.shape, mine.dtype)] * 2
         + [pltpu.VMEM(shape, jnp.float32) for shape in shapes]
         + [pltpu.SemaphoreType.DMA((6,))],
-        compiler_params=pltpu.CompilerParams(vmem_limit_bytes=56 * 1024 * 1024),
+        compiler_params=pltpu.CompilerParams(vmem_limit_bytes=24 * 1024 * 1024),
         cost_estimate=pl.CostEstimate(flops=0, bytes_accessed=12 * 1024 * 1024, transcendentals=0),
         name="unpack_sums",
     )(core, mine, theirs)
@@ -616,7 +616,7 @@
     head_sum, down_sum, up_sum, embed_sum, gain_sum, mean_distance = unpack_sums(
         core, half, core_swap(half)
     )
-    return (mean_distance.reshape(()), embed_sum, gain_sum.reshape(D_S), up_sum, down_sum, head_sum)
+    return (mean_distance.reshape(()), embed_sum, gain_sum, up_sum, down_sum, head_sum)
 
 
 def solution(mesh):

time: 297 us -> 292 us (0.983)
  no operation moved by 1% of the time
where the time goes in v4:
time: 292 us; the launch traced here: 287 us
  Pallas kernels  85.3 us (29%)
  waiting for transfers between devices  50.6 us (17%)
  starting transfers between devices  45.3 us (16%)
  blocking collectives  34.5 us (12%)
  matrix products  24.3 us (8%)
  between operations  18.8 us (6%)
  local copies, waits for them, and re-layouts  16.5 us (6%)
  other arithmetic  11.3 us (4%)
    pallas_call x1, Pallas kernels, teacher_and_head(): pl.pallas_call(teacher_kernel, in_specs=[smem] * 3 + [vmem] * 2 + [anywhe...  58.1 us
    all_to_all x1, blocking collectives, to_all_ranks(): lax.all_to_all(values, BOTH, 0, 0, axis_index_groups=core_groups(), tiled...  34.5 us
    all_to_all x1, waiting for transfers between devices, to_all_ranks(): lax.all_to_all(values, BOTH, 0, 0, axis_index_groups=core_groups(), tiled...  27.4 us
    ppermute x19, starting transfers between devices, moved(): return lax.ppermute(values, BOTH, pairs)  25.9 us
    dot_general x11, matrix products, bf16_dot(): lax.dot_general(left, right, dims, preferred_element_type=jnp.float32)  24.3 us
    pallas_call x1, Pallas kernels, trunk_backward(): pl.pallas_call(trunk_kernel, grid=(S_HID // tile,), in_specs=[pl.BlockSpe...  22.3 us
    all_to_all x1, starting transfers between devices, to_all_ranks(): lax.all_to_all(values, BOTH, 0, 0, axis_index_groups=core_groups(), tiled...  10.1 us
    ppermute x3, waiting for transfers between devices, core_swap(): return lax.ppermute(values, BOTH, pairs)  7.69 us
  transfers between devices with their start and end apart: 25, of which 10 were waited for; matrix products, arithmetic and copies ran while one was open for 15% of the time, Pallas kernels for 8%

profile of v4, /device:TPU:1, one launch (start us, length us, event | category | flops | bytes accessed | tf_op | source)
XLA Modules:
  0.0 286.6 jit_solution(16131256533476488401)
XLA Ops:
  11.3 3.4 %collective-permute-start.2 = (bf16[192,1536]{1,0:T(8,128)(2,1)S(1)}, bf16[192,1536]{1,0:T(8,128)(2,1)}, u32[]{:S(2)}, u32[]{:S(2)}) collective-permute-start(bf16[192,1536]{1,0:T(8,128)(2,1)S(1)} %pad_maximum_fusion.1.rest_0_), channel_id=1, source_target_pairs={{0,96},{1,97},{2,98},{3,99},{4,100},{5,101},{6,102},{7,103},{8,104... | collective-permute-start | bytes 1769480 | tf_op jit(solution)/shard_map/ppermute | solution.py:109
  14.7 3.6 %collective-permute-start = (bf16[192,1536]{1,0:T(8,128)(2,1)S(1)}, bf16[192,1536]{1,0:T(8,128)(2,1)}, u32[]{:S(2)}, u32[]{:S(2)}) collective-permute-start(bf16[192,1536]{1,0:T(8,128)(2,1)S(1)} %pad_maximum_fusion.1.rest_0_), channel_id=1, source_target_pairs={{0,16},{1,17},{2,18},{3,19},{4,20},{5,21},{6,22},{7,23},{8,24},{9,... | collective-permute-start | bytes 1769480 | tf_op jit(solution)/shard_map/ppermute | solution.py:109
  29.4 2.5 fusion.5
  31.9 1.7 fusion.6
  34.5 4.7 %all-to-all-start = ((bf16[8,128,640]{2,1,0:T(8,128)(2,1)}), bf16[8,128,640]{2,1,0:T(8,128)(2,1)S(1)}, u32[]{:S(2)}, u32[]{:S(2)}) async-start(bf16[8,128,640]{2,1,0:T(8,128)(2,1)} %pad.12), calls=%async_computation | async-start | bytes 2621440 | tf_op jit(solution)/shard_map/all_to_all | solution.py:583
  39.3 4.2 %collective-permute-start.7 = (bf16[192,1536]{1,0:T(8,128)(2,1)}, bf16[192,1536]{1,0:T(8,128)(2,1)}, u32[]{:S(2)}, u32[]{:S(2)}) collective-permute-start(bf16[192,1536]{1,0:T(8,128)(2,1)} %copy-done.21), channel_id=1, source_target_pairs={{0,8},{1,9},{2,10},{3,11},{4,12},{5,13},{6,14},{7,15},{8,0},{9,1},... | collective-permute-start | bytes 1769480 | tf_op jit(solution)/shard_map/ppermute | solution.py:109
  43.4 3.3 %collective-permute-start.4 = (bf16[192,1536]{1,0:T(8,128)(2,1)}, bf16[192,1536]{1,0:T(8,128)(2,1)}, u32[]{:S(2)}, u32[]{:S(2)}) collective-permute-start(bf16[192,1536]{1,0:T(8,128)(2,1)} %collective-permute-done.rest_1_), channel_id=1, source_target_pairs={{0,96},{1,97},{2,98},{3,99},{4,100},{5,101},{6,102},{7,103},{8,104... | collective-permute-start | bytes 1769480 | tf_op jit(solution)/shard_map/ppermute | solution.py:109
  48.4 1.7 slice.45
  50.1 2.7 collective-permute-start.6
  53.3 4.0 %all-to-all-done = bf16[8,128,640]{2,1,0:T(8,128)(2,1)S(1)} async-done(((bf16[8,128,640]{2,1,0:T(8,128)(2,1)}), bf16[8,128,640]{2,1,0:T(8,128)(2,1)S(1)}, u32[]{:S(2)}, u32[]{:S(2)}) %all-to-all-start) | async-done | bytes 1310752 | tf_op jit(solution)/shard_map/all_to_all | solution.py:583
  59.6 1.8 fusion.15
  61.5 1.8 fusion.14
  63.3 5.3 %fusion.4 = (f32[1024,1536]{1,0:T(8,128)}, f32[1024,1536]{1,0:T(8,128)S(1)}) fusion(f32[1024,1536]{1,0:T(8,128)S(1)} %fusion.14, f32[1024,1536]{1,0:T(8,128)S(1)} %fusion.15, bf16[1024,384]{1,0:T(8,128)(2,1)S(1)} %get-tuple-element.97.normed_hi, bf16[384,1536]{1,0:T(8,128)(2,1)S(1)} %copy-done.6), kind=kOutput, calls=%fused_computation.7 | convolution fusion | flops 1223688192 | bytes 27131904 | tf_op jit(solution)/shard_map/dot_general | solution.py:42
  68.6 2.0 fusion
  70.6 4.5 %collective-permute-done.6.rest_16_ = bf16[96,1536]{1,0:T(8,128)(2,1)} collective-permute-done((bf16[96,1536]{1,0:T(8,128)(2,1)}, bf16[96,1536]{1,0:T(8,128)(2,1)}, u32[]{:S(2)}, u32[]{:S(2)}) %collective-permute-start.6) | collective-permute-done | bytes 294944 | tf_op jit(solution)/shard_map/ppermute | solution.py:109
  77.9 2.3 collective-permute-start.11
  83.8 1.8 fusion.17
  85.6 1.8 fusion.16
  87.5 1.9 fusion.9
  91.0 1.8 fusion.18
  92.8 1.8 fusion.19
  95.8 4.4 %add_add_fusion.rest_20_ = f32[1024,1536]{1,0:T(8,128)} fusion(f32[1024,1536]{1,0:T(8,128)S(1)} %fusion.18, f32[1024,1536]{1,0:T(8,128)S(1)} %fusion.19, bf16[1024,384]{1,0:T(8,128)(2,1)S(1)} %reduce-precision_convert_fusion.4.rest_21_, bf16[384,1536]{1,0:T(8,128)(2,1)S(1)} %copy-done.7), kind=kOutput, calls=%fused_computation.8 | convolution fusion | flops 1211105280 | bytes 20840448 | tf_op jit(solution)/shard_map/dot_general | solution.py:42
  103.6 4.1 %all-gather.3.cloned.1.call-done = bf16[3840,1536]{1,0:T(8,128)(2,1)} async-done(((bf16[240,1536]{1,0:T(8,128)(2,1)}), bf16[3840,1536]{1,0:T(8,128)(2,1)}) %all-gather.3.cloned.1.call-update) | async-done | bytes 11796496 | tf_op jit(solution)/shard_map/all_gather | solution.py:556
  107.8 58.1 %teacher_and_head.1 = (f32[4096,128]{1,0:T(8,128)}, f32[4096,128]{1,0:T(8,128)}, f32[1536,128]{1,0:T(8,128)}, f32[1024,384]{1,0:T(8,128)}, f32[8,128]{1,0:T(8,128)}) custom-call(s32[1]{0:T(128)} %bitcast.core, s32[16]{0:T(128)} %stack.67.project_owners.output_owners, s32[16]{0:T(128)} %stack.67.project_owners.output_owners, bf16[1024,640]{1,0:T(8,128)(2,1)} %bitcast.64, ...), custom_call_target="tpu_custom_call" | custom-call | flops 32212254720 | bytes 52428800 | tf_op jit(solution)/shard_map/teacher_and_head/pallas_call | solution.py:307
  166.4 22.3 %trunk_backward.1 = (f32[4096,128]{1,0:T(8,128)}, f32[4096,128]{1,0:T(8,128)}) custom-call(s32[1]{0:T(128)} %bitcast.core, f32[1024,384]{1,0:T(8,128)} %get-tuple-element.68.d_hidden, f32[1024,1536]{1,0:T(8,128)} %get-tuple-element.69.slope, bf16[1536,384]{1,0:T(8,128)(2,1)} %get-tuple-element.57.down_hi, bf16[1536,384]{1,0:T(8,128)(2,1)} %get-tuple-element.59.down_lo, ...), custom_call_target="tpu_custom_call" | custom-call | flops 11878268928 | bytes 31457280 | tf_op jit(solution)/shard_map/trunk_backward/pallas_call | solution.py:389
  189.3 3.9 %collective-permute-done.20 = f32[4096,128]{1,0:T(8,128)S(1)} collective-permute-done((f32[4096,128]{1,0:T(8,128)}, f32[4096,128]{1,0:T(8,128)S(1)}, u32[]{:S(2)}, u32[]{:S(2)}) %collective-permute-start.20) | collective-permute-done | bytes 2097184 | tf_op jit(solution)/shard_map/ppermute | solution.py:136
  195.0 10.1 %all-to-all-start.1 = ((bf16[64,128,128]{2,1,0:T(8,128)(2,1)}), bf16[64,128,128]{2,1,0:T(8,128)(2,1)S(1)}, u32[]{:S(2)}, u32[]{:S(2)}) async-start(bf16[64,128,128]{2,1,0:T(8,128)(2,1)} %pad_maximum_fusion), calls=%async_computation.1 | async-start | bytes 4194304 | tf_op jit(solution)/shard_map/all_to_all | solution.py:511
  205.1 27.4 %all-to-all-done.1.got = bf16[64,128,128]{2,1,0:T(8,128)(2,1)S(1)} async-done(((bf16[64,128,128]{2,1,0:T(8,128)(2,1)}), bf16[64,128,128]{2,1,0:T(8,128)(2,1)S(1)}, u32[]{:S(2)}, u32[]{:S(2)}) %all-to-all-start.1) | async-done | bytes 2097184 | tf_op jit(solution)/shard_map/all_to_all | solution.py:511
  233.1 34.5 %all_to_all.15.mine_hbm = bf16[64,128,128]{2,1,0:T(8,128)(2,1)S(1)} all-to-all(bf16[64,128,128]{2,1,0:T(8,128)(2,1)S(1)} %add_chunk.1), channel_id=1, replica_groups={{0,1,2,3,4,5,6,7,16,17,18,19,20,21,22,23,32,33,34,35,36,37,38,39,48,49,..., dimensions={0} | all-to-all | bytes 4194304 | tf_op jit(solution)/shard_map/all_to_all | solution.py:511
  267.6 3.7 %collective-permute-start.21 = (bf16[64,128,128]{2,1,0:T(8,128)(2,1)S(1)}, bf16[64,128,128]{2,1,0:T(8,128)(2,1)S(1)}, u32[]{:S(2)}, u32[]{:S(2)}) collective-permute-start(bf16[64,128,128]{2,1,0:T(8,128)(2,1)S(1)} %all_to_all.15.mine_hbm), channel_id=1, source_target_pairs={{0,8},{1,9},{2,10},{3,11},{4,12},{5,13},{6,14},{7,15},{8,0},{9,1},... | collective-permute-start | bytes 6291464 | tf_op jit(solution)/shard_map/ppermute | solution.py:136
  271.3 3.8 %collective-permute-done.21.theirs_hbm = bf16[64,128,128]{2,1,0:T(8,128)(2,1)S(1)} collective-permute-done((bf16[64,128,128]{2,1,0:T(8,128)(2,1)S(1)}, bf16[64,128,128]{2,1,0:T(8,128)(2,1)S(1)}, u32[]{:S(2)}, u32[]{:S(2)}) %collective-permute-start.21) | collective-permute-done | bytes 2097184 | tf_op jit(solution)/shard_map/ppermute | solution.py:136
  275.1 4.4 %unpack_sums.1 = (f32[384,1536]{1,0:T(8,128)}, f32[1536,384]{1,0:T(8,128)}, f32[384,1536]{1,0:T(8,128)}, f32[588,384]{1,0:T(8,128)}, f32[384]{0:T(512)}, /*index=5*/f32[1]{0:T(128)}) custom-call(s32[1]{0:T(128)} %bitcast.core, bf16[64,128,128]{2,1,0:T(8,128)(2,1)S(1)} %all_to_all.15.mine_hbm, bf16[64,128,128]{2,1,0:T(8,128)(2,1)S(1)} %collective-permute-done.21.theirs_hbm), custom_call_target="tpu_custom_call" | custom-call | bytes 12582912 | tf_op jit(solution)/shard_map/unpack_sums/pallas_call | solution.py:492
  (140 shorter events, 32.7 us)
Async XLA Ops:
  7.2 100.6 %all-gather.3.cloned.1.call-start = ((), (), s32[]{:S(2)}) async-start(), calls=%async_computation.3 | async-start | bytes 12533760 | tf_op jit(solution)/shard_map/all_gather | solution.py:556
  11.3 16.4 %copy-start.21 = (bf16[192,1536]{1,0:T(8,128)(2,1)}, bf16[192,1536]{1,0:T(8,128)(2,1)S(1)}, u32[]{:S(2)}) copy-start(bf16[192,1536]{1,0:T(8,128)(2,1)S(1)} %pad_maximum_fusion.1.rest_0_) | copy-start | bytes 1769476
  11.3 22.4 %collective-permute-start.2 = (bf16[192,1536]{1,0:T(8,128)(2,1)S(1)}, bf16[192,1536]{1,0:T(8,128)(2,1)}, u32[]{:S(2)}, u32[]{:S(2)}) collective-permute-start(bf16[192,1536]{1,0:T(8,128)(2,1)S(1)} %pad_maximum_fusion.1.rest_0_), channel_id=1, source_target_pairs={{0,96},{1,97},{2,98},{3,99},{4,100},{5,101},{6,102},{7,103},{8,104... | collective-permute-start | bytes 1769480 | tf_op jit(solution)/shard_map/ppermute | solution.py:109
  14.7 19.0 %collective-permute-start.1 = (bf16[192,1536]{1,0:T(8,128)(2,1)S(1)}, bf16[192,1536]{1,0:T(8,128)(2,1)S(1)}, u32[]{:S(2)}, u32[]{:S(2)}) collective-permute-start(bf16[192,1536]{1,0:T(8,128)(2,1)S(1)} %pad_maximum_fusion.1.rest_0_), channel_id=1, source_target_pairs={{0,32},{1,33},{2,34},{3,35},{4,36},{5,37},{6,38},{7,39},{8,40},{9,... | collective-permute-start | bytes 1769480 | tf_op jit(solution)/shard_map/ppermute | solution.py:109
  14.7 19.6 %collective-permute-start = (bf16[192,1536]{1,0:T(8,128)(2,1)S(1)}, bf16[192,1536]{1,0:T(8,128)(2,1)}, u32[]{:S(2)}, u32[]{:S(2)}) collective-permute-start(bf16[192,1536]{1,0:T(8,128)(2,1)S(1)} %pad_maximum_fusion.1.rest_0_), channel_id=1, source_target_pairs={{0,16},{1,17},{2,18},{3,19},{4,20},{5,21},{6,22},{7,23},{8,24},{9,... | collective-permute-start | bytes 1769480 | tf_op jit(solution)/shard_map/ppermute | solution.py:109
  31.9 29.5 %copy-start.1 = (bf16[384,1536]{1,0:T(8,128)(2,1)}, bf16[384,1536]{1,0:T(8,128)(2,1)S(1)}, u32[]{:S(2)}) copy-start(bf16[384,1536]{1,0:T(8,128)(2,1)S(1)} %get-tuple-element.50.up_hi) | copy-start | bytes 3538948
  34.5 22.7 %all-to-all-start = ((bf16[8,128,640]{2,1,0:T(8,128)(2,1)}), bf16[8,128,640]{2,1,0:T(8,128)(2,1)S(1)}, u32[]{:S(2)}, u32[]{:S(2)}) async-start(bf16[8,128,640]{2,1,0:T(8,128)(2,1)} %pad.12), calls=%async_computation | async-start | bytes 2621440 | tf_op jit(solution)/shard_map/all_to_all | solution.py:583
  39.3 55.3 %collective-permute-start.7 = (bf16[192,1536]{1,0:T(8,128)(2,1)}, bf16[192,1536]{1,0:T(8,128)(2,1)}, u32[]{:S(2)}, u32[]{:S(2)}) collective-permute-start(bf16[192,1536]{1,0:T(8,128)(2,1)} %copy-done.21), channel_id=1, source_target_pairs={{0,8},{1,9},{2,10},{3,11},{4,12},{5,13},{6,14},{7,15},{8,0},{9,1},... | collective-permute-start | bytes 1769480 | tf_op jit(solution)/shard_map/ppermute | solution.py:109
  43.4 36.7 %collective-permute-start.4 = (bf16[192,1536]{1,0:T(8,128)(2,1)}, bf16[192,1536]{1,0:T(8,128)(2,1)}, u32[]{:S(2)}, u32[]{:S(2)}) collective-permute-start(bf16[192,1536]{1,0:T(8,128)(2,1)} %collective-permute-done.rest_1_), channel_id=1, source_target_pairs={{0,96},{1,97},{2,98},{3,99},{4,100},{5,101},{6,102},{7,103},{8,104... | collective-permute-start | bytes 1769480 | tf_op jit(solution)/shard_map/ppermute | solution.py:109
  46.7 33.5 %collective-permute-start.3 = (bf16[192,1536]{1,0:T(8,128)(2,1)}, bf16[192,1536]{1,0:T(8,128)(2,1)}, u32[]{:S(2)}, u32[]{:S(2)}) collective-permute-start(bf16[192,1536]{1,0:T(8,128)(2,1)} %collective-permute-done.rest_1_), channel_id=1, source_target_pairs={{0,32},{1,33},{2,34},{3,35},{4,36},{5,37},{6,38},{7,39},{8,40},{9,... | collective-permute-start | bytes 1769480 | tf_op jit(solution)/shard_map/ppermute | solution.py:109
  50.1 25.0 %collective-permute-start.6 = (bf16[96,1536]{1,0:T(8,128)(2,1)}, bf16[96,1536]{1,0:T(8,128)(2,1)}, u32[]{:S(2)}, u32[]{:S(2)}) collective-permute-start(bf16[96,1536]{1,0:T(8,128)(2,1)} %slice.45), channel_id=1, source_target_pairs={{0,96},{1,97},{2,98},{3,99},{4,100},{5,101},{6,102},{7,103},{8,104... | collective-permute-start | bytes 884744 | tf_op jit(solution)/shard_map/ppermute | solution.py:109
  52.8 25.1 %collective-permute-start.5 = (bf16[96,1536]{1,0:T(8,128)(2,1)}, bf16[96,1536]{1,0:T(8,128)(2,1)}, u32[]{:S(2)}, u32[]{:S(2)}) collective-permute-start(bf16[96,1536]{1,0:T(8,128)(2,1)} %slice.44), channel_id=1, source_target_pairs={{0,32},{1,33},{2,34},{3,35},{4,36},{5,37},{6,38},{7,39},{8,40},{9,... | collective-permute-start | bytes 884744 | tf_op jit(solution)/shard_map/ppermute | solution.py:109
  59.2 28.2 %copy-start.5 = (f32[1024,384]{1,0:T(8,128)}, f32[1024,384]{1,0:T(8,128)S(1)}, u32[]{:S(2)}) copy-start(f32[1024,384]{1,0:T(8,128)S(1)} %get-tuple-element.109.lifted) | copy-start | bytes 4718596
  68.6 15.3 %copy-start.18 = (bf16[1536,384]{1,0:T(8,128)(2,1)S(1)}, bf16[1536,384]{1,0:T(8,128)(2,1)}, u32[]{:S(2)}) copy-start(bf16[1536,384]{1,0:T(8,128)(2,1)} %get-tuple-element.57.down_hi) | copy-start | bytes 3538948
  70.6 15.1 %copy-start.9 = (bf16[1024,1536]{1,0:T(8,128)(2,1)}, bf16[1024,1536]{1,0:T(8,128)(2,1)S(1)}, u32[]{:S(2)}) copy-start(bf16[1024,1536]{1,0:T(8,128)(2,1)S(1)} %get-tuple-element.58.rest_24_) | copy-start | bytes 9437188
  70.6 16.9 %copy-start.10 = (bf16[1024,1536]{1,0:T(8,128)(2,1)}, bf16[1024,1536]{1,0:T(8,128)(2,1)S(1)}, u32[]{:S(2)}) copy-start(bf16[1024,1536]{1,0:T(8,128)(2,1)S(1)} %get-tuple-element.56.rest_23_) | copy-start | bytes 9437188
  75.1 20.1 %collective-permute-start.9 = (bf16[192,1536]{1,0:T(8,128)(2,1)S(1)}, bf16[192,1536]{1,0:T(8,128)(2,1)S(1)}, u32[]{:S(2)}, u32[]{:S(2)}) collective-permute-start(bf16[192,1536]{1,0:T(8,128)(2,1)S(1)} %copy-done.24), channel_id=1, source_target_pairs={{0,8},{1,9},{2,10},{3,11},{4,12},{5,13},{6,14},{7,15},{8,0},{9,1},... | collective-permute-start | bytes 1769480 | tf_op jit(solution)/shard_map/ppermute | solution.py:109
  77.9 22.4 %collective-permute-start.11 = (bf16[192,1536]{1,0:T(8,128)(2,1)}, bf16[192,1536]{1,0:T(8,128)(2,1)S(1)}, u32[]{:S(2)}, u32[]{:S(2)}) collective-permute-start(bf16[192,1536]{1,0:T(8,128)(2,1)} %collective-permute-done.2.rest_4_), channel_id=1, source_target_pairs={{0,8},{1,9},{2,10},{3,11},{4,12},{5,13},{6,14},{7,15},{8,0},{9,1},... | collective-permute-start | bytes 1769480 | tf_op jit(solution)/shard_map/ppermute | solution.py:109
  82.1 13.2 %collective-permute-start.14 = (bf16[96,1536]{1,0:T(8,128)(2,1)S(1)}, bf16[96,1536]{1,0:T(8,128)(2,1)S(1)}, u32[]{:S(2)}, u32[]{:S(2)}) collective-permute-start(bf16[96,1536]{1,0:T(8,128)(2,1)S(1)} %slice.47), channel_id=1, source_target_pairs={{0,96},{1,97},{2,98},{3,99},{4,100},{5,101},{6,102},{7,103},{8,104... | collective-permute-start | bytes 884744 | tf_op jit(solution)/shard_map/ppermute | solution.py:109
  82.3 13.4 %collective-permute-start.13 = (bf16[96,1536]{1,0:T(8,128)(2,1)S(1)}, bf16[96,1536]{1,0:T(8,128)(2,1)S(1)}, u32[]{:S(2)}, u32[]{:S(2)}) collective-permute-start(bf16[96,1536]{1,0:T(8,128)(2,1)S(1)} %slice.46), channel_id=1, source_target_pairs={{0,32},{1,33},{2,34},{3,35},{4,36},{5,37},{6,38},{7,39},{8,40},{9,... | collective-permute-start | bytes 884744 | tf_op jit(solution)/shard_map/ppermute | solution.py:109
  94.6 6.2 %collective-permute-start.8 = (bf16[192,1536]{1,0:T(8,128)(2,1)}, bf16[192,1536]{1,0:T(8,128)(2,1)S(1)}, u32[]{:S(2)}, u32[]{:S(2)}) collective-permute-start(bf16[192,1536]{1,0:T(8,128)(2,1)} %collective-permute-done.rest_1_), channel_id=1, source_target_pairs={{0,8},{1,9},{2,10},{3,11},{4,12},{5,13},{6,14},{7,15},{8,0},{9,1},... | collective-permute-start | bytes 1769480 | tf_op jit(solution)/shard_map/ppermute | solution.py:109
  95.2 8.4 %collective-permute-start.10 = (bf16[192,1536]{1,0:T(8,128)(2,1)}, bf16[192,1536]{1,0:T(8,128)(2,1)S(1)}, u32[]{:S(2)}, u32[]{:S(2)}) collective-permute-start(bf16[192,1536]{1,0:T(8,128)(2,1)} %collective-permute-done.3.rest_3_), channel_id=1, source_target_pairs={{0,8},{1,9},{2,10},{3,11},{4,12},{5,13},{6,14},{7,15},{8,0},{9,1},... | collective-permute-start | bytes 1769480 | tf_op jit(solution)/shard_map/ppermute | solution.py:109
  95.3 8.3 %collective-permute-start.12 = (bf16[192,1536]{1,0:T(8,128)(2,1)}, bf16[192,1536]{1,0:T(8,128)(2,1)S(1)}, u32[]{:S(2)}, u32[]{:S(2)}) collective-permute-start(bf16[192,1536]{1,0:T(8,128)(2,1)} %collective-permute-done.4.rest_5_), channel_id=1, source_target_pairs={{0,8},{1,9},{2,10},{3,11},{4,12},{5,13},{6,14},{7,15},{8,0},{9,1},... | collective-permute-start | bytes 1769480 | tf_op jit(solution)/shard_map/ppermute | solution.py:109
  95.7 5.2 %collective-permute-start.15 = (bf16[96,1536]{1,0:T(8,128)(2,1)}, bf16[96,1536]{1,0:T(8,128)(2,1)S(1)}, u32[]{:S(2)}, u32[]{:S(2)}) collective-permute-start(bf16[96,1536]{1,0:T(8,128)(2,1)} %collective-permute-done.5.rest_12_), channel_id=1, source_target_pairs={{0,8},{1,9},{2,10},{3,11},{4,12},{5,13},{6,14},{7,15},{8,0},{9,1},... | collective-permute-start | bytes 884744 | tf_op jit(solution)/shard_map/ppermute | solution.py:109
  100.3 2.1 collective-permute-start.17
  100.8 2.2 collective-permute-start.16
  101.0 2.6 collective-permute-start.18
  165.8 22.9 %collective-permute-start.19 = (f32[4096,128]{1,0:T(8,128)}, f32[4096,128]{1,0:T(8,128)S(1)}, u32[]{:S(2)}, u32[]{:S(2)}) collective-permute-start(f32[4096,128]{1,0:T(8,128)} %get-tuple-element.67), channel_id=1, source_target_pairs={{0,8},{1,9},{2,10},{3,11},{4,12},{5,13},{6,14},{7,15},{8,0},{9,1},... | collective-permute-start | bytes 6291464 | tf_op jit(solution)/shard_map/ppermute | solution.py:136
  166.4 22.7 %copy-start.14 = (f32[4096,128]{1,0:T(8,128)S(1)}, f32[4096,128]{1,0:T(8,128)}, u32[]{:S(2)}) copy-start(f32[4096,128]{1,0:T(8,128)} %get-tuple-element.66) | copy-start | bytes 6291460
  188.7 4.5 %collective-permute-start.20 = (f32[4096,128]{1,0:T(8,128)}, f32[4096,128]{1,0:T(8,128)S(1)}, u32[]{:S(2)}, u32[]{:S(2)}) collective-permute-start(f32[4096,128]{1,0:T(8,128)} %get-tuple-element.77), channel_id=1, source_target_pairs={{0,8},{1,9},{2,10},{3,11},{4,12},{5,13},{6,14},{7,15},{8,0},{9,1},... | collective-permute-start | bytes 6291464 | tf_op jit(solution)/shard_map/ppermute | solution.py:136
  195.0 37.6 %all-to-all-start.1 = ((bf16[64,128,128]{2,1,0:T(8,128)(2,1)}), bf16[64,128,128]{2,1,0:T(8,128)(2,1)S(1)}, u32[]{:S(2)}, u32[]{:S(2)}) async-start(bf16[64,128,128]{2,1,0:T(8,128)(2,1)} %pad_maximum_fusion), calls=%async_computation.1 | async-start | bytes 4194304 | tf_op jit(solution)/shard_map/all_to_all | solution.py:511
  267.6 7.5 %collective-permute-start.21 = (bf16[64,128,128]{2,1,0:T(8,128)(2,1)S(1)}, bf16[64,128,128]{2,1,0:T(8,128)(2,1)S(1)}, u32[]{:S(2)}, u32[]{:S(2)}) collective-permute-start(bf16[64,128,128]{2,1,0:T(8,128)(2,1)S(1)} %all_to_all.15.mine_hbm), channel_id=1, source_target_pairs={{0,8},{1,9},{2,10},{3,11},{4,12},{5,13},{6,14},{7,15},{8,0},{9,1},... | collective-permute-start | bytes 6291464 | tf_op jit(solution)/shard_map/ppermute | solution.py:136
  (31 other events, 147.4 us)
Sparse Core Ops, SparseCore 0:
  11.0 96.7 all-gather.2

commit v5 on v4

--- a/solution.py
+++ b/solution.py
@@ -22,7 +22,7 @@
 O_ROWS = 96
 NEAR = 12
 FAR = 4
-CUT = 192
+CUT = 208
 REST = P_ROWS - CUT
 STUDENTS = 16
 EMBED_PACK = 48
@@ -203,7 +203,7 @@
         copy.start()
     for copy in first:
         copy.wait()
-    step = 2 * BLK
+    step = 4 * BLK
 
     @pl.loop(0, rows.shape[0] // step)
     def _(r):
@@ -215,7 +215,7 @@
 
     for copy in copies:
         copy.wait()
-    tile = 512
+    tile = 1536
 
     @pl.loop(0, 3 * D_T // tile)
     def _(n):

time: 292 us -> 291 us (level)
  starting transfers between devices: 45.3 us -> 38.3 us
  waiting for transfers between devices: 50.6 us -> 56.8 us
    all_gather x1, waiting for transfers between devices: 4.12 us -> 13.4 us  [on_device(): lax.all_gather(jnp.concatenate([project[:CUT], embed_shard], axis=0), 'st...]
    ppermute x19, waiting for transfers between devices: 7.37 us -> 1.25 us  [moved(): return lax.ppermute(values, BOTH, pairs)]
    all_to_all x1, starting transfers between devices: 10.1 us -> 6.36 us  [to_all_ranks(): lax.all_to_all(values, BOTH, 0, 0, axis_index_groups=core_groups(), tiled...]
    ppermute x19, starting transfers between devices: 25.9 us -> 22.5 us  [moved(): return lax.ppermute(values, BOTH, pairs)]
  transfers between devices with their start and end apart: 25 -> 25, of which waited for: 10 -> 6; matrix products, arithmetic and copies ran while one was open for 15% -> 15% of each run, Pallas kernels for 8% -> 8%
where the time goes in v5:
time: 291 us; the launch traced here: 285 us
  Pallas kernels  84.1 us (29%)
  waiting for transfers between devices  56.8 us (20%)
  starting transfers between devices  38.3 us (13%)
  blocking collectives  34.1 us (12%)
  matrix products  24.4 us (8%)
  between operations  19 us (7%)
  local copies, waits for them, and re-layouts  17.1 us (6%)
  other arithmetic  11.4 us (4%)
    pallas_call x1, Pallas kernels, teacher_and_head(): pl.pallas_call(teacher_kernel, in_specs=[smem] * 3 + [vmem] * 2 + [anywhe...  56.9 us
    all_to_all x1, blocking collectives, to_all_ranks(): lax.all_to_all(values, BOTH, 0, 0, axis_index_groups=core_groups(), tiled...  34.1 us
    all_to_all x1, waiting for transfers between devices, to_all_ranks(): lax.all_to_all(values, BOTH, 0, 0, axis_index_groups=core_groups(), tiled...  27.7 us
    dot_general x11, matrix products, bf16_dot(): lax.dot_general(left, right, dims, preferred_element_type=jnp.float32)  24.4 us
    ppermute x19, starting transfers between devices, moved(): return lax.ppermute(values, BOTH, pairs)  22.5 us
    pallas_call x1, Pallas kernels, trunk_backward(): pl.pallas_call(trunk_kernel, grid=(S_HID // tile,), in_specs=[pl.BlockSpe...  22.3 us
    all_gather x1, waiting for transfers between devices, on_device(): lax.all_gather(jnp.concatenate([project[:CUT], embed_shard], axis=0), 'st...  13.4 us
    ppermute x3, waiting for transfers between devices, core_swap(): return lax.ppermute(values, BOTH, pairs)  7.68 us
  transfers between devices with their start and end apart: 25, of which 6 were waited for; matrix products, arithmetic and copies ran while one was open for 15% of the time, Pallas kernels for 8%

profile of v5, /device:TPU:1, one launch (start us, length us, event | category | flops | bytes accessed | tf_op | source)
XLA Modules:
  0.0 285.3 jit_solution(10800259129049265522)
XLA Ops:
  11.3 3.4 %collective-permute-start.2 = (bf16[176,1536]{1,0:T(8,128)(2,1)S(1)}, bf16[176,1536]{1,0:T(8,128)(2,1)}, u32[]{:S(2)}, u32[]{:S(2)}) collective-permute-start(bf16[176,1536]{1,0:T(8,128)(2,1)S(1)} %pad_maximum_fusion.1.rest_0_), channel_id=1, source_target_pairs={{0,96},{1,97},{2,98},{3,99},{4,100},{5,101},{6,102},{7,103},{8,104... | collective-permute-start | bytes 1622024 | tf_op jit(solution)/shard_map/ppermute | solution.py:109
  14.7 3.6 %collective-permute-start = (bf16[176,1536]{1,0:T(8,128)(2,1)S(1)}, bf16[176,1536]{1,0:T(8,128)(2,1)}, u32[]{:S(2)}, u32[]{:S(2)}) collective-permute-start(bf16[176,1536]{1,0:T(8,128)(2,1)S(1)} %pad_maximum_fusion.1.rest_0_), channel_id=1, source_target_pairs={{0,16},{1,17},{2,18},{3,19},{4,20},{5,21},{6,22},{7,23},{8,24},{9,... | collective-permute-start | bytes 1622024 | tf_op jit(solution)/shard_map/ppermute | solution.py:109
  29.5 2.5 fusion.5
  32.0 1.8 fusion.6
  34.5 4.8 %all-to-all-start = ((bf16[8,128,640]{2,1,0:T(8,128)(2,1)}), bf16[8,128,640]{2,1,0:T(8,128)(2,1)S(1)}, u32[]{:S(2)}, u32[]{:S(2)}) async-start(bf16[8,128,640]{2,1,0:T(8,128)(2,1)} %pad.12), calls=%async_computation | async-start | bytes 2621440 | tf_op jit(solution)/shard_map/all_to_all | solution.py:583
  39.3 2.0 collective-permute-start.7
  41.3 3.3 %collective-permute-start.4 = (bf16[176,1536]{1,0:T(8,128)(2,1)}, bf16[176,1536]{1,0:T(8,128)(2,1)}, u32[]{:S(2)}, u32[]{:S(2)}) collective-permute-start(bf16[176,1536]{1,0:T(8,128)(2,1)} %collective-permute-done.rest_1_), channel_id=1, source_target_pairs={{0,96},{1,97},{2,98},{3,99},{4,100},{5,101},{6,102},{7,103},{8,104... | collective-permute-start | bytes 1622024 | tf_op jit(solution)/shard_map/ppermute | solution.py:109
  44.5 1.7 slice.44
  46.2 1.7 slice.45
  47.9 3.2 %collective-permute-start.6 = (bf16[96,1536]{1,0:T(8,128)(2,1)}, bf16[96,1536]{1,0:T(8,128)(2,1)}, u32[]{:S(2)}, u32[]{:S(2)}) collective-permute-start(bf16[96,1536]{1,0:T(8,128)(2,1)} %slice.45), channel_id=1, source_target_pairs={{0,96},{1,97},{2,98},{3,99},{4,100},{5,101},{6,102},{7,103},{8,104... | collective-permute-start | bytes 884744 | tf_op jit(solution)/shard_map/ppermute | solution.py:109
  51.1 6.8 %all-to-all-done = bf16[8,128,640]{2,1,0:T(8,128)(2,1)S(1)} async-done(((bf16[8,128,640]{2,1,0:T(8,128)(2,1)}), bf16[8,128,640]{2,1,0:T(8,128)(2,1)S(1)}, u32[]{:S(2)}, u32[]{:S(2)}) %all-to-all-start) | async-done | bytes 1310752 | tf_op jit(solution)/shard_map/all_to_all | solution.py:583
  60.3 1.8 fusion.15
  62.1 1.8 fusion.14
  63.9 5.3 %fusion.4 = (f32[1024,1536]{1,0:T(8,128)}, f32[1024,1536]{1,0:T(8,128)S(1)}) fusion(f32[1024,1536]{1,0:T(8,128)S(1)} %fusion.14, f32[1024,1536]{1,0:T(8,128)S(1)} %fusion.15, bf16[1024,384]{1,0:T(8,128)(2,1)S(1)} %get-tuple-element.97.normed_hi, bf16[384,1536]{1,0:T(8,128)(2,1)S(1)} %copy-done.6), kind=kOutput, calls=%fused_computation.7 | convolution fusion | flops 1223688192 | bytes 27131904 | tf_op jit(solution)/shard_map/dot_general | solution.py:42
  69.2 2.0 fusion
  74.9 2.7 collective-permute-start.14
  77.6 1.8 fusion.17
  79.4 1.8 fusion.16
  81.2 1.9 fusion.9
  84.7 1.8 fusion.18
  86.5 1.8 fusion.19
  90.0 4.5 %add_add_fusion.rest_20_ = f32[1024,1536]{1,0:T(8,128)} fusion(f32[1024,1536]{1,0:T(8,128)S(1)} %fusion.18, f32[1024,1536]{1,0:T(8,128)S(1)} %fusion.19, bf16[1024,384]{1,0:T(8,128)(2,1)S(1)} %reduce-precision_convert_fusion.4.rest_21_, bf16[384,1536]{1,0:T(8,128)(2,1)S(1)} %copy-done.7), kind=kOutput, calls=%fused_computation.8 | convolution fusion | flops 1211105280 | bytes 20840448 | tf_op jit(solution)/shard_map/dot_general | solution.py:42
  97.8 13.4 %all-gather.3.cloned.1.call-done = bf16[4096,1536]{1,0:T(8,128)(2,1)} async-done(((bf16[256,1536]{1,0:T(8,128)(2,1)}), bf16[4096,1536]{1,0:T(8,128)(2,1)}) %all-gather.3.cloned.1.call-update) | async-done | bytes 12582928 | tf_op jit(solution)/shard_map/all_gather | solution.py:556
  111.2 56.9 %teacher_and_head.1 = (f32[4096,128]{1,0:T(8,128)}, f32[4096,128]{1,0:T(8,128)}, f32[1536,128]{1,0:T(8,128)}, f32[1024,384]{1,0:T(8,128)}, f32[8,128]{1,0:T(8,128)}) custom-call(s32[1]{0:T(128)} %bitcast.core, s32[16]{0:T(128)} %stack.67.project_owners.output_owners, s32[16]{0:T(128)} %stack.67.project_owners.output_owners, bf16[1024,640]{1,0:T(8,128)(2,1)} %bitcast.64, ...), custom_call_target="tpu_custom_call" | custom-call | flops 32212254720 | bytes 52428800 | tf_op jit(solution)/shard_map/teacher_and_head/pallas_call | solution.py:307
  168.7 22.3 %trunk_backward.1 = (f32[4096,128]{1,0:T(8,128)}, f32[4096,128]{1,0:T(8,128)}) custom-call(s32[1]{0:T(128)} %bitcast.core, f32[1024,384]{1,0:T(8,128)} %get-tuple-element.68.d_hidden, f32[1024,1536]{1,0:T(8,128)} %get-tuple-element.69.slope, bf16[1536,384]{1,0:T(8,128)(2,1)} %get-tuple-element.57.down_hi, bf16[1536,384]{1,0:T(8,128)(2,1)} %get-tuple-element.59.down_lo, ...), custom_call_target="tpu_custom_call" | custom-call | flops 11878268928 | bytes 31457280 | tf_op jit(solution)/shard_map/trunk_backward/pallas_call | solution.py:389
  191.5 3.9 %collective-permute-done.20 = f32[4096,128]{1,0:T(8,128)S(1)} collective-permute-done((f32[4096,128]{1,0:T(8,128)}, f32[4096,128]{1,0:T(8,128)S(1)}, u32[]{:S(2)}, u32[]{:S(2)}) %collective-permute-start.20) | collective-permute-done | bytes 2097184 | tf_op jit(solution)/shard_map/ppermute | solution.py:136
  197.3 6.4 %all-to-all-start.1 = ((bf16[64,128,128]{2,1,0:T(8,128)(2,1)}), bf16[64,128,128]{2,1,0:T(8,128)(2,1)S(1)}, u32[]{:S(2)}, u32[]{:S(2)}) async-start(bf16[64,128,128]{2,1,0:T(8,128)(2,1)} %pad_maximum_fusion), calls=%async_computation.1 | async-start | bytes 4194304 | tf_op jit(solution)/shard_map/all_to_all | solution.py:511
  203.7 27.7 %all-to-all-done.1.got = bf16[64,128,128]{2,1,0:T(8,128)(2,1)S(1)} async-done(((bf16[64,128,128]{2,1,0:T(8,128)(2,1)}), bf16[64,128,128]{2,1,0:T(8,128)(2,1)S(1)}, u32[]{:S(2)}, u32[]{:S(2)}) %all-to-all-start.1) | async-done | bytes 2097184 | tf_op jit(solution)/shard_map/all_to_all | solution.py:511
  231.9 34.1 %all_to_all.15.mine_hbm = bf16[64,128,128]{2,1,0:T(8,128)(2,1)S(1)} all-to-all(bf16[64,128,128]{2,1,0:T(8,128)(2,1)S(1)} %add_chunk.1), channel_id=1, replica_groups={{0,1,2,3,4,5,6,7,16,17,18,19,20,21,22,23,32,33,34,35,36,37,38,39,48,49,..., dimensions={0} | all-to-all | bytes 4194304 | tf_op jit(solution)/shard_map/all_to_all | solution.py:511
  266.0 3.8 %collective-permute-start.21 = (bf16[64,128,128]{2,1,0:T(8,128)(2,1)S(1)}, bf16[64,128,128]{2,1,0:T(8,128)(2,1)S(1)}, u32[]{:S(2)}, u32[]{:S(2)}) collective-permute-start(bf16[64,128,128]{2,1,0:T(8,128)(2,1)S(1)} %all_to_all.15.mine_hbm), channel_id=1, source_target_pairs={{0,8},{1,9},{2,10},{3,11},{4,12},{5,13},{6,14},{7,15},{8,0},{9,1},... | collective-permute-start | bytes 6291464 | tf_op jit(solution)/shard_map/ppermute | solution.py:136
  269.8 3.8 %collective-permute-done.21.theirs_hbm = bf16[64,128,128]{2,1,0:T(8,128)(2,1)S(1)} collective-permute-done((bf16[64,128,128]{2,1,0:T(8,128)(2,1)S(1)}, bf16[64,128,128]{2,1,0:T(8,128)(2,1)S(1)}, u32[]{:S(2)}, u32[]{:S(2)}) %collective-permute-start.21) | collective-permute-done | bytes 2097184 | tf_op jit(solution)/shard_map/ppermute | solution.py:136
  273.6 4.4 %unpack_sums.1 = (f32[384,1536]{1,0:T(8,128)}, f32[1536,384]{1,0:T(8,128)}, f32[384,1536]{1,0:T(8,128)}, f32[588,384]{1,0:T(8,128)}, f32[384]{0:T(512)}, /*index=5*/f32[1]{0:T(128)}) custom-call(s32[1]{0:T(128)} %bitcast.core, bf16[64,128,128]{2,1,0:T(8,128)(2,1)S(1)} %all_to_all.15.mine_hbm, bf16[64,128,128]{2,1,0:T(8,128)(2,1)S(1)} %collective-permute-done.21.theirs_hbm), custom_call_target="tpu_custom_call" | custom-call | bytes 12582912 | tf_op jit(solution)/shard_map/unpack_sums/pallas_call | solution.py:492
  (142 shorter events, 28.0 us)
Async XLA Ops:
  7.2 104.0 %all-gather.3.cloned.1.call-start = ((), (), s32[]{:S(2)}) async-start(), calls=%async_computation.3 | async-start | bytes 13369344 | tf_op jit(solution)/shard_map/all_gather | solution.py:556
  11.3 16.4 %copy-start.21 = (bf16[176,1536]{1,0:T(8,128)(2,1)}, bf16[176,1536]{1,0:T(8,128)(2,1)S(1)}, u32[]{:S(2)}) copy-start(bf16[176,1536]{1,0:T(8,128)(2,1)S(1)} %pad_maximum_fusion.1.rest_0_) | copy-start | bytes 1622020
  11.3 22.4 %collective-permute-start.2 = (bf16[176,1536]{1,0:T(8,128)(2,1)S(1)}, bf16[176,1536]{1,0:T(8,128)(2,1)}, u32[]{:S(2)}, u32[]{:S(2)}) collective-permute-start(bf16[176,1536]{1,0:T(8,128)(2,1)S(1)} %pad_maximum_fusion.1.rest_0_), channel_id=1, source_target_pairs={{0,96},{1,97},{2,98},{3,99},{4,100},{5,101},{6,102},{7,103},{8,104... | collective-permute-start | bytes 1622024 | tf_op jit(solution)/shard_map/ppermute | solution.py:109
  14.7 19.1 %collective-permute-start.1 = (bf16[176,1536]{1,0:T(8,128)(2,1)S(1)}, bf16[176,1536]{1,0:T(8,128)(2,1)S(1)}, u32[]{:S(2)}, u32[]{:S(2)}) collective-permute-start(bf16[176,1536]{1,0:T(8,128)(2,1)S(1)} %pad_maximum_fusion.1.rest_0_), channel_id=1, source_target_pairs={{0,32},{1,33},{2,34},{3,35},{4,36},{5,37},{6,38},{7,39},{8,40},{9,... | collective-permute-start | bytes 1622024 | tf_op jit(solution)/shard_map/ppermute | solution.py:109
  14.7 19.1 %collective-permute-start = (bf16[176,1536]{1,0:T(8,128)(2,1)S(1)}, bf16[176,1536]{1,0:T(8,128)(2,1)}, u32[]{:S(2)}, u32[]{:S(2)}) collective-permute-start(bf16[176,1536]{1,0:T(8,128)(2,1)S(1)} %pad_maximum_fusion.1.rest_0_), channel_id=1, source_target_pairs={{0,16},{1,17},{2,18},{3,19},{4,20},{5,21},{6,22},{7,23},{8,24},{9,... | collective-permute-start | bytes 1622024 | tf_op jit(solution)/shard_map/ppermute | solution.py:109
  32.0 30.1 %copy-start.1 = (bf16[384,1536]{1,0:T(8,128)(2,1)}, bf16[384,1536]{1,0:T(8,128)(2,1)S(1)}, u32[]{:S(2)}) copy-start(bf16[384,1536]{1,0:T(8,128)(2,1)S(1)} %get-tuple-element.50.up_hi) | copy-start | bytes 3538948
  34.5 23.4 %all-to-all-start = ((bf16[8,128,640]{2,1,0:T(8,128)(2,1)}), bf16[8,128,640]{2,1,0:T(8,128)(2,1)S(1)}, u32[]{:S(2)}, u32[]{:S(2)}) async-start(bf16[8,128,640]{2,1,0:T(8,128)(2,1)} %pad.12), calls=%async_computation | async-start | bytes 2621440 | tf_op jit(solution)/shard_map/all_to_all | solution.py:583
  39.3 49.0 %collective-permute-start.7 = (bf16[176,1536]{1,0:T(8,128)(2,1)}, bf16[176,1536]{1,0:T(8,128)(2,1)}, u32[]{:S(2)}, u32[]{:S(2)}) collective-permute-start(bf16[176,1536]{1,0:T(8,128)(2,1)} %copy-done.21), channel_id=1, source_target_pairs={{0,8},{1,9},{2,10},{3,11},{4,12},{5,13},{6,14},{7,15},{8,0},{9,1},... | collective-permute-start | bytes 1622024 | tf_op jit(solution)/shard_map/ppermute | solution.py:109
  41.3 31.0 %collective-permute-start.4 = (bf16[176,1536]{1,0:T(8,128)(2,1)}, bf16[176,1536]{1,0:T(8,128)(2,1)}, u32[]{:S(2)}, u32[]{:S(2)}) collective-permute-start(bf16[176,1536]{1,0:T(8,128)(2,1)} %collective-permute-done.rest_1_), channel_id=1, source_target_pairs={{0,96},{1,97},{2,98},{3,99},{4,100},{5,101},{6,102},{7,103},{8,104... | collective-permute-start | bytes 1622024 | tf_op jit(solution)/shard_map/ppermute | solution.py:109
  44.5 27.8 %collective-permute-start.3 = (bf16[176,1536]{1,0:T(8,128)(2,1)}, bf16[176,1536]{1,0:T(8,128)(2,1)}, u32[]{:S(2)}, u32[]{:S(2)}) collective-permute-start(bf16[176,1536]{1,0:T(8,128)(2,1)} %collective-permute-done.rest_1_), channel_id=1, source_target_pairs={{0,32},{1,33},{2,34},{3,35},{4,36},{5,37},{6,38},{7,39},{8,40},{9,... | collective-permute-start | bytes 1622024 | tf_op jit(solution)/shard_map/ppermute | solution.py:109
  46.2 25.1 %collective-permute-start.5 = (bf16[80,1536]{1,0:T(8,128)(2,1)}, bf16[80,1536]{1,0:T(8,128)(2,1)}, u32[]{:S(2)}, u32[]{:S(2)}) collective-permute-start(bf16[80,1536]{1,0:T(8,128)(2,1)} %slice.44), channel_id=1, source_target_pairs={{0,32},{1,33},{2,34},{3,35},{4,36},{5,37},{6,38},{7,39},{8,40},{9,... | collective-permute-start | bytes 737288 | tf_op jit(solution)/shard_map/ppermute | solution.py:109
  47.9 24.3 %collective-permute-start.6 = (bf16[96,1536]{1,0:T(8,128)(2,1)}, bf16[96,1536]{1,0:T(8,128)(2,1)}, u32[]{:S(2)}, u32[]{:S(2)}) collective-permute-start(bf16[96,1536]{1,0:T(8,128)(2,1)} %slice.45), channel_id=1, source_target_pairs={{0,96},{1,97},{2,98},{3,99},{4,100},{5,101},{6,102},{7,103},{8,104... | collective-permute-start | bytes 884744 | tf_op jit(solution)/shard_map/ppermute | solution.py:109
  59.8 21.3 %copy-start.5 = (f32[1024,384]{1,0:T(8,128)}, f32[1024,384]{1,0:T(8,128)S(1)}, u32[]{:S(2)}) copy-start(f32[1024,384]{1,0:T(8,128)S(1)} %get-tuple-element.109.lifted) | copy-start | bytes 4718596
  71.3 18.1 %collective-permute-start.9 = (bf16[176,1536]{1,0:T(8,128)(2,1)S(1)}, bf16[176,1536]{1,0:T(8,128)(2,1)S(1)}, u32[]{:S(2)}, u32[]{:S(2)}) collective-permute-start(bf16[176,1536]{1,0:T(8,128)(2,1)S(1)} %copy-done.24), channel_id=1, source_target_pairs={{0,8},{1,9},{2,10},{3,11},{4,12},{5,13},{6,14},{7,15},{8,0},{9,1},... | collective-permute-start | bytes 1622024 | tf_op jit(solution)/shard_map/ppermute | solution.py:109
  72.2 22.3 %collective-permute-start.11 = (bf16[176,1536]{1,0:T(8,128)(2,1)}, bf16[176,1536]{1,0:T(8,128)(2,1)S(1)}, u32[]{:S(2)}, u32[]{:S(2)}) collective-permute-start(bf16[176,1536]{1,0:T(8,128)(2,1)} %collective-permute-done.2.rest_4_), channel_id=1, source_target_pairs={{0,8},{1,9},{2,10},{3,11},{4,12},{5,13},{6,14},{7,15},{8,0},{9,1},... | collective-permute-start | bytes 1622024 | tf_op jit(solution)/shard_map/ppermute | solution.py:109
  73.6 15.9 %collective-permute-start.13 = (bf16[80,1536]{1,0:T(8,128)(2,1)S(1)}, bf16[80,1536]{1,0:T(8,128)(2,1)S(1)}, u32[]{:S(2)}, u32[]{:S(2)}) collective-permute-start(bf16[80,1536]{1,0:T(8,128)(2,1)S(1)} %slice.46), channel_id=1, source_target_pairs={{0,32},{1,33},{2,34},{3,35},{4,36},{5,37},{6,38},{7,39},{8,40},{9,... | collective-permute-start | bytes 737288 | tf_op jit(solution)/shard_map/ppermute | solution.py:109
  74.9 15.0 %collective-permute-start.14 = (bf16[96,1536]{1,0:T(8,128)(2,1)S(1)}, bf16[96,1536]{1,0:T(8,128)(2,1)S(1)}, u32[]{:S(2)}, u32[]{:S(2)}) collective-permute-start(bf16[96,1536]{1,0:T(8,128)(2,1)S(1)} %slice.47), channel_id=1, source_target_pairs={{0,96},{1,97},{2,98},{3,99},{4,100},{5,101},{6,102},{7,103},{8,104... | collective-permute-start | bytes 884744 | tf_op jit(solution)/shard_map/ppermute | solution.py:109
  88.3 6.7 %collective-permute-start.8 = (bf16[176,1536]{1,0:T(8,128)(2,1)}, bf16[176,1536]{1,0:T(8,128)(2,1)S(1)}, u32[]{:S(2)}, u32[]{:S(2)}) collective-permute-start(bf16[176,1536]{1,0:T(8,128)(2,1)} %collective-permute-done.rest_1_), channel_id=1, source_target_pairs={{0,8},{1,9},{2,10},{3,11},{4,12},{5,13},{6,14},{7,15},{8,0},{9,1},... | collective-permute-start | bytes 1622024 | tf_op jit(solution)/shard_map/ppermute | solution.py:109
  89.3 8.4 %collective-permute-start.10 = (bf16[176,1536]{1,0:T(8,128)(2,1)}, bf16[176,1536]{1,0:T(8,128)(2,1)S(1)}, u32[]{:S(2)}, u32[]{:S(2)}) collective-permute-start(bf16[176,1536]{1,0:T(8,128)(2,1)} %collective-permute-done.3.rest_3_), channel_id=1, source_target_pairs={{0,8},{1,9},{2,10},{3,11},{4,12},{5,13},{6,14},{7,15},{8,0},{9,1},... | collective-permute-start | bytes 1622024 | tf_op jit(solution)/shard_map/ppermute | solution.py:109
  89.5 8.3 %collective-permute-start.12 = (bf16[176,1536]{1,0:T(8,128)(2,1)}, bf16[176,1536]{1,0:T(8,128)(2,1)S(1)}, u32[]{:S(2)}, u32[]{:S(2)}) collective-permute-start(bf16[176,1536]{1,0:T(8,128)(2,1)} %collective-permute-done.4.rest_5_), channel_id=1, source_target_pairs={{0,8},{1,9},{2,10},{3,11},{4,12},{5,13},{6,14},{7,15},{8,0},{9,1},... | collective-permute-start | bytes 1622024 | tf_op jit(solution)/shard_map/ppermute | solution.py:109
  89.9 5.3 %collective-permute-start.15 = (bf16[80,1536]{1,0:T(8,128)(2,1)}, bf16[80,1536]{1,0:T(8,128)(2,1)S(1)}, u32[]{:S(2)}, u32[]{:S(2)}) collective-permute-start(bf16[80,1536]{1,0:T(8,128)(2,1)} %collective-permute-done.5.rest_12_), channel_id=1, source_target_pairs={{0,8},{1,9},{2,10},{3,11},{4,12},{5,13},{6,14},{7,15},{8,0},{9,1},... | collective-permute-start | bytes 737288 | tf_op jit(solution)/shard_map/ppermute | solution.py:109
  94.5 16.7 %copy-start.29 = (bf16[176,1536]{1,0:T(8,128)(2,1)}, bf16[176,1536]{1,0:T(8,128)(2,1)S(1)}, u32[]{:S(2)}) copy-start(bf16[176,1536]{1,0:T(8,128)(2,1)S(1)} %collective-permute-done.11.rest_10_) | copy-start | bytes 1622020
  94.5 2.0 collective-permute-start.17
  95.0 16.2 %copy-start.30 = (bf16[176,1536]{1,0:T(8,128)(2,1)}, bf16[176,1536]{1,0:T(8,128)(2,1)S(1)}, u32[]{:S(2)}) copy-start(bf16[176,1536]{1,0:T(8,128)(2,1)S(1)} %collective-permute-done.8.rest_7_) | copy-start | bytes 1622020
  95.0 2.8 collective-permute-start.18
  95.1 2.6 collective-permute-start.16
  96.5 14.7 %copy-start.34 = (bf16[96,1536]{1,0:T(8,128)(2,1)}, bf16[96,1536]{1,0:T(8,128)(2,1)S(1)}, u32[]{:S(2)}) copy-start(bf16[96,1536]{1,0:T(8,128)(2,1)S(1)} %collective-permute-done.17.rest_18_) | copy-start | bytes 884740
  168.1 22.9 %collective-permute-start.19 = (f32[4096,128]{1,0:T(8,128)}, f32[4096,128]{1,0:T(8,128)S(1)}, u32[]{:S(2)}, u32[]{:S(2)}) collective-permute-start(f32[4096,128]{1,0:T(8,128)} %get-tuple-element.67), channel_id=1, source_target_pairs={{0,8},{1,9},{2,10},{3,11},{4,12},{5,13},{6,14},{7,15},{8,0},{9,1},... | collective-permute-start | bytes 6291464 | tf_op jit(solution)/shard_map/ppermute | solution.py:136
  168.7 22.7 %copy-start.14 = (f32[4096,128]{1,0:T(8,128)S(1)}, f32[4096,128]{1,0:T(8,128)}, u32[]{:S(2)}) copy-start(f32[4096,128]{1,0:T(8,128)} %get-tuple-element.66) | copy-start | bytes 6291460
  191.0 4.5 %collective-permute-start.20 = (f32[4096,128]{1,0:T(8,128)}, f32[4096,128]{1,0:T(8,128)S(1)}, u32[]{:S(2)}, u32[]{:S(2)}) collective-permute-start(f32[4096,128]{1,0:T(8,128)} %get-tuple-element.77), channel_id=1, source_target_pairs={{0,8},{1,9},{2,10},{3,11},{4,12},{5,13},{6,14},{7,15},{8,0},{9,1},... | collective-permute-start | bytes 6291464 | tf_op jit(solution)/shard_map/ppermute | solution.py:136
  197.3 34.1 %all-to-all-start.1 = ((bf16[64,128,128]{2,1,0:T(8,128)(2,1)}), bf16[64,128,128]{2,1,0:T(8,128)(2,1)S(1)}, u32[]{:S(2)}, u32[]{:S(2)}) async-start(bf16[64,128,128]{2,1,0:T(8,128)(2,1)} %pad_maximum_fusion), calls=%async_computation.1 | async-start | bytes 4194304 | tf_op jit(solution)/shard_map/all_to_all | solution.py:511
  266.0 7.6 %collective-permute-start.21 = (bf16[64,128,128]{2,1,0:T(8,128)(2,1)S(1)}, bf16[64,128,128]{2,1,0:T(8,128)(2,1)S(1)}, u32[]{:S(2)}, u32[]{:S(2)}) collective-permute-start(bf16[64,128,128]{2,1,0:T(8,128)(2,1)S(1)} %all_to_all.15.mine_hbm), channel_id=1, source_target_pairs={{0,8},{1,9},{2,10},{3,11},{4,12},{5,13},{6,14},{7,15},{8,0},{9,1},... | collective-permute-start | bytes 6291464 | tf_op jit(solution)/shard_map/ppermute | solution.py:136
  (32 other events, 190.2 us)
Sparse Core Ops, SparseCore 0:
  11.0 100.1 all-gather.2
